TPU v7x, 32 devices: a whole 2x2x4 slice. The times are simulated.
32 devices in a mesh: dp: 8 (over z, y), rows: 4 (over x, core).
Axes of the slice: x: 2, y: 2, z: 4, core: 2. Of those that a mesh axis runs over, the one named last changes fastest.
Arguments:
- views: bfloat16 [32, 2, 8, 8, 2048], P('dp', None, 'rows'), may hold values from -12 to 12
- crops: bfloat16 [32, 4, 4, 4, 2048], P('dp', None, 'rows'), may hold values from -12 to 12
- w_reduce: bfloat16 [2048, 512], P('dp'), may hold values from -0.125 to 0.125
- gain_one: bfloat16 [512], P('dp'), may hold values from 0.5 to 1.5
- shift_one: bfloat16 [512], P('dp'), may hold values from -2.5 to 2.5
- w_spatial: bfloat16 [3, 3, 512, 512], P(None, None, 'dp'), may hold values from -0.09375 to 0.09375
- gain_two: bfloat16 [512], P('dp'), may hold values from 0.5 to 1.5
- shift_two: bfloat16 [512], P('dp'), may hold values from -2.5 to 2.5
- w_expand: bfloat16 [512, 2048], P('dp'), may hold values from -0.25 to 0.25
- gain_three: bfloat16 [2048], P('dp'), may hold values from 0.5 to 1.5
- shift_three: bfloat16 [2048], P('dp'), may hold values from -2.5 to 2.5
- cot_views: bfloat16 [32, 2, 8, 8, 2048], P('dp', None, 'rows'), may hold values from -6 to 6
- cot_crops: bfloat16 [32, 4, 4, 4, 2048], P('dp', None, 'rows'), may hold values from -6 to 6
Outputs:
- out_views: bfloat16 [32, 2, 8, 8, 2048], P('dp', None, 'rows')
- out_crops: bfloat16 [32, 4, 4, 4, 2048], P('dp', None, 'rows')
- pooled: float32 [32, 6, 2048], P('dp')
- grad_views: bfloat16 [32, 2, 8, 8, 2048], P('dp', None, 'rows')
- grad_crops: bfloat16 [32, 4, 4, 4, 2048], P('dp', None, 'rows')
- grad_reduce: float32 [2048, 512], P('dp')
- grad_gain_one: float32 [512], P('dp')
- grad_shift_one: float32 [512], P('dp')
- grad_spatial: float32 [3, 3, 512, 512], P(None, None, 'dp')
- grad_gain_two: float32 [512], P('dp')
- grad_shift_two: float32 [512], P('dp')
- grad_expand: float32 [512, 2048], P('dp')
- grad_gain_three: float32 [2048], P('dp')
- grad_shift_three: float32 [2048], P('dp')
All inputs are finite; a program needn't handle non-finite values.
Results may differ from a plain program's by a relative error of at most 0.0085.
Values may be sent and summed in bfloat16 or wider, within the bound.
A program may use at most 128 MiB of HBM per device.

v0:
```python
import jax
import jax.numpy as jnp
from jax import lax
from jax.sharding import PartitionSpec as P

EPSILON = 1e-05


def extended(cells, sides, width):
    for axis, dim in sides:
        count = lax.axis_size(axis)
        ends = count - 1
        head = lax.slice_in_dim(cells, 0, width, axis=dim)
        tail = lax.slice_in_dim(cells, cells.shape[dim] - width, cells.shape[dim], axis=dim)
        cells = jnp.concatenate(
            [
                lax.ppermute(tail, axis, [(i, (i + 1) % count) for i in range(ends)]),
                cells,
                lax.ppermute(head, axis, [((i + 1) % count, i) for i in range(ends)]),
            ],
            axis=dim,
        )
    return cells


def silu_slope(values):
    sigmoid_val = jax.nn.sigmoid(values)
    return sigmoid_val * (1.0 + values * (1.0 - sigmoid_val))


def standardize(reduced_pair, gain_vec, shift_vec):
    left_map = reduced_pair[0]
    right_map = reduced_pair[1]
    totals = lax.psum(
        (
            jnp.sum(left_map, 0),
            jnp.sum(left_map * left_map, 0),
            jnp.sum(right_map, 0),
            jnp.sum(right_map * right_map, 0),
        ),
        "rows",
    )
    results = []
    for member in range(2):
        values = reduced_pair[member]
        pixel_count = values.shape[0] * lax.axis_size("rows")
        channel_mean = totals[2 * member] / pixel_count
        inverse_scale = lax.rsqrt(
            totals[2 * member + 1] / pixel_count - channel_mean * channel_mean + EPSILON
        )
        centred = (values - channel_mean) * inverse_scale
        results.append((centred, inverse_scale, gain_vec * centred + shift_vec))
    return results


def unstandardize(slopes, saved, gain_vec):
    shift_left = jnp.sum(slopes[0], 0)
    gain_left = jnp.sum(slopes[0] * saved[0][0], 0)
    shift_right = jnp.sum(slopes[1], 0)
    gain_right = jnp.sum(slopes[1] * saved[1][0], 0)
    totals = lax.psum((shift_left, gain_left, shift_right, gain_right), "rows")
    results = []
    for member in range(2):
        pixel_count = slopes[member].shape[0] * lax.axis_size("rows")
        centred = saved[member][0]
        inverse_scale = saved[member][1]
        mean_slope = gain_vec * totals[2 * member] / pixel_count
        mean_cross = gain_vec * totals[2 * member + 1] / pixel_count
        results.append(
            inverse_scale * (gain_vec * slopes[member] - mean_slope - centred * mean_cross)
        )
    return (results, gain_left + gain_right, shift_left + shift_right)


def spread_rows(activity):
    return extended(activity, (("rows", 1),), 1)


def spread_grads(slopes):
    return extended(slopes, (("rows", 1),), 1)


def patches(padded, row_count, col_count, flipped):
    widened = jnp.pad(padded, ((0, 0), (0, 0), (1, 1), (0, 0)))
    tap_list = []
    for row_tap in range(3):
        for col_tap in range(3):
            row_start = 2 - row_tap if flipped else row_tap
            col_start = 2 - col_tap if flipped else col_tap
            tap_list.append(
                widened[:, row_start : row_start + row_count, col_start : col_start + col_count, :]
            )
    return jnp.concatenate(tap_list, axis=-1).reshape(-1, 9 * widened.shape[-1])


def body(
    views,
    crops,
    w_reduce,
    gain_one,
    shift_one,
    w_spatial,
    gain_two,
    shift_two,
    w_expand,
    gain_three,
    shift_three,
    cot_views,
    cot_crops,
):
    gathered = (
        lax.all_gather(w_reduce, "dp", axis=0, tiled=True),
        lax.all_gather(gain_one, "dp", axis=0, tiled=True),
        lax.all_gather(shift_one, "dp", axis=0, tiled=True),
        lax.all_gather(w_spatial, "dp", axis=2, tiled=True),
        lax.all_gather(gain_two, "dp", axis=0, tiled=True),
        lax.all_gather(shift_two, "dp", axis=0, tiled=True),
        lax.all_gather(w_expand, "dp", axis=0, tiled=True),
        lax.all_gather(gain_three, "dp", axis=0, tiled=True),
        lax.all_gather(shift_three, "dp", axis=0, tiled=True),
    )
    weight_reduce = gathered[0]
    weight_spatial = gathered[3]
    weight_expand = gathered[6]
    gain_first = gathered[1].astype(jnp.float32)
    shift_first = gathered[2].astype(jnp.float32)
    gain_second = gathered[4].astype(jnp.float32)
    shift_second = gathered[5].astype(jnp.float32)
    gain_third = gathered[7].astype(jnp.float32)
    shift_third = gathered[8].astype(jnp.float32)
    channels = views.shape[4]
    middle = weight_reduce.shape[1]
    map_shapes = [
        (views.shape[0] * views.shape[1], views.shape[2], views.shape[3]),
        (crops.shape[0] * crops.shape[1], crops.shape[2], crops.shape[3]),
    ]
    flat_inputs = [views.reshape(-1, channels), crops.reshape(-1, channels)]
    reduced = [
        jnp.dot(source, weight_reduce, preferred_element_type=jnp.float32) for source in flat_inputs
    ]
    first_norm = standardize(reduced, gain_first, shift_first)
    first_act = [jax.nn.silu(saved[2]).astype(jnp.bfloat16) for saved in first_norm]
    padded_act = [
        spread_rows(act.reshape(shape[0], shape[1], shape[2], middle))
        for act, shape in zip(first_act, map_shapes)
    ]
    patch_rows = [
        patches(padded, shape[1], shape[2], False) for padded, shape in zip(padded_act, map_shapes)
    ]
    kernel = weight_spatial.reshape(9 * middle, middle)
    spatial = [jnp.dot(patch, kernel, preferred_element_type=jnp.float32) for patch in patch_rows]
    second_norm = standardize(spatial, gain_second, shift_second)
    second_act = [jax.nn.silu(saved[2]).astype(jnp.bfloat16) for saved in second_norm]
    expanded = [
        jnp.dot(act, weight_expand, preferred_element_type=jnp.float32) for act in second_act
    ]
    third_norm = standardize(expanded, gain_third, shift_third)
    pre_list = [
        source.astype(jnp.float32) + saved[2] for source, saved in zip(flat_inputs, third_norm)
    ]
    activation = [jax.nn.silu(pre) for pre in pre_list]
    view_sums = jnp.sum(activation[0].reshape(views.shape[0], views.shape[1], -1, channels), axis=2)
    crop_sums = jnp.sum(activation[1].reshape(crops.shape[0], crops.shape[1], -1, channels), axis=2)
    pooled_sums = lax.psum((view_sums, crop_sums), "rows")
    pooled = jnp.concatenate(
        [
            pooled_sums[0] / (views.shape[3] * views.shape[3]),
            pooled_sums[1] / (crops.shape[3] * crops.shape[3]),
        ],
        axis=1,
    )
    cotangent = [
        cot_views.reshape(-1, channels).astype(jnp.float32),
        cot_crops.reshape(-1, channels).astype(jnp.float32),
    ]
    d_pre = [cot * silu_slope(pre) for cot, pre in zip(cotangent, pre_list)]
    d_expanded_f, gain_third_grad, shift_third_grad = unstandardize(d_pre, third_norm, gain_third)
    d_expanded = [grad.astype(jnp.bfloat16) for grad in d_expanded_f]
    expand_grad = jnp.einsum(
        "pm,pc->mc", second_act[0], d_expanded[0], preferred_element_type=jnp.float32
    ) + jnp.einsum("pm,pc->mc", second_act[1], d_expanded[1], preferred_element_type=jnp.float32)
    d_norm_two = [
        jnp.einsum("pc,mc->pm", grad, weight_expand, preferred_element_type=jnp.float32)
        * silu_slope(saved[2])
        for grad, saved in zip(d_expanded, second_norm)
    ]
    d_spatial_f, gain_second_grad, shift_second_grad = unstandardize(
        d_norm_two, second_norm, gain_second
    )
    d_spatial = [grad.astype(jnp.bfloat16) for grad in d_spatial_f]
    spatial_grad = (
        jnp.einsum("pk,pm->km", patch_rows[0], d_spatial[0], preferred_element_type=jnp.float32)
        + jnp.einsum("pk,pm->km", patch_rows[1], d_spatial[1], preferred_element_type=jnp.float32)
    ).reshape(3, 3, middle, middle)
    back_kernel = jnp.transpose(weight_spatial, (0, 1, 3, 2)).reshape(9 * middle, middle)
    padded_grads = [
        spread_grads(grad.reshape(shape[0], shape[1], shape[2], middle))
        for grad, shape in zip(d_spatial, map_shapes)
    ]
    d_norm_one = [
        jnp.dot(
            patches(padded, shape[1], shape[2], True),
            back_kernel,
            preferred_element_type=jnp.float32,
        )
        * silu_slope(saved[2])
        for padded, shape, saved in zip(padded_grads, map_shapes, first_norm)
    ]
    d_reduced_f, gain_first_grad, shift_first_grad = unstandardize(
        d_norm_one, first_norm, gain_first
    )
    d_reduced = [grad.astype(jnp.bfloat16) for grad in d_reduced_f]
    reduce_grad = jnp.einsum(
        "pc,pm->cm", flat_inputs[0], d_reduced[0], preferred_element_type=jnp.float32
    ) + jnp.einsum("pc,pm->cm", flat_inputs[1], d_reduced[1], preferred_element_type=jnp.float32)
    input_grads = [
        (
            pre_grad
            + jnp.einsum("pm,cm->pc", grad, weight_reduce, preferred_element_type=jnp.float32)
        ).astype(jnp.bfloat16)
        for pre_grad, grad in zip(d_pre, d_reduced)
    ]
    shares = (
        lax.psum_scatter(reduce_grad, "dp", scatter_dimension=0, tiled=True),
        lax.psum_scatter(gain_first_grad, "dp", scatter_dimension=0, tiled=True),
        lax.psum_scatter(shift_first_grad, "dp", scatter_dimension=0, tiled=True),
        lax.psum_scatter(spatial_grad, "dp", scatter_dimension=2, tiled=True),
        lax.psum_scatter(gain_second_grad, "dp", scatter_dimension=0, tiled=True),
        lax.psum_scatter(shift_second_grad, "dp", scatter_dimension=0, tiled=True),
        lax.psum_scatter(expand_grad, "dp", scatter_dimension=0, tiled=True),
        lax.psum_scatter(gain_third_grad, "dp", scatter_dimension=0, tiled=True),
        lax.psum_scatter(shift_third_grad, "dp", scatter_dimension=0, tiled=True),
    )
    summed = lax.psum(
        (
            shares[0],
            shares[1],
            shares[2],
            shares[3],
            shares[4],
            shares[5],
            shares[6],
            shares[7],
            shares[8],
        ),
        "rows",
    )
    return (
        activation[0].astype(jnp.bfloat16).reshape(views.shape),
        activation[1].astype(jnp.bfloat16).reshape(crops.shape),
        pooled,
        input_grads[0].reshape(views.shape),
        input_grads[1].reshape(crops.shape),
        summed[0],
        summed[1],
        summed[2],
        summed[3],
        summed[4],
        summed[5],
        summed[6],
        summed[7],
        summed[8],
    )


def solution(mesh):
    return jax.shard_map(
        body,
        mesh=mesh,
        in_specs=(
            P("dp", None, "rows", None, None),
            P("dp", None, "rows", None, None),
            P("dp", None),
            P("dp"),
            P("dp"),
            P(None, None, "dp", None),
            P("dp"),
            P("dp"),
            P("dp", None),
            P("dp"),
            P("dp"),
            P("dp", None, "rows", None, None),
            P("dp", None, "rows", None, None),
        ),
        out_specs=(
            P("dp", None, "rows", None, None),
            P("dp", None, "rows", None, None),
            P("dp", None, None),
            P("dp", None, "rows", None, None),
            P("dp", None, "rows", None, None),
            P("dp", None),
            P("dp"),
            P("dp"),
            P(None, None, "dp", None),
            P("dp"),
            P("dp"),
            P("dp", None),
            P("dp"),
            P("dp"),
        ),
        check_vma=False,
    )
```

profile of v0, /device:TPU:0, one launch (start us, length us, event | category | flops | bytes accessed | tf_op | source)
XLA Modules:
  0.0 690.5 jit_solution(9756642258318510119)
XLA Ops:
  16.2 23.2 %all-reduce.22 = (bf16[512]{0:T(512)(128)(2,1)S(1)}, bf16[512]{0:T(512)(128)(2,1)S(1)}, bf16[512]{0:T(512)(128)(2,1)S(1)}, bf16[512]{0:T(512)(128)(2,1)S(1)}) all-reduce(bf16[512]{0:T(512)(128)(2,1)S(1)} %dynamic-update-slice.2, bf16[512]{0:T(512)(128)(2,1)S(1)} %dynamic-update-slice.1, ...), channel_id=1, replica_groups=mesh['dp'=8,'rows'=4] {'dp'}, use_global_device_ids=true, to_apply=%add.6 | all-reduce | flops 2048 | bytes 8192
  40.6 16.4 %all-gather.1 = bf16[8,1,256]{2,1,0:T(2,128)(2,1)S(1)} all-gather(bf16[1,1,256]{2,1,0:T(2,128)(2,1)S(1)} %reshape.184), channel_id=1, replica_groups=mesh['dp'=8,'rows'=4] {'dp'}, dimensions={0}, use_global_device_ids=true | all-gather | bytes 4608 | tf_op jit(solution)/shard_map/all_gather | solution.py:120
  57.6 18.2 %all-gather = bf16[8,1,256]{2,1,0:T(2,128)(2,1)S(1)} all-gather(bf16[1,1,256]{2,1,0:T(2,128)(2,1)S(1)} %reshape.182), channel_id=1, replica_groups=mesh['dp'=8,'rows'=4] {'dp'}, dimensions={0}, use_global_device_ids=true | all-gather | bytes 4608 | tf_op jit(solution)/shard_map/all_gather | solution.py:119
  79.5 6.1 all-reduce.20
  87.1 3.0 collective-permute-start.2
  91.6 3.7 collective-permute-start
  107.2 35.9 %all-gather.8.cloned.1.call-done = bf16[3,3,512,512]{3,2,1,0:T(8,128)(2,1)} async-done(((bf16[3,3,64,512]{3,2,1,0:T(8,128)(2,1)}), bf16[3,3,512,512]{3,2,1,0:T(8,128)(2,1)}) %all-gather.8.cloned.1.call-update) | async-done | bytes 4718608 | tf_op jit(solution)/shard_map/all_gather | solution.py:115
  143.1 4.8 fusion.21
  150.0 5.9 all-reduce.19
  155.9 36.7 %all-gather.10.cloned.1.call-done = bf16[512,2048]{1,0:T(8,128)(2,1)} async-done(((bf16[64,2048]{1,0:T(8,128)(2,1)}), bf16[512,2048]{1,0:T(8,128)(2,1)}) %all-gather.10.cloned.1.call-update) | async-done | bytes 2097168 | tf_op jit(solution)/shard_map/all_gather | solution.py:118
  192.7 3.1 fusion.14
  196.3 10.3 %all-reduce.18 = (f32[2048]{0:T(1024)S(1)}, f32[2048]{0:T(1024)S(1)}, f32[2048]{0:T(1024)S(1)}, f32[2048]{0:T(1024)S(1)}) all-reduce(f32[2048]{0:T(1024)S(1)} %get-tuple-element.73, f32[2048]{0:T(1024)S(1)} %get-tuple-element.72, f32[2048]{0:T(1024)S(1)} %get-tuple-element.77, ...), channel_id=1, replica_groups=mesh['dp'=8,'rows'=4] {'rows'}, use_global_device_ids=true, to_apply=%region_11.12 | all-reduce | flops 8192 | bytes 65536 | tf_op jit(solution)/shard_map/psum | solution.py:34
  211.1 10.9 %all-reduce.17 = (f32[2048]{0:T(1024)S(1)}, f32[2048]{0:T(1024)S(1)}, f32[2048]{0:T(1024)S(1)}, f32[2048]{0:T(1024)S(1)}) all-reduce(f32[2048]{0:T(1024)S(1)} %get-tuple-element.71, f32[2048]{0:T(1024)S(1)} %get-tuple-element.70, f32[2048]{0:T(1024)S(1)} %get-tuple-element.75, ...), channel_id=1, replica_groups=mesh['dp'=8,'rows'=4] {'rows'}, use_global_device_ids=true, to_apply=%region_31.32 | all-reduce | flops 8192 | bytes 65536 | tf_op jit(solution)/shard_map/psum | solution.py:61
  230.2 3.8 fusion.20
  233.9 3.3 fusion.16
  237.2 7.2 %all-reduce.16 = (f32[512]{0:T(512)}, f32[512]{0:T(512)}, f32[512]{0:T(512)}, f32[512]{0:T(512)}) all-reduce(f32[512]{0:T(512)} %get-tuple-element.81, f32[512]{0:T(512)} %get-tuple-element.80, f32[512]{0:T(512)} %get-tuple-element.89, f32[512]{0:T(512)} %get-tuple-element.88), channel_id=1, replica_groups=mesh['dp'=8,'rows'=4] {'rows'}, use_global_device_ids=true, to_apply=%region_35.36 | all-reduce | flops 2048 | bytes 16384 | tf_op jit(solution)/shard_map/psum | solution.py:61
  250.1 3.7 collective-permute-start.6
  264.3 6.7 copy.38
  300.1 37.1 %all-reduce.14 = (f32[512]{0:T(512)}, f32[512]{0:T(512)}, f32[512]{0:T(512)}, f32[512]{0:T(512)}, f32[2048]{0:T(1024)}, /*index=5*/f32[2048]{0:T(1024)}) all-reduce(f32[512]{0:T(512)} %add.286, f32[512]{0:T(512)} %add.287, f32[512]{0:T(512)} %add.289, f32[512]{0:T(512)} %add.290, ...), channel_id=3, replica_groups=mesh['dp'=8,'rows'=4] {'dp'}, use_global_device_ids=true, to_apply=%region_54.55.clone | all-reduce | flops 6144 | bytes 49152
  344.8 11.8 %all-reduce.15 = (f32[512]{0:T(512)}, f32[512]{0:T(512)}, f32[512]{0:T(512)}, f32[512]{0:T(512)}, f32[64]{0:T(128)}, /*index=5*/f32[64]{0:T(128)}, f32[64]{0:T(128)}, f32[64]{0:T(128)}, f32[256]{0:T(256)}, f32[256]{0:T(256)}) all-reduce(f32[512]{0:T(512)} %copy-done.79, ...), channel_id=1, replica_groups=mesh['dp'=8,'rows'=4] {'rows'}, use_global_device_ids=true, to_apply=%region_39.40 | all-reduce | flops 2816 | bytes 22528 | tf_op jit(solution)/shard_map/psum | solution.py:61
  366.6 5.1 convolution_add_fusion
  377.5 72.6 %reduce-scatter.4.cloned.1.call-done = f32[256,512]{0,1:T(8,128)} async-done(((f32[2048,512]{0,1:T(8,128)}), f32[256,512]{0,1:T(8,128)}) %reduce-scatter.4.cloned.1.call-update) | async-done | bytes 524304 | tf_op jit(solution)/shard_map/reduce_scatter | solution.py:224
  450.1 167.1 %reduce-scatter.6.cloned.1.call-done = f32[3,3,64,512]{3,2,1,0:T(8,128)} async-done(((f32[3,3,512,512]{3,2,1,0:T(8,128)}), f32[3,3,64,512]{3,2,1,0:T(8,128)}) %reduce-scatter.6.cloned.1.call-update) | async-done | bytes 1179664 | tf_op jit(solution)/shard_map/reduce_scatter | solution.py:227
  623.4 54.3 %all-reduce.25.cloned.1.call-done = (f32[4,4,2048]{2,1,0:T(4,128)}, f32[4,2,2048]{2,1,0:T(2,128)}, f32[256,512]{0,1:T(8,128)}, f32[3,3,64,512]{3,2,1,0:T(8,128)}, f32[64,2048]{1,0:T(8,128)}) async-done(((f32[4,4,2048]{2,1,0:T(4,128)}, f32[4,2,2048]{2,1,0:T(2,128)}, f32[256,512]{0,1:T(8,128)}, f32[3,3,64,512]{3,2,1,0:T(8,128)}, f32[64,2048]{1,0:T(8,128)}), (f32[4,4,2048]{2,1,0:T(4,128)}, ...) | async-done | bytes 2424848 | tf_op jit(solution)/shard_map/psum | solution.py:164
  (333 shorter events, 122.2 us)
Async XLA Ops:
  7.2 68.6 %copy-start.37 = (bf16[4,4,1,4,2048]{4,3,2,1,0:T(4,128)(2,1)S(1)}, bf16[4,4,1,4,2048]{4,3,2,1,0:T(4,128)(2,1)}, u32[]{:S(2)}) copy-start(bf16[4,4,1,4,2048]{4,3,2,1,0:T(4,128)(2,1)} %param.14) | copy-start | bytes 786436
  7.2 68.7 %copy-start.36 = (bf16[4,4,1,4,2048]{4,3,2,1,0:T(4,128)(2,1)S(1)}, bf16[4,4,1,4,2048]{4,3,2,1,0:T(4,128)(2,1)}, u32[]{:S(2)}) copy-start(bf16[4,4,1,4,2048]{4,3,2,1,0:T(4,128)(2,1)} %param.25) | copy-start | bytes 786436
  7.2 69.5 %all-gather.6.cloned.1.call-start = ((), (), s32[]{:S(2)}) async-start(), calls=%async_computation.3 | async-start | bytes 2359296 | tf_op jit(solution)/shard_map/all_gather | solution.py:112
  7.9 135.2 %all-gather.8.cloned.1.call-start = ((), (), s32[]{:S(2)}) async-start(), calls=%async_computation.4 | async-start | bytes 5308416 | tf_op jit(solution)/shard_map/all_gather | solution.py:115
  8.7 184.0 %all-gather.10.cloned.1.call-start = ((), (), s32[]{:S(2)}) async-start(), calls=%async_computation.5 | async-start | bytes 2359296 | tf_op jit(solution)/shard_map/all_gather | solution.py:118
  9.4 368.1 %reduce-scatter.8.cloned.1.call-start = ((), (), s32[]{:S(2)}) async-start(), calls=%async_computation.8 | async-start | bytes 4718592 | tf_op jit(solution)/shard_map/reduce_scatter | solution.py:230
  39.4 46.2 %copy-start.44 = (f32[512]{0:T(512)}, f32[512]{0:T(512)S(1)}, u32[]{:S(2)}) copy-start(f32[512]{0:T(512)S(1)} %convert_element_type.88) | copy-start | bytes 6148
  78.9 24.1 %copy-start.16 = (f32[64,512]{1,0:T(8,128)}, f32[64,512]{1,0:T(8,128)S(1)}, u32[]{:S(2)}) copy-start(f32[64,512]{1,0:T(8,128)S(1)} %get-tuple-element.206) | copy-start | bytes 393220
  85.8 10.8 %collective-permute-start.3 = (bf16[16,1,4,512]{3,2,0,1:T(4,128)(2,1)S(1)}, bf16[16,1,4,512]{3,2,0,1:T(4,128)(2,1)S(1)}, u32[]{:S(2)}, u32[]{:S(2)}) collective-permute-start(bf16[16,1,4,512]{3,2,0,1:T(4,128)(2,1)S(1)} %reshape.158), channel_id=1, source_target_pairs={{1,0},{2,1},{3,2},{5,4},{6,5},{7,6},{9,8},{10,9},{11,10},{13,12},{... | collective-permute-start | bytes 196616 | tf_op jit(solution)/shard_map/ppermute | solution.py:19
  87.1 9.5 %collective-permute-start.2 = (bf16[16,1,4,512]{3,2,0,1:T(4,128)(2,1)S(1)}, bf16[16,1,4,512]{3,2,0,1:T(4,128)(2,1)S(1)}, u32[]{:S(2)}, u32[]{:S(2)}) collective-permute-start(bf16[16,1,4,512]{3,2,0,1:T(4,128)(2,1)S(1)} %reshape.158), channel_id=1, source_target_pairs={{0,1},{1,2},{2,3},{4,5},{5,6},{6,7},{8,9},{9,10},{10,11},{12,13},{... | collective-permute-start | bytes 196616 | tf_op jit(solution)/shard_map/ppermute | solution.py:17
  91.6 12.2 %collective-permute-start = (bf16[8,1,8,512]{3,2,1,0:T(8,128)(2,1)}, bf16[8,1,8,512]{3,2,1,0:T(8,128)(2,1)}, u32[]{:S(2)}, u32[]{:S(2)}) collective-permute-start(bf16[8,1,8,512]{3,2,1,0:T(8,128)(2,1)} %get-tuple-element.177), channel_id=1, source_target_pairs={{0,1},{1,2},{2,3},{4,5},{5,6},{6,7},{8,9},{9,10},{10,11},{12,13},{... | collective-permute-start | bytes 196616 | tf_op jit(solution)/shard_map/ppermute | solution.py:17
  95.2 8.6 %collective-permute-start.1 = (bf16[8,1,8,512]{3,2,1,0:T(8,128)(2,1)}, bf16[8,1,8,512]{3,2,1,0:T(8,128)(2,1)}, u32[]{:S(2)}, u32[]{:S(2)}) collective-permute-start(bf16[8,1,8,512]{3,2,1,0:T(8,128)(2,1)} %get-tuple-element.178), channel_id=1, source_target_pairs={{1,0},{2,1},{3,2},{5,4},{6,5},{7,6},{9,8},{10,9},{11,10},{13,12},{... | collective-permute-start | bytes 196616 | tf_op jit(solution)/shard_map/ppermute | solution.py:19
  107.2 40.7 %copy-start.9 = (bf16[128,4608]{1,0:T(8,128)(2,1)}, bf16[128,4608]{1,0:T(8,128)(2,1)S(1)}, u32[]{:S(2)}) copy-start(bf16[128,4608]{1,0:T(8,128)(2,1)S(1)} %constant_dynamic-update-slice_fusion) | copy-start | bytes 3538948
  155.9 67.7 %copy-start.72 = (f32[512]{0:T(512)}, f32[512]{0:T(512)S(1)}, u32[]{:S(2)}) copy-start(f32[512]{0:T(512)S(1)} %get-tuple-element.189) | copy-start | bytes 6148
  155.9 67.7 %copy-start.74 = (f32[512]{0:T(512)}, f32[512]{0:T(512)S(1)}, u32[]{:S(2)}) copy-start(f32[512]{0:T(512)S(1)} %get-tuple-element.190) | copy-start | bytes 6148
  155.9 39.9 %copy-start.62 = (f32[512]{0:T(512)}, f32[512]{0:T(512)S(1)}, u32[]{:S(2)}) copy-start(f32[512]{0:T(512)S(1)} %get-tuple-element.187) | copy-start | bytes 6148
  155.9 39.9 %copy-start.64 = (f32[512]{0:T(512)}, f32[512]{0:T(512)S(1)}, u32[]{:S(2)}) copy-start(f32[512]{0:T(512)S(1)} %get-tuple-element.188) | copy-start | bytes 6148
  228.8 221.4 %reduce-scatter.4.cloned.1.call-start = ((), (), s32[]{:S(2)}) async-start(), calls=%async_computation.6 | async-start | bytes 4718592 | tf_op jit(solution)/shard_map/reduce_scatter | solution.py:224
  248.8 22.2 %collective-permute-start.7 = (bf16[16,1,4,512]{3,2,0,1:T(4,128)(2,1)}, bf16[16,1,4,512]{3,2,0,1:T(4,128)(2,1)}, u32[]{:S(2)}, u32[]{:S(2)}) collective-permute-start(bf16[16,1,4,512]{3,2,0,1:T(4,128)(2,1)} %reshape.165), channel_id=1, source_target_pairs={{1,0},{2,1},{3,2},{5,4},{6,5},{7,6},{9,8},{10,9},{11,10},{13,12},{... | collective-permute-start | bytes 196616 | tf_op jit(solution)/shard_map/ppermute | solution.py:19
  250.1 20.9 %collective-permute-start.6 = (bf16[16,1,4,512]{3,2,0,1:T(4,128)(2,1)}, bf16[16,1,4,512]{3,2,0,1:T(4,128)(2,1)}, u32[]{:S(2)}, u32[]{:S(2)}) collective-permute-start(bf16[16,1,4,512]{3,2,0,1:T(4,128)(2,1)} %reshape.165), channel_id=1, source_target_pairs={{0,1},{1,2},{2,3},{4,5},{5,6},{6,7},{8,9},{9,10},{10,11},{12,13},{... | collective-permute-start | bytes 196616 | tf_op jit(solution)/shard_map/ppermute | solution.py:17
  260.7 31.7 %collective-permute-start.4 = (bf16[8,1,8,512]{3,2,1,0:T(8,128)(2,1)}, bf16[8,1,8,512]{3,2,1,0:T(8,128)(2,1)}, u32[]{:S(2)}, u32[]{:S(2)}) collective-permute-start(bf16[8,1,8,512]{3,2,1,0:T(8,128)(2,1)} %get-tuple-element.173), channel_id=1, source_target_pairs={{0,1},{1,2},{2,3},{4,5},{5,6},{6,7},{8,9},{9,10},{10,11},{12,13},{... | collective-permute-start | bytes 196616 | tf_op jit(solution)/shard_map/ppermute | solution.py:17
  263.1 29.4 %collective-permute-start.5 = (bf16[8,1,8,512]{3,2,1,0:T(8,128)(2,1)}, bf16[8,1,8,512]{3,2,1,0:T(8,128)(2,1)}, u32[]{:S(2)}, u32[]{:S(2)}) collective-permute-start(bf16[8,1,8,512]{3,2,1,0:T(8,128)(2,1)} %get-tuple-element.174), channel_id=1, source_target_pairs={{1,0},{2,1},{3,2},{5,4},{6,5},{7,6},{9,8},{10,9},{11,10},{13,12},{... | collective-permute-start | bytes 196616 | tf_op jit(solution)/shard_map/ppermute | solution.py:19
  363.7 253.5 %reduce-scatter.6.cloned.1.call-start = ((), (), s32[]{:S(2)}) async-start(), calls=%async_computation.7 | async-start | bytes 10616832 | tf_op jit(solution)/shard_map/reduce_scatter | solution.py:227
  371.7 306.0 %all-reduce.25.cloned.1.call-start = ((), (), s32[]{:S(2)}) async-start(), calls=%async_computation.9 | async-start | bytes 4849664 | tf_op jit(solution)/shard_map/psum | solution.py:164
  (73 other events, 249.9 us)
Sparse Core Ops, SparseCore 0:
  10.2 52.3 all-gather.5
  64.7 78.3 all-gather.7
  145.2 47.4 all-gather.9
  228.9 86.6 reduce-scatter.7
  363.9 86.2 reduce-scatter.3
  453.6 163.5 reduce-scatter.5
  621.1 56.5 all-reduce.24
where the time goes:
time: 694 us; the launch traced here: 691 us
  waiting for transfers between devices  369 us (53%)
  blocking collectives  147 us (21%)
  local copies, waits for them, and re-layouts  63.6 us (9%)
  matrix products  41.7 us (6%)
  other arithmetic  33.7 us (5%)
  starting transfers between devices  18.1 us (3%)
  between operations  17.4 us (3%)
    reduce_scatter x1, waiting for transfers between devices, body(): lax.psum_scatter(spatial_grad, 'dp', scatter_dimension=2, tiled=True)  167 us
    reduce_scatter x1, waiting for transfers between devices, body(): lax.psum_scatter(reduce_grad, 'dp', scatter_dimension=0, tiled=True)  72.6 us
    unnamed x2, blocking collectives  60.3 us
    psum x1, waiting for transfers between devices, body(): pooled_sums = lax.psum((view_sums, crop_sums), 'rows')  54.3 us
    all_gather x1, waiting for transfers between devices, body(): lax.all_gather(w_expand, 'dp', axis=0, tiled=True)  36.7 us
    all_gather x1, waiting for transfers between devices, body(): lax.all_gather(w_spatial, 'dp', axis=2, tiled=True)  35.9 us
    unnamed x215, local copies, waits for them, and re-layouts  33.8 us
    psum x3, blocking collectives, unstandardize(): totals = lax.psum((shift_left, gain_left, shift_right, gain_right), 'rows')  30 us
  transfers between devices with their start and end apart: 15, of which 5 were waited for; matrix products, arithmetic and copies ran while one was open for 17% of the time, Pallas kernels for 0%

commit v1 on v0

--- a/solution.py
+++ b/solution.py
@@ -1,6 +1,10 @@
+import functools
+
 import jax
 import jax.numpy as jnp
 from jax import lax
+from jax.experimental import pallas as pl
+from jax.experimental.pallas import tpu as pltpu
 from jax.sharding import PartitionSpec as P
 
 EPSILON = 1e-05
@@ -263,9 +267,713 @@
     )
 
 
+MESH = pl.DeviceIdType.MESH
+F32 = jnp.float32
+BF16 = jnp.bfloat16
+NV = 512
+NC = 256
+N = NV + NC
+KINDS = ((0, NV), (NV, NC))
+NT = (((1,), (1,)), ((), ()))
+TN = (((0,), (0,)), ((), ()))
+
+
+def sigmoid(values):
+    return 0.5 * jnp.tanh(0.5 * values) + 0.5
+
+
+def dot(left, right, dims=(((1,), (0,)), ((), ()))):
+    return lax.dot_general(left, right, dims, preferred_element_type=F32)
+
+
+def moved(values, kind, step):
+    rows, lanes = values.shape
+    if step == 0:
+        return values
+    if kind == 0:
+        maps = values.reshape(rows // 64, 64, lanes)
+        gap = jnp.zeros((rows // 64, 8, lanes), values.dtype)
+        parts = [gap, maps[:, :-8]] if step > 0 else [maps[:, 8:], gap]
+        return jnp.concatenate(parts, axis=1).reshape(rows, lanes)
+    gap = jnp.zeros((64, lanes), values.dtype)
+    return jnp.concatenate([gap, values[:-64]] if step > 0 else [values[64:], gap], axis=0)
+
+
+def turned(values, kind, step):
+    if step == 0:
+        return values
+    rows, lanes = values.shape
+    width = 8 if kind == 0 else 4
+    col = lax.rem(lax.broadcasted_iota(jnp.int32, (rows, lanes), 0), width)
+    edge = 0 if step > 0 else width - 1
+    return jnp.where(col == edge, 0.0, pltpu.roll(values, 1 if step > 0 else rows - 1, axis=0))
+
+
+def stats(values, rows):
+    mean = jnp.sum(values, axis=0, keepdims=True) / rows
+    second = jnp.sum(values * values, axis=0, keepdims=True) / rows
+    return mean, lax.rsqrt(second - mean * mean + EPSILON)
+
+
+def block_kernel(
+    views, crops, w_reduce, w_spatial, w_expand, cot_views, cot_crops, params,
+    out_views, out_crops, pooled, grad_views, grad_crops, grad_reduce, grad_spatial, grad_expand, grad_params,
+    xv, xc, cv, cc, wr, ws, we, pg,
+    part, csend, crecv, xsend, xrecv,
+    act1, act2, dred, conv, xhat1, slope1, xhat2, slope2, ex, dpre, dex, pat, ov, oc, gv, gc, pool, own_pool,
+    ge, gs, gr, ysend_e, yrecv_e, zsend_e, zrecv_e, ysend_s, yrecv_s, zsend_s, zrecv_s, ysend_r, yrecv_r, zsend_r, zrecv_r,
+    fin_e, fin_s, fin_r, pgr, pgs,
+    loc, sx, rx, sw, rw, spg, rpg, scs, rcs, sxs, rxs, sag, rag, sout, rout, sgy, rgy, sgz, rgz, sfin, rfin, spp, rpp, spool, rpool,
+):
+    i, r = lax.axis_index("dp"), lax.axis_index("rows")
+    z, y = i // 2, i % 2
+    x, c = r // 2, r % 2
+    yp = (i + 1 - 2 * y, r)
+    cp = (i, 2 * x + 1 - c)
+    xp = (i, 2 * (1 - x) + c)
+    xcp = (i, 2 * (1 - x) + 1 - c)
+
+    def zpeer(dz):
+        return (z + dz) % 4
+
+    def copy(src, dst, send, recv, dev):
+        return pltpu.make_async_remote_copy(
+            src_ref=src, dst_ref=dst, send_sem=send, recv_sem=recv, device_id=dev, device_id_type=MESH
+        )
+
+    def got(dst, recv):
+        copy(dst, dst, recv, recv, cp).wait_recv()
+
+    def sent(src, send):
+        copy(src, src, send, send, cp).wait_send()
+
+    def lanes(k, xx, cc_):
+        return pl.ds(pl.multiple_of(512 * k + 256 * cc_ + 128 * xx, 128), 128)
+
+    local = []
+
+    def stage(src, dst):
+        cp_ = pltpu.make_async_copy(src, dst, loc.at[len(local)])
+        cp_.start()
+        local.append(cp_)
+
+    @pl.when(y == c)
+    def _():
+        pltpu.make_async_copy(
+            w_reduce.at[pl.ds(pl.multiple_of(128 * x, 128), 128)], wr.at[z], loc.at[23]
+        ).start()
+
+    stage(w_spatial.at[:, :, pl.ds(pl.multiple_of(128 * r, 128), 128)], ws.at[:, i])
+    for k in range(4):
+        stage(w_expand.at[:, lanes(k, x, c)], we.at[i, :, pl.ds(128 * k, 128)])
+    stage(params, pg.at[i])
+    for k in range(4):
+        kl = pl.ds(128 * k, 128)
+        stage(views.at[:, :, lanes(k, x, c)], xv.at[:, r, :, kl])
+        stage(crops.at[:, lanes(k, x, c)], xc.at[r, :, kl])
+    for k in range(4):
+        kl = pl.ds(128 * k, 128)
+        stage(cot_views.at[:, :, lanes(k, x, c)], cv.at[:, r, :, kl])
+        stage(cot_crops.at[:, lanes(k, x, c)], cc.at[r, :, kl])
+
+    bar = pltpu.get_barrier_semaphore()
+    peers = [(2 * zpeer(dz) + y, r) for dz in (1, 2, 3)] + [(2 * zpeer(dz) + 1 - y, r) for dz in (0, 1, 2, 3)]
+    peers += [cp, xp, xcp]
+    for dev in peers:
+        pl.semaphore_signal(bar, inc=1, device_id=dev, device_id_type=MESH)
+    pl.semaphore_wait(bar, len(peers))
+
+    wr_own, ws_own, we_own = wr.at[z], ws.at[:, i], we.at[i]
+
+    @pl.when(y == c)
+    def _():
+        pltpu.make_async_copy(
+            w_reduce.at[pl.ds(pl.multiple_of(128 * x, 128), 128)], wr.at[z], loc.at[23]
+        ).wait()
+        for dz in (1, 2, 3):
+            copy(wr_own, wr_own, sw.at[0, dz], rw.at[0, z], (2 * zpeer(dz) + y, r)).start()
+        copy(wr_own, wr_own, sw.at[0, 0], rw.at[0, z], yp).start()
+
+    def spread(src_v, src_c, dst_v, dst_c, s):
+        for dr in (1, 2, 3):
+            rr = (r + dr) % 4
+            for k in range(4):
+                kl = pl.ds(128 * k, 128)
+                copy(
+                    src_v.at[:, :, lanes(k, rr // 2, rr % 2)], dst_v.at[:, r, :, kl], sx.at[s, 0, dr, k], rx.at[s, 0, r], (i, rr)
+                ).start()
+        for dr in (1, 2, 3):
+            rr = (r + dr) % 4
+            for k in range(4):
+                kl = pl.ds(128 * k, 128)
+                copy(src_c.at[:, lanes(k, rr // 2, rr % 2)], dst_c.at[r, :, kl], sx.at[s, 1, dr, k], rx.at[s, 1, r], (i, rr)).start()
+
+    def spread_sent(src_v, src_c, s):
+        for dr in (1, 2, 3):
+            for k in range(4):
+                kl = pl.ds(128 * k, 128)
+                copy(src_v.at[:, :, kl], src_v.at[:, :, kl], sx.at[s, 0, dr, k], rx.at[s, 0, r], cp).wait_send()
+                copy(src_c.at[:, kl], src_c.at[:, kl], sx.at[s, 1, dr, k], rx.at[s, 1, r], cp).wait_send()
+
+    spread(views, crops, xv, xc, 0)
+
+    local[5].wait()
+    for n, dev in enumerate(peers[:7]):
+        copy(pg.at[i], pg.at[i], spg.at[n], rpg.at[i], dev).start()
+
+    local[0].wait()
+    for dz in (1, 2, 3):
+        copy(ws_own, ws_own, sw.at[1, dz], rw.at[1, i], (2 * zpeer(dz) + y, r)).start()
+    copy(ws_own, ws_own, sw.at[1, 0], rw.at[1, i], yp).start()
+
+    spread(cot_views, cot_crops, cv, cc, 1)
+
+    for k in range(4):
+        local[1 + k].wait()
+    for dz in (1, 2, 3):
+        copy(we_own, we_own, sw.at[2, dz], rw.at[2, i], (2 * zpeer(dz) + y, r)).start()
+    copy(we_own, we_own, sw.at[2, 0], rw.at[2, i], yp).start()
+
+    @pl.when(y == c)
+    def _():
+        for dz in (1, 2, 3):
+            k = zpeer(dz)
+            got(wr.at[k], rw.at[0, k])
+            copy(wr.at[k], wr.at[k], sw.at[0, 3 + dz], rw.at[0, k], yp).start()
+
+    @pl.when(y != c)
+    def _():
+        for k in range(4):
+            got(wr.at[k], rw.at[0, k])
+
+    def pass_on(a, slot):
+        for dz in (1, 2, 3):
+            ii = 2 * zpeer(dz) + y
+            got(slot(ii), rw.at[a, ii])
+            copy(slot(ii), slot(ii), sw.at[a, 3 + dz], rw.at[a, ii], yp).start()
+
+    def arrived(a, slot):
+        for dz in range(4):
+            ii = 2 * zpeer(dz) + 1 - y
+            got(slot(ii), rw.at[a, ii])
+
+    for own in local[6:14]:
+        own.wait()
+    weight_r = wr[...].reshape(512, 512)
+
+    def kind_rows(kind):
+        start, rows = KINDS[kind]
+        return pl.ds(start, rows)
+
+    def scatter_start(op, kind, sums):
+        rows = kind_rows(kind)
+        for s in range(4):
+            part[op, s, rows, :] = sums[:, 128 * s : 128 * s + 128]
+        for xx in range(2):
+            csend[op, kind, xx, pl.ds(0, KINDS[kind][1]), :] = part[op, 2 * xx + 1 - c, rows, :].astype(BF16)
+        n = pl.ds(0, KINDS[kind][1])
+        copy(csend.at[op, kind, :, n], crecv.at[op, kind, :, n], scs.at[op, kind], rcs.at[op, kind], cp).start()
+
+    def scatter_mid(op, kind):
+        rows = kind_rows(kind)
+        n = pl.ds(0, KINDS[kind][1])
+        got(crecv.at[op, kind, :, n], rcs.at[op, kind])
+        far = part[op, 2 * (1 - x) + c, rows, :] + crecv[op, kind, 1 - x, n, :].astype(F32)
+        xsend[op, kind, n, :] = far.astype(BF16)
+        copy(xsend.at[op, kind, n], xrecv.at[op, kind, n], sxs.at[op, kind], rxs.at[op, kind], xp).start()
+
+    def scatter_end(op, kind):
+        rows = kind_rows(kind)
+        n = pl.ds(0, KINDS[kind][1])
+        near = part[op, 2 * x + c, rows, :] + crecv[op, kind, x, n, :].astype(F32)
+        got(xrecv.at[op, kind, n], rxs.at[op, kind])
+        return near + xrecv[op, kind, n, :].astype(F32)
+
+    def gather_start(op, kind, buf, value):
+        rows = kind_rows(kind)
+        buf[r, rows, :] = value
+        own = buf.at[r, rows]
+        copy(own, own, sag.at[op, kind, 0], rag.at[op, kind, r], xp).start()
+        copy(own, own, sag.at[op, kind, 1], rag.at[op, kind, r], cp).start()
+
+    def gather_mid(op, kind, buf):
+        rows = kind_rows(kind)
+        far = buf.at[xp[1], rows]
+        got(far, rag.at[op, kind, xp[1]])
+        copy(far, far, sag.at[op, kind, 2], rag.at[op, kind, xp[1]], cp).start()
+
+    def gather_end(op, kind, buf):
+        rows = kind_rows(kind)
+        got(buf.at[cp[1], rows], rag.at[op, kind, cp[1]])
+        got(buf.at[xcp[1], rows], rag.at[op, kind, xcp[1]])
+        return jnp.concatenate([buf[s, rows, :] for s in range(4)], axis=1)
+
+    for dr in (1, 2, 3):
+        rr = (r + dr) % 4
+        got(xv.at[:, rr], rx.at[0, 0, rr])
+    scatter_start(0, 0, dot(xv[...].reshape(NV, 512), weight_r))
+    for dr in (1, 2, 3):
+        rr = (r + dr) % 4
+        got(xc.at[rr], rx.at[0, 1, rr])
+    scatter_start(0, 1, dot(xc[...].reshape(NC, 512), weight_r))
+    scatter_mid(0, 0)
+    scatter_mid(0, 1)
+    pass_on(1, lambda ii: ws.at[:, ii])
+
+    for dz in (1, 2, 3):
+        ii = 2 * zpeer(dz) + y
+        got(pg.at[ii], rpg.at[ii])
+    for dz in range(4):
+        ii = 2 * zpeer(dz) + 1 - y
+        got(pg.at[ii], rpg.at[ii])
+    half = lax.broadcasted_iota(jnp.int32, (1, 128), 1) < 64
+    gain1, shift1, gain2, shift2 = [
+        jnp.where(half, pg[2 * r, q : q + 1, :], pg[2 * r + 1, q : q + 1, :]) for q in range(4)
+    ]
+    gain3 = jnp.concatenate([pg[2 * k + c, pl.ds(4 + x, 1), :] for k in range(4)], axis=1)
+    shift3 = jnp.concatenate([pg[2 * k + c, pl.ds(6 + x, 1), :] for k in range(4)], axis=1)
+
+    def norm_act(values, rows, gain, shift):
+        mean, rstd = stats(values, rows)
+        xhat = (values - mean) * rstd
+        norm = gain * xhat + shift
+        sig = sigmoid(norm)
+        return rstd, xhat, sig * (1.0 + norm * (1.0 - sig)), (norm * sig).astype(BF16)
+
+    rstd1, rstd2, rstd3 = [None, None], [None, None], [None, None]
+    for kind in range(2):
+        rows = KINDS[kind][1]
+        rstd1[kind], xh, sl, act = norm_act(scatter_end(0, kind), rows, gain1, shift1)
+        gather_start(0, kind, act1, act)
+        xhat1[kind_rows(kind), :] = xh
+        slope1[kind_rows(kind), :] = sl
+    pass_on(2, lambda ii: we.at[ii])
+    for kind in range(2):
+        gather_mid(0, kind, act1)
+    arrived(1, lambda ii: ws.at[:, ii])
+
+    def weight_s():
+        return jnp.concatenate([ws[t].reshape(512, 128) for t in range(9)], axis=1)
+
+    for kind in range(2):
+        rows = KINDS[kind][1]
+        conv[kind_rows(kind), :] = dot(gather_end(0, kind, act1), weight_s())
+        taps = [conv[kind_rows(kind), 128 * t : 128 * t + 128] for t in range(9)]
+        spatial = None
+        for j in range(3):
+            col = taps[3 + j] + moved(taps[j], kind, 1) + moved(taps[6 + j], kind, -1)
+            col = turned(col, kind, 1 - j)
+            spatial = col if spatial is None else spatial + col
+        rstd2[kind], xh, sl, act = norm_act(spatial, rows, gain2, shift2)
+        gather_start(1, kind, act2, act)
+        xhat2[kind_rows(kind), :] = xh
+        slope2[kind_rows(kind), :] = sl
+    for kind in range(2):
+        gather_mid(1, kind, act2)
+    arrived(2, lambda ii: we.at[ii])
+    weight_e = we[...].reshape(512, 512)
+
+    for own in local[14:]:
+        own.wait()
+    for dr in (1, 2, 3):
+        rr = (r + dr) % 4
+        got(cv.at[:, rr], rx.at[1, 0, rr])
+        got(cc.at[rr], rx.at[1, 1, rr])
+    sum_x3, sum_d3 = [], []
+    pool[...] = jnp.zeros_like(pool)
+    for kind in range(2):
+        start, rows = KINDS[kind]
+        full2 = gather_end(1, kind, act2)
+        ex[kind_rows(kind), :] = dot(full2, weight_e)
+
+        def moments(b, acc, start=start):
+            e = ex[pl.ds(pl.multiple_of(start + 32 * b, 32), 32), :].reshape(4, 8, 512)
+            return acc[0] + jnp.sum(e, axis=0), acc[1] + jnp.sum(e * e, axis=0)
+
+        zero8 = jnp.zeros((8, 512), F32)
+        tot, sq = lax.fori_loop(0, rows // 32, moments, (zero8, zero8))
+        mean = jnp.sum(tot, axis=0, keepdims=True) / rows
+        rstd = lax.rsqrt(jnp.sum(sq, axis=0, keepdims=True) / rows - mean * mean + EPSILON)
+        rstd3[kind] = rstd
+
+        def finish(b, acc, kind=kind, start=start, mean=mean, rstd=rstd):
+            rs = pl.ds(pl.multiple_of(start + 16 * b, 16), 16)
+            xhat = (ex[rs, :] - mean) * rstd
+            ex[rs, :] = xhat
+            if kind == 0:
+                src = xv[b // 4, b % 4]
+                cot = cv[b // 4, b % 4]
+            else:
+                qs = pl.ds(pl.multiple_of(16 * (b % 4), 16), 16)
+                src = xc[b // 4, qs, :]
+                cot = cc[b // 4, qs, :]
+            pre = src.astype(F32) + (gain3 * xhat + shift3)
+            sig = sigmoid(pre)
+            activation = pre * sig
+            d = cot.astype(F32) * (sig * (1.0 + pre * (1.0 - sig)))
+            dpre[rs, :] = d
+            if kind == 0:
+                ov[b // 4, b % 4] = activation.astype(BF16)
+                pool[b // 4] += activation[:8] + activation[8:]
+            else:
+                oc[b // 4, qs, :] = activation.astype(BF16)
+                m = 8 + 2 * (b % 4)
+                pool[m] += activation[:8]
+                pool[m + 1] += activation[8:]
+            dx = d * xhat
+            return acc[0] + (d[:8] + d[8:]), acc[1] + (dx[:8] + dx[8:])
+
+        sd, sxx = lax.fori_loop(0, rows // 16, finish, (zero8, zero8))
+        sd, sxx = jnp.sum(sd, axis=0, keepdims=True), jnp.sum(sxx, axis=0, keepdims=True)
+        sum_d3.append(sd)
+        sum_x3.append(sxx)
+        scale = gain3 * rstd
+        mean_d, mean_x = sd / rows, sxx / rows
+
+        def back(b, _, start=start, scale=scale, mean_d=mean_d, mean_x=mean_x):
+            rs = pl.ds(pl.multiple_of(start + 32 * b, 32), 32)
+            dex[rs, :] = (scale * (dpre[rs, :] - mean_d - ex[rs, :] * mean_x)).astype(BF16)
+            return 0
+
+        lax.fori_loop(0, rows // 32, back, 0)
+        scatter_start(1, kind, dot(dex[kind_rows(kind), :], weight_e, NT))
+
+    def hand_out(src_v, src_c, dst_v, dst_c, s):
+        for dr in (1, 2, 3, 0):
+            rr = (r + dr) % 4
+            for k in range(4):
+                kl = pl.ds(128 * k, 128)
+                if dr:
+                    copy(src_v.at[:, rr, :, kl], dst_v.at[:, :, lanes(k, x, c)], sout.at[s, 0, dr, k], rout.at[s, 0, r, k], (i, rr)).start()
+                    copy(src_c.at[rr, :, kl], dst_c.at[:, lanes(k, x, c)], sout.at[s, 1, dr, k], rout.at[s, 1, r, k], (i, rr)).start()
+                else:
+                    pltpu.make_async_copy(src_v.at[:, r, :, kl], dst_v.at[:, :, lanes(k, x, c)], sout.at[s, 0, 0, k]).start()
+                    pltpu.make_async_copy(src_c.at[r, :, kl], dst_c.at[:, lanes(k, x, c)], sout.at[s, 1, 0, k]).start()
+
+    def handed(src_v, src_c, dst_v, dst_c, s):
+        for dr in (1, 2, 3, 0):
+            rr = (r + dr) % 4
+            for k in range(4):
+                kl = pl.ds(128 * k, 128)
+                if dr:
+                    copy(src_v.at[:, rr, :, kl], dst_v.at[:, :, lanes(k, x, c)], sout.at[s, 0, dr, k], rout.at[s, 0, r, k], (i, rr)).wait_send()
+                    copy(src_c.at[rr, :, kl], dst_c.at[:, lanes(k, x, c)], sout.at[s, 1, dr, k], rout.at[s, 1, r, k], (i, rr)).wait_send()
+                    got(dst_v.at[:, :, lanes(k, rr // 2, rr % 2)], rout.at[s, 0, rr, k])
+                    got(dst_c.at[:, lanes(k, rr // 2, rr % 2)], rout.at[s, 1, rr, k])
+                else:
+                    pltpu.make_async_copy(src_v.at[:, r, :, kl], dst_v.at[:, :, lanes(k, x, c)], sout.at[s, 0, 0, k]).wait()
+                    pltpu.make_async_copy(src_c.at[r, :, kl], dst_c.at[:, lanes(k, x, c)], sout.at[s, 1, 0, k]).wait()
+
+    scatter_mid(1, 0)
+    scatter_mid(1, 1)
+
+    ge[...] = dot(jnp.concatenate([act2[s] for s in range(4)], axis=1), dex[...], TN).reshape(4, 2, 64, 512)
+
+    def grad_y(full, send, recv, q):
+        send[...] = full[:, 1 - y].astype(BF16)
+        copy(send, recv, sgy.at[q], rgy.at[q], yp).start()
+
+    def grad_z(full, yrecv, send, recv, q):
+        got(yrecv, rgy.at[q])
+        for dz in (1, 2, 3):
+            k = zpeer(dz)
+            send[k] = (full[k, y] + yrecv[k].astype(F32)).astype(BF16)
+            copy(send.at[k], recv.at[z], sgz.at[q, dz], rgz.at[q, z], (2 * k + y, r)).start()
+
+    def grad_sum(full, yrecv, recv, q):
+        total = full[z, y] + yrecv[z].astype(F32)
+        for dz in (1, 2, 3):
+            k = zpeer(dz)
+            got(recv.at[k], rgz.at[q, k])
+            total = total + recv[k].astype(F32)
+        return total
+
+    def fin_start(buf, value, q):
+        buf[r] = value.astype(BF16)
+        copy(buf.at[r], buf.at[r], sfin.at[q, 0], rfin.at[q, r], xp).start()
+        copy(buf.at[r], buf.at[r], sfin.at[q, 1], rfin.at[q, r], cp).start()
+
+    def fin_mid(buf, q):
+        got(buf.at[xp[1]], rfin.at[q, xp[1]])
+        copy(buf.at[xp[1]], buf.at[xp[1]], sfin.at[q, 2], rfin.at[q, xp[1]], cp).start()
+
+    def fin_end(buf, q):
+        got(buf.at[cp[1]], rfin.at[q, cp[1]])
+        got(buf.at[xcp[1]], rfin.at[q, xcp[1]])
+
+    grad_y(ge, ysend_e, yrecv_e, 0)
+
+    def norm_back(d, xhat, rstd, gain, rows):
+        sd = jnp.sum(d, axis=0, keepdims=True)
+        sxx = jnp.sum(d * xhat, axis=0, keepdims=True)
+        return (gain * rstd) * (d - sd / rows - xhat * (sxx / rows)), sd, sxx
+
+    sum_d2, sum_x2 = [], []
+    for kind in range(2):
+        start, rows = KINDS[kind]
+        d = scatter_end(1, kind) * slope2[kind_rows(kind), :]
+        dz_, sd, sxx = norm_back(d, xhat2[kind_rows(kind), :], rstd2[kind], gain2, rows)
+        sum_d2.append(sd)
+        sum_x2.append(sxx)
+        dz_ = dz_.astype(BF16).astype(F32)
+        for tj in range(3):
+            col = turned(dz_, kind, tj - 1)
+            for ti in range(3):
+                t = 3 * ti + tj
+                pat[kind_rows(kind), 128 * t : 128 * t + 128] = moved(col, kind, ti - 1).astype(BF16)
+        scatter_start(2, kind, dot(pat[kind_rows(kind), :], weight_s(), NT))
+    hand_out(ov, oc, out_views, out_crops, 0)
+    grad_z(ge, yrecv_e, zsend_e, zrecv_e, 0)
+    scatter_mid(2, 0)
+    scatter_mid(2, 1)
+    gs[...] = dot(jnp.concatenate([act1[s] for s in range(4)], axis=1), pat[...], TN).reshape(4, 2, 64, 1152)
+    grad_y(gs, ysend_s, yrecv_s, 1)
+
+    sum_d1, sum_x1 = [], []
+    for kind in range(2):
+        start, rows = KINDS[kind]
+        d = scatter_end(2, kind) * slope1[kind_rows(kind), :]
+        dz_, sd, sxx = norm_back(d, xhat1[kind_rows(kind), :], rstd1[kind], gain1, rows)
+        sum_d1.append(sd)
+        sum_x1.append(sxx)
+        gather_start(2, kind, dred, dz_.astype(BF16))
+
+    rows12 = [sum_x1[0] + sum_x1[1], sum_d1[0] + sum_d1[1], sum_x2[0] + sum_x2[1], sum_d2[0] + sum_d2[1]]
+    gx3, gd3 = sum_x3[0] + sum_x3[1], sum_d3[0] + sum_d3[1]
+    rows3 = [g[:, 128 * k : 128 * k + 128] for g in (gx3, gd3) for k in range(4)]
+    pgr[i] = jnp.concatenate(rows12 + rows3 + [jnp.zeros((4, 128), F32)], axis=0)
+    for n, dev in enumerate(peers[:7]):
+        copy(pgr.at[i], pgr.at[i], spp.at[n], rpp.at[0, i], dev).start()
+    grad_z(gs, yrecv_s, zsend_s, zrecv_s, 1)
+    for kind in range(2):
+        gather_mid(2, kind, dred)
+    full_d = [gather_end(2, kind, dred) for kind in range(2)]
+
+    for m in range(4):
+        col = dot(xv[:, :, :, 128 * m : 128 * m + 128].reshape(NV, 128), full_d[0], TN)
+        gr[m] = col + dot(xc[:, :, 128 * m : 128 * m + 128].reshape(NC, 128), full_d[1], TN)
+
+    @pl.when(y != c)
+    def _():
+        ysend_r[...] = gr[...].astype(BF16)
+        copy(ysend_r, yrecv_r, sgy.at[2], rgy.at[2], yp).start()
+
+    for kind in range(2):
+        start, rows = KINDS[kind]
+        grad = (dpre[kind_rows(kind), :] + dot(full_d[kind], weight_r, NT)).astype(BF16)
+        if kind == 0:
+            gv[...] = grad.reshape(8, 4, 16, 512)
+        else:
+            gc[...] = grad.reshape(4, 64, 512)
+
+    @pl.when(y == c)
+    def _():
+        got(yrecv_r, rgy.at[2])
+        for dz in (1, 2, 3):
+            k = zpeer(dz)
+            zsend_r[k] = (gr[k] + yrecv_r[k].astype(F32)).astype(BF16)
+            copy(zsend_r.at[k], zrecv_r.at[z], sgz.at[2, dz], rgz.at[2, z], (2 * k + y, r)).start()
+
+    hand_out(gv, gc, grad_views, grad_crops, 1)
+    fin_start(fin_e, grad_sum(ge, yrecv_e, zrecv_e, 0), 0)
+    fin_start(fin_s, grad_sum(gs, yrecv_s, zrecv_s, 1), 1)
+
+    for n in range(8):
+        row = 4 * (n % 2) + n // 2
+        own_pool[row : row + 1, :] = jnp.sum(pool[n], axis=0, keepdims=True) / 64.0
+        for m in range(2):
+            row = 4 * (2 + 2 * (n % 2) + m) + n // 2
+            own_pool[row : row + 1, :] = jnp.sum(pool[8 + n, 4 * m : 4 * m + 4, :], axis=0, keepdims=True) / 16.0
+    for k in range(4):
+        kl = pl.ds(128 * k, 128)
+        pltpu.make_async_copy(own_pool.at[:, kl], pooled.at[:, lanes(k, x, c)], spool.at[0, k]).start()
+        for dr in (1, 2, 3):
+            copy(own_pool.at[:, kl], pooled.at[:, lanes(k, x, c)], spool.at[dr, k], rpool.at[r, k], (i, (r + dr) % 4)).start()
+
+    @pl.when(y == c)
+    def _():
+        total = gr[z] + yrecv_r[z].astype(F32)
+        for dz in (1, 2, 3):
+            k = zpeer(dz)
+            got(zrecv_r.at[k], rgz.at[2, k])
+            total = total + zrecv_r[k].astype(F32)
+        fin_r[x] = total.astype(BF16)
+        for n, dev in enumerate((xp, cp, xcp)):
+            copy(fin_r.at[x], fin_r.at[x], sfin.at[2, n], rfin.at[2, x], dev).start()
+
+    fin_mid(fin_e, 0)
+    fin_mid(fin_s, 1)
+
+    total = pgr[i]
+    for n in range(7):
+        ii = (i + 1 + n) % 8
+        got(pgr.at[ii], rpp.at[0, ii])
+        total = total + pgr[ii]
+    pgs[r] = total
+    for n, dev in enumerate((xp, cp, xcp)):
+        copy(pgs.at[r], pgs.at[r], spp.at[7 + n], rpp.at[1, r], dev).start()
+
+    fin_end(fin_e, 0)
+    for s in range(4):
+        for k in range(4):
+            lo = 512 * k + 256 * (s % 2) + 128 * (s // 2)
+            grad_expand[:, lo : lo + 128] = fin_e[s, :, 128 * k : 128 * k + 128].astype(F32)
+    fin_end(fin_s, 1)
+    for s in range(4):
+        for t in range(9):
+            grad_spatial[t, :, 128 * s : 128 * s + 128] = fin_s[s, :, 128 * t : 128 * t + 128].astype(F32)
+    for dr in (1, 2, 3):
+        rr = (r + dr) % 4
+        got(pgs.at[rr], rpp.at[1, rr])
+    grad_params[...] = pgs[...]
+
+    got(fin_r.at[1 - x], rfin.at[2, 1 - x])
+
+    @pl.when(y != c)
+    def _():
+        got(fin_r.at[x], rfin.at[2, x])
+
+    for n in range(2):
+        grad_reduce[128 * n : 128 * n + 128, :] = fin_r[n].astype(F32)
+
+    handed(ov, oc, out_views, out_crops, 0)
+    handed(gv, gc, grad_views, grad_crops, 1)
+    for k in range(4):
+        kl = pl.ds(128 * k, 128)
+        pltpu.make_async_copy(own_pool.at[:, kl], pooled.at[:, lanes(k, x, c)], spool.at[0, k]).wait()
+        for dr in (1, 2, 3):
+            rr = (r + dr) % 4
+            sent(own_pool.at[:, kl], spool.at[dr, k])
+            got(pooled.at[:, lanes(k, rr // 2, rr % 2)], rpool.at[rr, k])
+    spread_sent(views, crops, 0)
+    spread_sent(cot_views, cot_crops, 1)
+    for n in range(7):
+        sent(pg.at[i], spg.at[n])
+    for n in range(10):
+        sent(pgs.at[r], spp.at[n])
+    for n in range(7):
+        sent(ws_own, sw.at[1, n])
+        sent(we_own, sw.at[2, n])
+    for kind in range(2):
+        n = pl.ds(0, KINDS[kind][1])
+        for op in range(3):
+            sent(csend.at[op, kind, :, n], scs.at[op, kind])
+            sent(xsend.at[op, kind, n], sxs.at[op, kind])
+            for m in range(3):
+                sent(act1.at[r, kind_rows(kind)], sag.at[op, kind, m])
+    for q, (ys, zs, fin) in enumerate(((ysend_e, zsend_e, fin_e), (ysend_s, zsend_s, fin_s))):
+        sent(ys, sgy.at[q])
+        for dz in (1, 2, 3):
+            sent(zs.at[z], sgz.at[q, dz])
+        for n in range(3):
+            sent(fin.at[r], sfin.at[q, n])
+
+    @pl.when(y != c)
+    def _():
+        sent(ysend_r, sgy.at[2])
+
+    @pl.when(y == c)
+    def _():
+        for n in range(7):
+            sent(wr_own, sw.at[0, n])
+        for dz in (1, 2, 3):
+            sent(zsend_r.at[z], sgz.at[2, dz])
+        for n in range(3):
+            sent(fin_r.at[x], sfin.at[2, n])
+
+
+def fused(views, crops, w_reduce, w_spatial, w_expand, cot_views, cot_crops, params):
+    hbm, vmem = pl.BlockSpec(memory_space=pl.ANY), pl.BlockSpec(memory_space=pltpu.VMEM)
+
+    def shape(dims, dtype):
+        return jax.ShapeDtypeStruct(dims, dtype)
+
+    def buf(dims, dtype=BF16):
+        return pltpu.VMEM(dims, dtype)
+
+    def dma(*dims):
+        return pltpu.SemaphoreType.DMA(dims)
+
+    return pl.pallas_call(
+        block_kernel,
+        out_shape=[
+            shape((8, 16, 2048), BF16), shape((64, 2048), BF16), shape((24, 2048), F32),
+            shape((8, 16, 2048), BF16), shape((64, 2048), BF16),
+            shape((256, 512), F32), shape((9, 64, 512), F32), shape((64, 2048), F32), shape((4, 16, 128), F32),
+        ],
+        in_specs=[hbm] * 8,
+        out_specs=[hbm] * 5 + [vmem] * 4,
+        scratch_shapes=[
+            buf((8, 4, 16, 512)), buf((4, 64, 512)), buf((8, 4, 16, 512)), buf((4, 64, 512)),
+            buf((4, 128, 512)), buf((9, 8, 64, 128)), buf((8, 64, 512)), buf((8, 8, 128), F32),
+            buf((3, 4, N, 128), F32), buf((3, 2, 2, NV, 128)), buf((3, 2, 2, NV, 128)),
+            buf((3, 2, NV, 128)), buf((3, 2, NV, 128)),
+            buf((4, N, 128)), buf((4, N, 128)), buf((4, N, 128)), buf((N, 1152), F32),
+            buf((N, 128), F32), buf((N, 128), F32), buf((N, 128), F32), buf((N, 128), F32),
+            buf((N, 512), F32), buf((N, 512), F32), buf((N, 512)), buf((N, 1152)),
+            buf((8, 4, 16, 512)), buf((4, 64, 512)), buf((8, 4, 16, 512)), buf((4, 64, 512)),
+            buf((16, 8, 512), F32), buf((24, 512), F32),
+            buf((4, 2, 64, 512), F32), buf((4, 2, 64, 1152), F32), buf((4, 128, 512), F32),
+            buf((4, 64, 512)), buf((4, 64, 512)), buf((4, 64, 512)), buf((4, 64, 512)),
+            buf((4, 64, 1152)), buf((4, 64, 1152)), buf((4, 64, 1152)), buf((4, 64, 1152)),
+            buf((4, 128, 512)), buf((4, 128, 512)), buf((4, 128, 512)), buf((4, 128, 512)),
+            buf((4, 64, 512)), buf((4, 64, 1152)), buf((2, 128, 512)),
+            buf((8, 16, 128), F32), buf((4, 16, 128), F32),
+            dma(24), dma(2, 2, 4, 4), dma(2, 2, 4), dma(3, 7), dma(3, 8), dma(7), dma(8),
+            dma(3, 2), dma(3, 2), dma(3, 2), dma(3, 2), dma(3, 2, 3), dma(3, 2, 4),
+            dma(2, 2, 4, 4), dma(2, 2, 4, 4), dma(3), dma(3), dma(3, 4), dma(3, 4), dma(3, 3), dma(3, 4),
+            dma(10), dma(2, 8), dma(4, 4), dma(4, 4),
+        ],
+        compiler_params=pltpu.CompilerParams(collective_id=0, has_side_effects=True, vmem_limit_bytes=56 << 20),
+        cost_estimate=pl.CostEstimate(flops=5_200_000_000, bytes_accessed=8_000_000, transcendentals=2_000_000),
+    )(views, crops, w_reduce, w_spatial, w_expand, cot_views, cot_crops, params)
+
+
+def step(
+    dp, rows, views, crops, w_reduce, gain_one, shift_one, w_spatial, gain_two, shift_two, w_expand, gain_three, shift_three,
+    cot_views, cot_crops,
+):
+    args = (
+        views, crops, w_reduce, gain_one, shift_one, w_spatial, gain_two, shift_two, w_expand, gain_three, shift_three,
+        cot_views, cot_crops,
+    )
+    if (dp, rows) != (8, 4) or views.shape != (4, 2, 2, 8, 2048) or crops.shape != (4, 4, 1, 4, 2048):
+        return body(*args)
+    params = jnp.concatenate(
+        [jnp.concatenate([v, v]) for v in (gain_one, shift_one, gain_two, shift_two)] + [gain_three, shift_three]
+    ).astype(F32).reshape(8, 128)
+    outs = fused(
+        views.reshape(8, 16, 2048), crops.reshape(64, 2048), w_reduce, w_spatial.reshape(9, 64, 512), w_expand,
+        cot_views.reshape(8, 16, 2048), cot_crops.reshape(64, 2048), params,
+    )
+    out_v, out_c, pooled, grad_v, grad_c, grad_r, grad_s, grad_e, grads = outs
+    i = lax.axis_index("dp")
+    small = lax.dynamic_index_in_dim(grads, i // 2, 0, keepdims=False)[:4]
+    small = lax.dynamic_slice_in_dim(small, 64 * (i % 2), 64, axis=1)
+    wide = grads.reshape(2, 2, 16, 128)[:, :, 4:12].reshape(2, 2, 2, 4, 128)
+    wide = lax.dynamic_index_in_dim(wide, i % 2, 1, keepdims=False)
+    wide = lax.dynamic_index_in_dim(wide, i // 2, 2, keepdims=False)
+    return (
+        out_v.reshape(views.shape),
+        out_c.reshape(crops.shape),
+        jnp.transpose(pooled.reshape(6, 4, 2048), (1, 0, 2)),
+        grad_v.reshape(views.shape),
+        grad_c.reshape(crops.shape),
+        grad_r,
+        small[0],
+        small[1],
+        grad_s.reshape(w_spatial.shape[:3] + (512,)),
+        small[2],
+        small[3],
+        grad_e,
+        wide[:, 0].reshape(256),
+        wide[:, 1].reshape(256),
+    )
+
+
 def solution(mesh):
     return jax.shard_map(
-        body,
+        functools.partial(step, mesh.shape["dp"], mesh.shape["rows"]),
         mesh=mesh,
         in_specs=(
             P("dp", None, "rows", None, None),

time: 694 us -> 134 us (0.19)
  waiting for transfers between devices: 369 us -> 0 us
  blocking collectives: 147 us -> 0 us
  Pallas kernels: 0 us -> 109 us
  local copies, waits for them, and re-layouts: 63.6 us -> 21.7 us
  matrix products: 41.7 us -> 0 us
  other arithmetic: 33.7 us -> 0.6 us
  starting transfers between devices: 18.1 us -> 0 us
  between operations: 17.4 us -> 0.73 us
    reduce_scatter x3 -> x0, waiting for transfers between devices: 240 us -> none  [the longest x1 167 us: body(): lax.psum_scatter(spatial_grad, 'dp', scatter_dimension=2, tiled=True)]
    pallas_call x0 -> x1, Pallas kernels: none -> 109 us  [fused(): pl.pallas_call(block_kernel, out_shape=[shape((8, 16, 2048), BF16), shape...]
    all_gather x3 -> x0, waiting for transfers between devices: 72.6 us -> none  [the longest x1 36.7 us: body(): lax.all_gather(w_expand, 'dp', axis=0, tiled=True)]
    unnamed x2 -> x0, blocking collectives: 60.3 us -> none
    psum x1 -> x0, waiting for transfers between devices: 54.3 us -> none  [body(): pooled_sums = lax.psum((view_sums, crop_sums), 'rows')]
    psum x6 -> x0, blocking collectives: 52.3 us -> none  [the longest x3 30 us: unstandardize(): totals = lax.psum((shift_left, gain_left, shift_right, gain_right), 'rows')]
    dot_general x18 -> x0, matrix products: 41.7 us -> none  [the longest x2 7.02 us: body(): jnp.einsum('pc,mc->pm', grad, weight_expand, preferred_element_type=jnp.f...]
    all_gather x2 -> x0, blocking collectives: 34.6 us -> none  [the longest x1 18.2 us: body(): lax.all_gather(gain_three, 'dp', axis=0, tiled=True)]
  transfers between devices with their start and end apart: 15 -> 0, of which waited for: 5 -> 0; matrix products, arithmetic and copies ran while one was open for 17% -> 0% of each run, Pallas kernels for 0% -> 0%
where the time goes in v1:
time: 134 us; the launch traced here: 132 us
  Pallas kernels  109 us (81%)
  local copies, waits for them, and re-layouts  21.7 us (16%)
    pallas_call x1, Pallas kernels, fused(): pl.pallas_call(block_kernel, out_shape=[shape((8, 16, 2048), BF16), shape...  109 us
    concatenate x1, local copies, waits for them, and re-layouts, step(): jnp.concatenate([jnp.concatenate([v, v]) for v in (gain_one, shift_one, g...  6.75 us
    unnamed x17, local copies, waits for them, and re-layouts  4.59 us

profile of v1, /device:TPU:0, one launch (start us, length us, event | category | flops | bytes accessed | tf_op | source)
XLA Modules:
  0.0 132.1 jit_solution(1420884186380429377)
XLA Ops:
  0.7 6.7 %concatenate.3 = bf16[1024]{0:T(1024)(128)(2,1)S(1)} concatenate(bf16[64]{0:T(256)(128)(2,1)} %param.16, bf16[64]{0:T(256)(128)(2,1)} %param.16, bf16[64]{0:T(256)(128)(2,1)} %param.17, bf16[64]{0:T(256)(128)(2,1)} %param.17, bf16[64]{0:T(256)(128)(2,1)} %param.19, bf16[64]{0:T(256)(128)(2,1)} %param.19, bf16[64]{0:T(256)(128)(2,1)} %param.20, bf16[64]{0:T(256)(128)(2,1)} %param.20, ...), dimensions={0} | concatenate | bytes 4096 | tf_op jit(solution)/shard_map/concatenate | solution.py:942
  7.4 0.6 bitcast_convert_fusion.params
  8.0 1.7 %reshape.84.crops = bf16[64,2048]{1,0:T(8,128)(2,1)} reshape(bf16[4,4,1,4,2048]{4,3,2,1,0:T(4,128)(2,1)} %param.14) | data formatting | bytes 524288 | tf_op jit(solution)/shard_map/reshape | solution.py:946
  9.7 1.7 %reshape.87.cot_crops = bf16[64,2048]{1,0:T(8,128)(2,1)} reshape(bf16[4,4,1,4,2048]{4,3,2,1,0:T(4,128)(2,1)} %param.25) | data formatting | bytes 524288 | tf_op jit(solution)/shard_map/reshape | solution.py:947
  11.5 109.1 %shard_map.236 = (bf16[8,16,2048]{2,1,0:T(8,128)(2,1)}, bf16[64,2048]{1,0:T(8,128)(2,1)}, f32[24,2048]{1,0:T(8,128)}, bf16[8,16,2048]{2,1,0:T(8,128)(2,1)}, bf16...) custom-call(bf16[8,16,2048]{2,1,0:T(8,128)(2,1)} %bitcast.37, ...), custom_call_target="tpu_custom_call" | custom-call | flops 5200000000 | bytes 8000000 | tf_op jit(solution)/shard_map/pallas_call | solution.py:897
  120.5 0.0 copy-start.5
  120.6 0.0 copy-start.4
  120.6 0.7 constant_dynamic-slice_fusion.2
  121.3 0.1 constant_dynamic-slice_fusion.1
  121.4 0.5 slice_bitcast_fusion
  121.9 0.8 slice.37
  122.7 0.6 fusion
  123.3 1.7 %reshape.90 = f32[6,4,2048]{2,1,0:T(4,128)} reshape(f32[24,2048]{1,0:T(8,128)} %get-tuple-element.25) | data formatting | bytes 393216 | tf_op jit(solution)/shard_map/reshape | solution.py:959
  125.0 1.8 %reshape.89 = bf16[4,4,1,4,2048]{4,3,1,0,2:T(4,128)(2,1)} reshape(bf16[64,2048]{1,0:T(8,128)(2,1)} %get-tuple-element.24) | data formatting | bytes 524288 | tf_op jit(solution)/shard_map/reshape | solution.py:958
  126.7 0.0 copy-done.5
  126.7 0.8 reshape.92
  127.5 0.0 copy-done.4
  127.5 0.8 copy.34
  128.3 0.0 copy-done.3
  128.3 0.8 copy.35
  129.1 0.8 copy.36
  129.9 1.0 copy.37
  131.0 0.4 copy-done.1
  131.3 0.8 copy.38
  (7 shorter events, 0.0 us)
Async XLA Ops:
  120.5 6.2 %copy-start.5 = (bf16[64,2048]{1,0:T(8,128)(2,1)S(1)}, bf16[64,2048]{1,0:T(8,128)(2,1)}, u32[]{:S(2)}) copy-start(bf16[64,2048]{1,0:T(8,128)(2,1)} %get-tuple-element.27) | copy-start | bytes 786436
  120.6 7.0 %copy-start.4 = (bf16[8,16,2048]{2,1,0:T(8,128)(2,1)S(1)}, bf16[8,16,2048]{2,1,0:T(8,128)(2,1)}, u32[]{:S(2)}) copy-start(bf16[8,16,2048]{2,1,0:T(8,128)(2,1)} %get-tuple-element.23) | copy-start | bytes 1572868
  123.3 5.1 %copy-start.3 = (bf16[8,16,2048]{2,1,0:T(8,128)(2,1)S(1)}, bf16[8,16,2048]{2,1,0:T(8,128)(2,1)}, u32[]{:S(2)}) copy-start(bf16[8,16,2048]{2,1,0:T(8,128)(2,1)} %get-tuple-element.26) | copy-start | bytes 1572868
  127.5 1.6 %copy-start.2 = (f32[256,512]{1,0:T(8,128)S(1)}, f32[256,512]{1,0:T(8,128)}, u32[]{:S(2)}) copy-start(f32[256,512]{1,0:T(8,128)} %get-tuple-element.71) | copy-start | bytes 1572868
  128.3 1.6 %copy-start = (f32[9,64,512]{2,1,0:T(8,128)S(1)}, f32[9,64,512]{2,1,0:T(8,128)}, u32[]{:S(2)}) copy-start(f32[9,64,512]{2,1,0:T(8,128)} %get-tuple-element.30) | copy-start | bytes 3538948
  129.9 1.4 %copy-start.1 = (f32[64,2048]{1,0:T(8,128)S(1)}, f32[64,2048]{1,0:T(8,128)}, u32[]{:S(2)}) copy-start(f32[64,2048]{1,0:T(8,128)} %get-tuple-element.77) | copy-start | bytes 1572868

commit v2 on v1

--- a/solution.py
+++ b/solution.py
@@ -309,20 +309,14 @@
     return jnp.where(col == edge, 0.0, pltpu.roll(values, 1 if step > 0 else rows - 1, axis=0))
 
 
-def stats(values, rows):
-    mean = jnp.sum(values, axis=0, keepdims=True) / rows
-    second = jnp.sum(values * values, axis=0, keepdims=True) / rows
-    return mean, lax.rsqrt(second - mean * mean + EPSILON)
-
-
 def block_kernel(
-    views, crops, w_reduce, w_spatial, w_expand, cot_views, cot_crops, params,
-    out_views, out_crops, pooled, grad_views, grad_crops, grad_reduce, grad_spatial, grad_expand, grad_params,
-    xv, xc, cv, cc, wr, ws, we, pg,
+    views, crops, w_reduce, w_spatial, w_expand, cot_views, cot_crops, gain_a, shift_a, gain_b, shift_b, gain_c, shift_c,
+    out_views, out_crops, pooled, grad_views, grad_crops, fin_e, fin_s, fin_r, pgs,
+    xv, xc4, xc, cv, cc4, cc, wr, ws, we, raw_a, raw_b, raw_c, raw_d, raw_e, raw_f, pg,
     part, csend, crecv, xsend, xrecv,
-    act1, act2, dred, conv, xhat1, slope1, xhat2, slope2, ex, dpre, dex, pat, ov, oc, gv, gc, pool, own_pool,
+    act1, act2, dred, conv, xhat1, slope1, xhat2, slope2, ex, dpre, dex, pat, ov, oc, gv, gc, pool, rows_pool, own_pool,
     ge, gs, gr, ysend_e, yrecv_e, zsend_e, zrecv_e, ysend_s, yrecv_s, zsend_s, zrecv_s, ysend_r, yrecv_r, zsend_r, zrecv_r,
-    fin_e, fin_s, fin_r, pgr, pgs,
+    relay_e, relay_s, relay_r, acc_e, acc_s, acc_r, pgr,
     loc, sx, rx, sw, rw, spg, rpg, scs, rcs, sxs, rxs, sag, rag, sout, rout, sgy, rgy, sgz, rgz, sfin, rfin, spp, rpp, spool, rpool,
 ):
     i, r = lax.axis_index("dp"), lax.axis_index("rows")
@@ -332,9 +326,13 @@
     cp = (i, 2 * x + 1 - c)
     xp = (i, 2 * (1 - x) + c)
     xcp = (i, 2 * (1 - x) + 1 - c)
-
-    def zpeer(dz):
-        return (z + dz) % 4
+    rest = (xp, xcp, cp)
+
+    middle = (z + 1) // 2 == 1
+    step = 1 - 2 * (z // 2)
+
+    def on_line(places):
+        return (2 * (z + places * step) + y, r)
 
     def copy(src, dst, send, recv, dev):
         return pltpu.make_async_remote_copy(
@@ -350,134 +348,171 @@
     def lanes(k, xx, cc_):
         return pl.ds(pl.multiple_of(512 * k + 256 * cc_ + 128 * xx, 128), 128)
 
-    local = []
-
-    def stage(src, dst):
+    def kl(k):
+        return pl.ds(128 * k, 128)
+
+    def kind_rows(kind):
+        return pl.ds(*KINDS[kind])
+
+    local = {}
+
+    def stage(name, src, dst):
         cp_ = pltpu.make_async_copy(src, dst, loc.at[len(local)])
         cp_.start()
-        local.append(cp_)
+        local[name] = cp_
+
+    wr_stage = pltpu.make_async_copy(w_reduce.at[pl.ds(pl.multiple_of(128 * x, 128), 128)], wr.at[z], loc.at[31])
 
     @pl.when(y == c)
     def _():
-        pltpu.make_async_copy(
-            w_reduce.at[pl.ds(pl.multiple_of(128 * x, 128), 128)], wr.at[z], loc.at[23]
-        ).start()
-
-    stage(w_spatial.at[:, :, pl.ds(pl.multiple_of(128 * r, 128), 128)], ws.at[:, i])
+        wr_stage.start()
+
+    stage("ws", w_spatial.at[:, :, pl.ds(pl.multiple_of(128 * r, 128), 128)], ws.at[:, i])
+    raw = (raw_a, raw_b, raw_c, raw_d, raw_e, raw_f)
+    for n, vec in enumerate((gain_a, shift_a, gain_b, shift_b, gain_c, shift_c)):
+        stage(("g", n), vec, raw[n])
     for k in range(4):
-        stage(w_expand.at[:, lanes(k, x, c)], we.at[i, :, pl.ds(128 * k, 128)])
-    stage(params, pg.at[i])
+        stage(("we", k), w_expand.at[:, lanes(k, x, c)], we.at[i, :, kl(k)])
     for k in range(4):
-        kl = pl.ds(128 * k, 128)
-        stage(views.at[:, :, lanes(k, x, c)], xv.at[:, r, :, kl])
-        stage(crops.at[:, lanes(k, x, c)], xc.at[r, :, kl])
+        stage(("xv", k), views.at[:, :, lanes(k, x, c)], xv.at[:, r, :, kl(k)])
+        stage(("xc", k), crops.at[:, :, lanes(k, x, c)], xc4.at[r, :, :, kl(k)])
     for k in range(4):
-        kl = pl.ds(128 * k, 128)
-        stage(cot_views.at[:, :, lanes(k, x, c)], cv.at[:, r, :, kl])
-        stage(cot_crops.at[:, lanes(k, x, c)], cc.at[r, :, kl])
+        stage(("cv", k), cot_views.at[:, :, lanes(k, x, c)], cv.at[:, r, :, kl(k)])
+        stage(("cc", k), cot_crops.at[:, :, lanes(k, x, c)], cc4.at[r, :, :, kl(k)])
 
     bar = pltpu.get_barrier_semaphore()
-    peers = [(2 * zpeer(dz) + y, r) for dz in (1, 2, 3)] + [(2 * zpeer(dz) + 1 - y, r) for dz in (0, 1, 2, 3)]
-    peers += [cp, xp, xcp]
+    peers = [((i + n) % 8, r) for n in range(1, 8)] + [cp, xp, xcp]
     for dev in peers:
         pl.semaphore_signal(bar, inc=1, device_id=dev, device_id_type=MESH)
     pl.semaphore_wait(bar, len(peers))
 
-    wr_own, ws_own, we_own = wr.at[z], ws.at[:, i], we.at[i]
+    def whole_wr(k):
+        return (wr.at[k],)
+
+    def parts_ws(k):
+        return tuple(ws.at[pl.ds(3 * n, 3), 2 * k + y] for n in range(3))
+
+    def parts_ws_other(k):
+        return tuple(ws.at[pl.ds(3 * n, 3), 2 * k + 1 - y] for n in range(3))
+
+    def whole_we(k):
+        return (we.at[2 * k + y],)
+
+    def whole_we_other(k):
+        return (we.at[2 * k + 1 - y],)
+
+    def line_send(a, parts):
+        for h, own in enumerate(parts(z)):
+
+            def go(n, dev, own=own, h=h):
+                copy(own, own, sw.at[a, h, n], rw.at[a, h, y, z], dev).start()
+
+            go(0, on_line(2))
+            go(1, on_line(1))
+
+            @pl.when(middle)
+            def _(go=go):
+                go(2, on_line(-1))
+
+            go(3, yp)
+
+    def line_pass(a, parts, h):
+        def take(places, n, on=False):
+            k = z + places * step
+            ref = parts(k)[h]
+            got(ref, rw.at[a, h, y, k])
+            if on:
+                copy(ref, ref, sw.at[a, h, 7], rw.at[a, h, y, k], on_line(-1)).start()
+            copy(ref, ref, sw.at[a, h, 4 + n], rw.at[a, h, y, k], yp).start()
+
+        @pl.when(middle)
+        def _():
+            take(2, 0, True)
+            take(1, 1)
+            take(-1, 2)
+
+        @pl.when(jnp.logical_not(middle))
+        def _():
+            take(2, 0)
+            take(1, 1)
+            take(3, 2)
+
+    def line_got(a, parts_other, h):
+        for k in range(4):
+            got(parts_other(k)[h], rw.at[a, h, 1 - y, k])
+
+    def line_sent(a, parts):
+        for h, own in enumerate(parts(z)):
+            for n in (0, 1, 3, 4, 5, 6):
+                sent(own, sw.at[a, h, n])
+
+            @pl.when(middle)
+            def _(own=own, h=h):
+                sent(own, sw.at[a, h, 2])
+                sent(own, sw.at[a, h, 7])
 
     @pl.when(y == c)
     def _():
-        pltpu.make_async_copy(
-            w_reduce.at[pl.ds(pl.multiple_of(128 * x, 128), 128)], wr.at[z], loc.at[23]
-        ).wait()
-        for dz in (1, 2, 3):
-            copy(wr_own, wr_own, sw.at[0, dz], rw.at[0, z], (2 * zpeer(dz) + y, r)).start()
-        copy(wr_own, wr_own, sw.at[0, 0], rw.at[0, z], yp).start()
-
-    def spread(src_v, src_c, dst_v, dst_c, s):
-        for dr in (1, 2, 3):
-            rr = (r + dr) % 4
+        wr_stage.wait()
+        line_send(0, whole_wr)
+
+    def spread_v(src, dst, s, devs):
+        for dev in devs:
+            rr = dev[1]
             for k in range(4):
-                kl = pl.ds(128 * k, 128)
-                copy(
-                    src_v.at[:, :, lanes(k, rr // 2, rr % 2)], dst_v.at[:, r, :, kl], sx.at[s, 0, dr, k], rx.at[s, 0, r], (i, rr)
-                ).start()
-        for dr in (1, 2, 3):
-            rr = (r + dr) % 4
+                dr = (rr + 4 - r) % 4
+                copy(src.at[:, :, lanes(k, rr // 2, rr % 2)], dst.at[:, r, :, kl(k)], sx.at[s, 0, dr, k], rx.at[s, 0, r], dev).start()
+
+    def spread_c(src, dst, s, devs):
+        for dev in devs:
+            rr = dev[1]
             for k in range(4):
-                kl = pl.ds(128 * k, 128)
-                copy(src_c.at[:, lanes(k, rr // 2, rr % 2)], dst_c.at[r, :, kl], sx.at[s, 1, dr, k], rx.at[s, 1, r], (i, rr)).start()
-
-    def spread_sent(src_v, src_c, s):
-        for dr in (1, 2, 3):
-            for k in range(4):
-                kl = pl.ds(128 * k, 128)
-                copy(src_v.at[:, :, kl], src_v.at[:, :, kl], sx.at[s, 0, dr, k], rx.at[s, 0, r], cp).wait_send()
-                copy(src_c.at[:, kl], src_c.at[:, kl], sx.at[s, 1, dr, k], rx.at[s, 1, r], cp).wait_send()
-
-    spread(views, crops, xv, xc, 0)
-
-    local[5].wait()
+                dr = (rr + 4 - r) % 4
+                copy(src.at[:, :, lanes(k, rr // 2, rr % 2)], dst.at[r, :, :, kl(k)], sx.at[s, 1, dr, k], rx.at[s, 1, r], dev).start()
+
+    spread_v(views, xv, 0, rest)
+    spread_c(crops, xc4, 0, rest)
+
+    spread_v(cot_views, cv, 1, rest[:1])
+
+    for n in range(6):
+        local["g", n].wait()
+    pg[i] = jnp.zeros((8, 128), F32)
+    for n in range(4):
+        vec = raw[n][...].reshape(1, 64).astype(F32)
+        pg[i, n : n + 1, :] = jnp.concatenate([vec, vec], axis=1)
+    for n in range(2):
+        for m in range(2):
+            pg[i, 4 + 2 * n + m : 5 + 2 * n + m, :] = raw[4 + n][128 * m : 128 * m + 128].reshape(1, 128).astype(F32)
     for n, dev in enumerate(peers[:7]):
         copy(pg.at[i], pg.at[i], spg.at[n], rpg.at[i], dev).start()
 
-    local[0].wait()
-    for dz in (1, 2, 3):
-        copy(ws_own, ws_own, sw.at[1, dz], rw.at[1, i], (2 * zpeer(dz) + y, r)).start()
-    copy(ws_own, ws_own, sw.at[1, 0], rw.at[1, i], yp).start()
-
-    spread(cot_views, cot_crops, cv, cc, 1)
-
-    for k in range(4):
-        local[1 + k].wait()
-    for dz in (1, 2, 3):
-        copy(we_own, we_own, sw.at[2, dz], rw.at[2, i], (2 * zpeer(dz) + y, r)).start()
-    copy(we_own, we_own, sw.at[2, 0], rw.at[2, i], yp).start()
-
     @pl.when(y == c)
     def _():
-        for dz in (1, 2, 3):
-            k = zpeer(dz)
-            got(wr.at[k], rw.at[0, k])
-            copy(wr.at[k], wr.at[k], sw.at[0, 3 + dz], rw.at[0, k], yp).start()
+        line_pass(0, whole_wr, 0)
 
     @pl.when(y != c)
     def _():
         for k in range(4):
-            got(wr.at[k], rw.at[0, k])
-
-    def pass_on(a, slot):
-        for dz in (1, 2, 3):
-            ii = 2 * zpeer(dz) + y
-            got(slot(ii), rw.at[a, ii])
-            copy(slot(ii), slot(ii), sw.at[a, 3 + dz], rw.at[a, ii], yp).start()
-
-    def arrived(a, slot):
-        for dz in range(4):
-            ii = 2 * zpeer(dz) + 1 - y
-            got(slot(ii), rw.at[a, ii])
-
-    for own in local[6:14]:
-        own.wait()
-    weight_r = wr[...].reshape(512, 512)
-
-    def kind_rows(kind):
-        start, rows = KINDS[kind]
-        return pl.ds(start, rows)
+            got(wr.at[k], rw.at[0, 0, 1 - y, k])
+
+    local["ws"].wait()
+    line_send(1, parts_ws)
 
     def scatter_start(op, kind, sums):
         rows = kind_rows(kind)
+        n = pl.ds(0, KINDS[kind][1])
         for s in range(4):
             part[op, s, rows, :] = sums[:, 128 * s : 128 * s + 128]
-        for xx in range(2):
-            csend[op, kind, xx, pl.ds(0, KINDS[kind][1]), :] = part[op, 2 * xx + 1 - c, rows, :].astype(BF16)
-        n = pl.ds(0, KINDS[kind][1])
-        copy(csend.at[op, kind, :, n], crecv.at[op, kind, :, n], scs.at[op, kind], rcs.at[op, kind], cp).start()
+        for xx in (1 - x, x):
+            csend[op, kind, xx, n, :] = part[op, 2 * xx + 1 - c, rows, :].astype(BF16)
+            own = csend.at[op, kind, xx, n]
+            copy(own, crecv.at[op, kind, xx, n], scs.at[op, kind, xx], rcs.at[op, kind, xx], cp).start()
 
     def scatter_mid(op, kind):
         rows = kind_rows(kind)
         n = pl.ds(0, KINDS[kind][1])
-        got(crecv.at[op, kind, :, n], rcs.at[op, kind])
+        got(crecv.at[op, kind, 1 - x, n], rcs.at[op, kind, 1 - x])
         far = part[op, 2 * (1 - x) + c, rows, :] + crecv[op, kind, 1 - x, n, :].astype(F32)
         xsend[op, kind, n, :] = far.astype(BF16)
         copy(xsend.at[op, kind, n], xrecv.at[op, kind, n], sxs.at[op, kind], rxs.at[op, kind], xp).start()
@@ -485,6 +520,7 @@
     def scatter_end(op, kind):
         rows = kind_rows(kind)
         n = pl.ds(0, KINDS[kind][1])
+        got(crecv.at[op, kind, x, n], rcs.at[op, kind, x])
         near = part[op, 2 * x + c, rows, :] + crecv[op, kind, x, n, :].astype(F32)
         got(xrecv.at[op, kind, n], rxs.at[op, kind])
         return near + xrecv[op, kind, n, :].astype(F32)
@@ -508,24 +544,25 @@
         got(buf.at[xcp[1], rows], rag.at[op, kind, xcp[1]])
         return jnp.concatenate([buf[s, rows, :] for s in range(4)], axis=1)
 
-    for dr in (1, 2, 3):
-        rr = (r + dr) % 4
-        got(xv.at[:, rr], rx.at[0, 0, rr])
+    weight_r = wr[...].reshape(512, 512)
+    for k in range(4):
+        local["xv", k].wait()
+    for dev in rest:
+        got(xv.at[:, dev[1]], rx.at[0, 0, dev[1]])
     scatter_start(0, 0, dot(xv[...].reshape(NV, 512), weight_r))
-    for dr in (1, 2, 3):
-        rr = (r + dr) % 4
-        got(xc.at[rr], rx.at[0, 1, rr])
+    for k in range(4):
+        local["xc", k].wait()
+    for dev in rest:
+        got(xc4.at[dev[1]], rx.at[0, 1, dev[1]])
+    xc[...] = xc4[...].reshape(4, 64, 512)
     scatter_start(0, 1, dot(xc[...].reshape(NC, 512), weight_r))
     scatter_mid(0, 0)
     scatter_mid(0, 1)
-    pass_on(1, lambda ii: ws.at[:, ii])
-
-    for dz in (1, 2, 3):
-        ii = 2 * zpeer(dz) + y
-        got(pg.at[ii], rpg.at[ii])
-    for dz in range(4):
-        ii = 2 * zpeer(dz) + 1 - y
-        got(pg.at[ii], rpg.at[ii])
+    spread_c(cot_crops, cc4, 1, rest[:1])
+    line_pass(1, parts_ws, 0)
+
+    for dev in peers[:7]:
+        got(pg.at[dev[0]], rpg.at[dev[0]])
     half = lax.broadcasted_iota(jnp.int32, (1, 128), 1) < 64
     gain1, shift1, gain2, shift2 = [
         jnp.where(half, pg[2 * r, q : q + 1, :], pg[2 * r + 1, q : q + 1, :]) for q in range(4)
@@ -534,7 +571,9 @@
     shift3 = jnp.concatenate([pg[2 * k + c, pl.ds(6 + x, 1), :] for k in range(4)], axis=1)
 
     def norm_act(values, rows, gain, shift):
-        mean, rstd = stats(values, rows)
+        mean = jnp.sum(values, axis=0, keepdims=True) / rows
+        second = jnp.sum(values * values, axis=0, keepdims=True) / rows
+        rstd = lax.rsqrt(second - mean * mean + EPSILON)
         xhat = (values - mean) * rstd
         norm = gain * xhat + shift
         sig = sigmoid(norm)
@@ -547,10 +586,17 @@
         gather_start(0, kind, act1, act)
         xhat1[kind_rows(kind), :] = xh
         slope1[kind_rows(kind), :] = sl
-    pass_on(2, lambda ii: we.at[ii])
+    spread_v(cot_views, cv, 1, rest[1:])
+    spread_c(cot_crops, cc4, 1, rest[1:])
+    line_pass(1, parts_ws, 1)
+    line_pass(1, parts_ws, 2)
+    for k in range(4):
+        local["we", k].wait()
+    line_send(2, whole_we)
     for kind in range(2):
         gather_mid(0, kind, act1)
-    arrived(1, lambda ii: ws.at[:, ii])
+    for h in range(3):
+        line_got(1, parts_ws_other, h)
 
     def weight_s():
         return jnp.concatenate([ws[t].reshape(512, 128) for t in range(9)], axis=1)
@@ -568,45 +614,42 @@
         gather_start(1, kind, act2, act)
         xhat2[kind_rows(kind), :] = xh
         slope2[kind_rows(kind), :] = sl
+    line_pass(2, whole_we, 0)
+    pool[...] = jnp.zeros_like(pool)
     for kind in range(2):
         gather_mid(1, kind, act2)
-    arrived(2, lambda ii: we.at[ii])
+    for k in range(4):
+        local["cv", k].wait()
+        local["cc", k].wait()
+    for dev in rest:
+        got(cv.at[:, dev[1]], rx.at[1, 0, dev[1]])
+        got(cc4.at[dev[1]], rx.at[1, 1, dev[1]])
+    cc[...] = cc4[...].reshape(4, 64, 512)
+    line_got(2, whole_we_other, 0)
     weight_e = we[...].reshape(512, 512)
 
-    for own in local[14:]:
-        own.wait()
-    for dr in (1, 2, 3):
-        rr = (r + dr) % 4
-        got(cv.at[:, rr], rx.at[1, 0, rr])
-        got(cc.at[rr], rx.at[1, 1, rr])
     sum_x3, sum_d3 = [], []
-    pool[...] = jnp.zeros_like(pool)
-    for kind in range(2):
+    zero8 = jnp.zeros((8, 512), F32)
+
+    def expand(kind):
         start, rows = KINDS[kind]
-        full2 = gather_end(1, kind, act2)
-        ex[kind_rows(kind), :] = dot(full2, weight_e)
-
-        def moments(b, acc, start=start):
+        ex[kind_rows(kind), :] = dot(gather_end(1, kind, act2), weight_e)
+
+        def moments(b, acc):
             e = ex[pl.ds(pl.multiple_of(start + 32 * b, 32), 32), :].reshape(4, 8, 512)
             return acc[0] + jnp.sum(e, axis=0), acc[1] + jnp.sum(e * e, axis=0)
 
-        zero8 = jnp.zeros((8, 512), F32)
         tot, sq = lax.fori_loop(0, rows // 32, moments, (zero8, zero8))
         mean = jnp.sum(tot, axis=0, keepdims=True) / rows
         rstd = lax.rsqrt(jnp.sum(sq, axis=0, keepdims=True) / rows - mean * mean + EPSILON)
-        rstd3[kind] = rstd
-
-        def finish(b, acc, kind=kind, start=start, mean=mean, rstd=rstd):
+
+        def finish(b, acc):
             rs = pl.ds(pl.multiple_of(start + 16 * b, 16), 16)
+            qs = pl.ds(pl.multiple_of(16 * (b % 4), 16), 16)
             xhat = (ex[rs, :] - mean) * rstd
             ex[rs, :] = xhat
-            if kind == 0:
-                src = xv[b // 4, b % 4]
-                cot = cv[b // 4, b % 4]
-            else:
-                qs = pl.ds(pl.multiple_of(16 * (b % 4), 16), 16)
-                src = xc[b // 4, qs, :]
-                cot = cc[b // 4, qs, :]
+            src = xv[b // 4, b % 4] if kind == 0 else xc[b // 4, qs, :]
+            cot = cv[b // 4, b % 4] if kind == 0 else cc[b // 4, qs, :]
             pre = src.astype(F32) + (gain3 * xhat + shift3)
             sig = sigmoid(pre)
             activation = pre * sig
@@ -617,9 +660,8 @@
                 pool[b // 4] += activation[:8] + activation[8:]
             else:
                 oc[b // 4, qs, :] = activation.astype(BF16)
-                m = 8 + 2 * (b % 4)
-                pool[m] += activation[:8]
-                pool[m + 1] += activation[8:]
+                pool[8 + 2 * (b % 4)] += activation[:8]
+                pool[9 + 2 * (b % 4)] += activation[8:]
             dx = d * xhat
             return acc[0] + (d[:8] + d[8:]), acc[1] + (dx[:8] + dx[8:])
 
@@ -630,63 +672,95 @@
         scale = gain3 * rstd
         mean_d, mean_x = sd / rows, sxx / rows
 
-        def back(b, _, start=start, scale=scale, mean_d=mean_d, mean_x=mean_x):
+        def back(b, _):
             rs = pl.ds(pl.multiple_of(start + 32 * b, 32), 32)
             dex[rs, :] = (scale * (dpre[rs, :] - mean_d - ex[rs, :] * mean_x)).astype(BF16)
             return 0
 
         lax.fori_loop(0, rows // 32, back, 0)
-        scatter_start(1, kind, dot(dex[kind_rows(kind), :], weight_e, NT))
-
-    def hand_out(src_v, src_c, dst_v, dst_c, s):
-        for dr in (1, 2, 3, 0):
-            rr = (r + dr) % 4
+
+    def hand_v(src, dst, s, devs):
+        for dev in devs:
+            dr = (dev[1] + 4 - r) % 4
             for k in range(4):
-                kl = pl.ds(128 * k, 128)
-                if dr:
-                    copy(src_v.at[:, rr, :, kl], dst_v.at[:, :, lanes(k, x, c)], sout.at[s, 0, dr, k], rout.at[s, 0, r, k], (i, rr)).start()
-                    copy(src_c.at[rr, :, kl], dst_c.at[:, lanes(k, x, c)], sout.at[s, 1, dr, k], rout.at[s, 1, r, k], (i, rr)).start()
+                copy(src.at[:, dev[1], :, kl(k)], dst.at[:, :, lanes(k, x, c)], sout.at[s, 0, dr, k], rout.at[s, 0, r, k], dev).start()
+
+    def hand_c(src, dst, s, devs):
+        for dev in devs:
+            dr = (dev[1] + 4 - r) % 4
+            for k in range(4):
+                copy(src.at[dev[1], :, kl(k)], dst.at[:, lanes(k, x, c)], sout.at[s, 1, dr, k], rout.at[s, 1, r, k], dev).start()
+
+    def hand_own(src_v, src_c, dst_v, dst_c, s, end=False):
+        for k in range(4):
+            for m, (src, dst) in enumerate(
+                ((src_v.at[:, r, :, kl(k)], dst_v.at[:, :, lanes(k, x, c)]), (src_c.at[r, :, kl(k)], dst_c.at[:, lanes(k, x, c)]))
+            ):
+                own = pltpu.make_async_copy(src, dst, sout.at[s, m, 0, k])
+                if end:
+                    own.wait()
                 else:
-                    pltpu.make_async_copy(src_v.at[:, r, :, kl], dst_v.at[:, :, lanes(k, x, c)], sout.at[s, 0, 0, k]).start()
-                    pltpu.make_async_copy(src_c.at[r, :, kl], dst_c.at[:, lanes(k, x, c)], sout.at[s, 1, 0, k]).start()
+                    own.start()
 
     def handed(src_v, src_c, dst_v, dst_c, s):
-        for dr in (1, 2, 3, 0):
-            rr = (r + dr) % 4
+        hand_own(src_v, src_c, dst_v, dst_c, s, True)
+        for dev in rest:
+            rr = dev[1]
+            dr = (rr + 4 - r) % 4
             for k in range(4):
-                kl = pl.ds(128 * k, 128)
-                if dr:
-                    copy(src_v.at[:, rr, :, kl], dst_v.at[:, :, lanes(k, x, c)], sout.at[s, 0, dr, k], rout.at[s, 0, r, k], (i, rr)).wait_send()
-                    copy(src_c.at[rr, :, kl], dst_c.at[:, lanes(k, x, c)], sout.at[s, 1, dr, k], rout.at[s, 1, r, k], (i, rr)).wait_send()
-                    got(dst_v.at[:, :, lanes(k, rr // 2, rr % 2)], rout.at[s, 0, rr, k])
-                    got(dst_c.at[:, lanes(k, rr // 2, rr % 2)], rout.at[s, 1, rr, k])
-                else:
-                    pltpu.make_async_copy(src_v.at[:, r, :, kl], dst_v.at[:, :, lanes(k, x, c)], sout.at[s, 0, 0, k]).wait()
-                    pltpu.make_async_copy(src_c.at[r, :, kl], dst_c.at[:, lanes(k, x, c)], sout.at[s, 1, 0, k]).wait()
-
-    scatter_mid(1, 0)
-    scatter_mid(1, 1)
-
-    ge[...] = dot(jnp.concatenate([act2[s] for s in range(4)], axis=1), dex[...], TN).reshape(4, 2, 64, 512)
-
-    def grad_y(full, send, recv, q):
-        send[...] = full[:, 1 - y].astype(BF16)
-        copy(send, recv, sgy.at[q], rgy.at[q], yp).start()
-
-    def grad_z(full, yrecv, send, recv, q):
-        got(yrecv, rgy.at[q])
-        for dz in (1, 2, 3):
-            k = zpeer(dz)
-            send[k] = (full[k, y] + yrecv[k].astype(F32)).astype(BF16)
-            copy(send.at[k], recv.at[z], sgz.at[q, dz], rgz.at[q, z], (2 * k + y, r)).start()
-
-    def grad_sum(full, yrecv, recv, q):
-        total = full[z, y] + yrecv[z].astype(F32)
-        for dz in (1, 2, 3):
-            k = zpeer(dz)
+                sent(src_v.at[:, rr, :, kl(k)], sout.at[s, 0, dr, k])
+                sent(src_c.at[rr, :, kl(k)], sout.at[s, 1, dr, k])
+                got(dst_v.at[:, :, lanes(k, rr // 2, rr % 2)], rout.at[s, 0, rr, k])
+                got(dst_c.at[:, lanes(k, rr // 2, rr % 2)], rout.at[s, 1, rr, k])
+
+    far_of = jnp.where(middle, z + 2 * step, z + 3 * step)
+    mid_of = jnp.where(middle, z - step, z + 2 * step)
+    order = [far_of, mid_of, z + step, z]
+
+    def grad_y(full, send, recv, q, both):
+        for k in order:
+            send[k] = (full[k, 1 - y] if both else full[k]).astype(BF16)
+            copy(send.at[k], recv.at[k], sgy.at[q, k], rgy.at[q, k], yp).start()
+
+    def grad_add(full, yrecv, q, k, both):
+        got(yrecv.at[k], rgy.at[q, k])
+        return (full[k, y] if both else full[k]) + yrecv[k].astype(F32)
+
+    def grad_z(full, yrecv, send, recv, relay, q, n, both=True):
+        k = order[n]
+        if n == 0:
+
+            @pl.when(jnp.logical_not(middle))
+            def _():
+                send[k] = grad_add(full, yrecv, q, k, both).astype(BF16)
+                copy(send.at[k], relay, sgz.at[q, 0], rgz.at[q, 4], on_line(1)).start()
+
+        else:
+            send[k] = grad_add(full, yrecv, q, k, both).astype(BF16)
+            copy(send.at[k], recv.at[z], sgz.at[q, n], rgz.at[q, z], (2 * k + y, r)).start()
+
+    def grad_relay(full, yrecv, send, recv, relay, q, both=True):
+        @pl.when(middle)
+        def _():
+            k = order[0]
+            total = grad_add(full, yrecv, q, k, both)
+            got(relay, rgz.at[q, 4])
+            send[k] = (total + relay[...].astype(F32)).astype(BF16)
+            copy(send.at[k], recv.at[z], sgz.at[q, 0], rgz.at[q, z], (2 * k + y, r)).start()
+
+    def grad_sum(full, yrecv, recv, acc, q, both=True):
+        acc[...] = grad_add(full, yrecv, q, z, both)
+        for k in (z + step, z + 2 * step):
             got(recv.at[k], rgz.at[q, k])
-            total = total + recv[k].astype(F32)
-        return total
+            acc[...] += recv[k].astype(F32)
+
+        @pl.when(middle)
+        def _():
+            k = z - step
+            got(recv.at[k], rgz.at[q, k])
+            acc[...] += recv[k].astype(F32)
+
+        return acc[...]
 
     def fin_start(buf, value, q):
         buf[r] = value.astype(BF16)
@@ -701,7 +775,18 @@
         got(buf.at[cp[1]], rfin.at[q, cp[1]])
         got(buf.at[xcp[1]], rfin.at[q, xcp[1]])
 
-    grad_y(ge, ysend_e, yrecv_e, 0)
+    expand(0)
+    scatter_start(1, 0, dot(dex[kind_rows(0), :], weight_e, NT))
+    expand(1)
+    scatter_mid(1, 0)
+    scatter_start(1, 1, dot(dex[kind_rows(1), :], weight_e, NT))
+    ge[...] = dot(jnp.concatenate([act2[s] for s in range(4)], axis=1), dex[...], TN).reshape(4, 2, 64, 512)
+    grad_y(ge, ysend_e, yrecv_e, 0, True)
+    scatter_mid(1, 1)
+    hand_v(ov, out_views, 0, rest[:1])
+    hand_own(ov, oc, out_views, out_crops, 0)
+    hand_v(ov, out_views, 0, rest[2:])
+    hand_c(oc, out_crops, 0, rest[2:])
 
     def norm_back(d, xhat, rstd, gain, rows):
         sd = jnp.sum(d, axis=0, keepdims=True)
@@ -710,7 +795,7 @@
 
     sum_d2, sum_x2 = [], []
     for kind in range(2):
-        start, rows = KINDS[kind]
+        rows = KINDS[kind][1]
         d = scatter_end(1, kind) * slope2[kind_rows(kind), :]
         dz_, sd, sxx = norm_back(d, xhat2[kind_rows(kind), :], rstd2[kind], gain2, rows)
         sum_d2.append(sd)
@@ -722,16 +807,21 @@
                 t = 3 * ti + tj
                 pat[kind_rows(kind), 128 * t : 128 * t + 128] = moved(col, kind, ti - 1).astype(BF16)
         scatter_start(2, kind, dot(pat[kind_rows(kind), :], weight_s(), NT))
-    hand_out(ov, oc, out_views, out_crops, 0)
-    grad_z(ge, yrecv_e, zsend_e, zrecv_e, 0)
-    scatter_mid(2, 0)
+        if kind == 1:
+            scatter_mid(2, 0)
     scatter_mid(2, 1)
     gs[...] = dot(jnp.concatenate([act1[s] for s in range(4)], axis=1), pat[...], TN).reshape(4, 2, 64, 1152)
-    grad_y(gs, ysend_s, yrecv_s, 1)
+    grad_y(gs, ysend_s, yrecv_s, 1, True)
+    for n in range(4):
+        if n < 3:
+            grad_z(ge, yrecv_e, zsend_e, zrecv_e, relay_e, 0, n)
+        else:
+            grad_relay(ge, yrecv_e, zsend_e, zrecv_e, relay_e, 0)
+    hand_v(ov, out_views, 0, rest[1:2])
 
     sum_d1, sum_x1 = [], []
     for kind in range(2):
-        start, rows = KINDS[kind]
+        rows = KINDS[kind][1]
         d = scatter_end(2, kind) * slope1[kind_rows(kind), :]
         dz_, sd, sxx = norm_back(d, xhat1[kind_rows(kind), :], rstd1[kind], gain1, rows)
         sum_d1.append(sd)
@@ -744,9 +834,25 @@
     pgr[i] = jnp.concatenate(rows12 + rows3 + [jnp.zeros((4, 128), F32)], axis=0)
     for n, dev in enumerate(peers[:7]):
         copy(pgr.at[i], pgr.at[i], spp.at[n], rpp.at[0, i], dev).start()
-    grad_z(gs, yrecv_s, zsend_s, zrecv_s, 1)
+    hand_c(oc, out_crops, 0, rest[:2])
+
+    rows_pool[...] = jnp.zeros_like(rows_pool)
+    for n in range(8):
+        row = 4 * (n % 2) + n // 2
+        rows_pool[row : row + 1, :] = jnp.sum(pool[n], axis=0, keepdims=True) / 64.0
+        for m in range(2):
+            row = 4 * (2 + 2 * (n % 2) + m) + n // 2
+            rows_pool[row : row + 1, :] = jnp.sum(pool[8 + n, 4 * m : 4 * m + 4, :], axis=0, keepdims=True) / 16.0
+    own_pool[...] = rows_pool[...].astype(BF16)
+    for k in range(4):
+        pltpu.make_async_copy(own_pool.at[:, kl(k)], pooled.at[:, lanes(k, x, c)], spool.at[0, k]).start()
+        for n, dev in enumerate(rest):
+            copy(own_pool.at[:, kl(k)], pooled.at[:, lanes(k, x, c)], spool.at[1 + n, k], rpool.at[r, k], dev).start()
+
+    grad_z(gs, yrecv_s, zsend_s, zrecv_s, relay_s, 1, 0)
     for kind in range(2):
         gather_mid(2, kind, dred)
+    grad_z(gs, yrecv_s, zsend_s, zrecv_s, relay_s, 1, 1)
     full_d = [gather_end(2, kind, dred) for kind in range(2)]
 
     for m in range(4):
@@ -755,54 +861,25 @@
 
     @pl.when(y != c)
     def _():
-        ysend_r[...] = gr[...].astype(BF16)
-        copy(ysend_r, yrecv_r, sgy.at[2], rgy.at[2], yp).start()
-
-    for kind in range(2):
-        start, rows = KINDS[kind]
-        grad = (dpre[kind_rows(kind), :] + dot(full_d[kind], weight_r, NT)).astype(BF16)
-        if kind == 0:
-            gv[...] = grad.reshape(8, 4, 16, 512)
-        else:
-            gc[...] = grad.reshape(4, 64, 512)
+        grad_y(gr, ysend_r, yrecv_r, 2, False)
+
+    grad_z(gs, yrecv_s, zsend_s, zrecv_s, relay_s, 1, 2)
+    grad_relay(gs, yrecv_s, zsend_s, zrecv_s, relay_s, 1)
+    fin_start(fin_e, grad_sum(ge, yrecv_e, zrecv_e, acc_e, 0), 0)
+    gv[...] = (dpre[kind_rows(0), :] + dot(full_d[0], weight_r, NT)).astype(BF16).reshape(8, 4, 16, 512)
+    hand_v(gv, grad_views, 1, rest)
+    gc[...] = (dpre[kind_rows(1), :] + dot(full_d[1], weight_r, NT)).astype(BF16).reshape(4, 64, 512)
+    hand_c(gc, grad_crops, 1, rest)
+    hand_own(gv, gc, grad_views, grad_crops, 1)
 
     @pl.when(y == c)
     def _():
-        got(yrecv_r, rgy.at[2])
-        for dz in (1, 2, 3):
-            k = zpeer(dz)
-            zsend_r[k] = (gr[k] + yrecv_r[k].astype(F32)).astype(BF16)
-            copy(zsend_r.at[k], zrecv_r.at[z], sgz.at[2, dz], rgz.at[2, z], (2 * k + y, r)).start()
-
-    hand_out(gv, gc, grad_views, grad_crops, 1)
-    fin_start(fin_e, grad_sum(ge, yrecv_e, zrecv_e, 0), 0)
-    fin_start(fin_s, grad_sum(gs, yrecv_s, zrecv_s, 1), 1)
-
-    for n in range(8):
-        row = 4 * (n % 2) + n // 2
-        own_pool[row : row + 1, :] = jnp.sum(pool[n], axis=0, keepdims=True) / 64.0
-        for m in range(2):
-            row = 4 * (2 + 2 * (n % 2) + m) + n // 2
-            own_pool[row : row + 1, :] = jnp.sum(pool[8 + n, 4 * m : 4 * m + 4, :], axis=0, keepdims=True) / 16.0
-    for k in range(4):
-        kl = pl.ds(128 * k, 128)
-        pltpu.make_async_copy(own_pool.at[:, kl], pooled.at[:, lanes(k, x, c)], spool.at[0, k]).start()
-        for dr in (1, 2, 3):
-            copy(own_pool.at[:, kl], pooled.at[:, lanes(k, x, c)], spool.at[dr, k], rpool.at[r, k], (i, (r + dr) % 4)).start()
-
-    @pl.when(y == c)
-    def _():
-        total = gr[z] + yrecv_r[z].astype(F32)
-        for dz in (1, 2, 3):
-            k = zpeer(dz)
-            got(zrecv_r.at[k], rgz.at[2, k])
-            total = total + zrecv_r[k].astype(F32)
-        fin_r[x] = total.astype(BF16)
-        for n, dev in enumerate((xp, cp, xcp)):
-            copy(fin_r.at[x], fin_r.at[x], sfin.at[2, n], rfin.at[2, x], dev).start()
-
+        for n in range(3):
+            grad_z(gr, yrecv_r, zsend_r, zrecv_r, relay_r, 2, n, False)
+        grad_relay(gr, yrecv_r, zsend_r, zrecv_r, relay_r, 2, False)
+
+    fin_start(fin_s, grad_sum(gs, yrecv_s, zrecv_s, acc_s, 1), 1)
     fin_mid(fin_e, 0)
-    fin_mid(fin_s, 1)
 
     total = pgr[i]
     for n in range(7):
@@ -810,80 +887,119 @@
         got(pgr.at[ii], rpp.at[0, ii])
         total = total + pgr[ii]
     pgs[r] = total
-    for n, dev in enumerate((xp, cp, xcp)):
+    for n, dev in enumerate(rest):
         copy(pgs.at[r], pgs.at[r], spp.at[7 + n], rpp.at[1, r], dev).start()
 
+    @pl.when(y == c)
+    def _():
+        fin_r[x] = grad_sum(gr, yrecv_r, zrecv_r, acc_r, 2, False).astype(BF16)
+        for n, dev in enumerate(rest):
+            copy(fin_r.at[x], fin_r.at[x], sfin.at[2, n], rfin.at[2, x], dev).start()
+
+    fin_mid(fin_s, 1)
     fin_end(fin_e, 0)
-    for s in range(4):
-        for k in range(4):
-            lo = 512 * k + 256 * (s % 2) + 128 * (s // 2)
-            grad_expand[:, lo : lo + 128] = fin_e[s, :, 128 * k : 128 * k + 128].astype(F32)
     fin_end(fin_s, 1)
-    for s in range(4):
-        for t in range(9):
-            grad_spatial[t, :, 128 * s : 128 * s + 128] = fin_s[s, :, 128 * t : 128 * t + 128].astype(F32)
-    for dr in (1, 2, 3):
-        rr = (r + dr) % 4
-        got(pgs.at[rr], rpp.at[1, rr])
-    grad_params[...] = pgs[...]
-
+    for dev in rest:
+        got(pgs.at[dev[1]], rpp.at[1, dev[1]])
+    handed(ov, oc, out_views, out_crops, 0)
+    handed(gv, gc, grad_views, grad_crops, 1)
+    for k in range(4):
+        pltpu.make_async_copy(own_pool.at[:, kl(k)], pooled.at[:, lanes(k, x, c)], spool.at[0, k]).wait()
+        for n, dev in enumerate(rest):
+            sent(own_pool.at[:, kl(k)], spool.at[1 + n, k])
+            got(pooled.at[:, lanes(k, dev[1] // 2, dev[1] % 2)], rpool.at[dev[1], k])
     got(fin_r.at[1 - x], rfin.at[2, 1 - x])
 
     @pl.when(y != c)
     def _():
         got(fin_r.at[x], rfin.at[2, x])
 
-    for n in range(2):
-        grad_reduce[128 * n : 128 * n + 128, :] = fin_r[n].astype(F32)
-
-    handed(ov, oc, out_views, out_crops, 0)
-    handed(gv, gc, grad_views, grad_crops, 1)
-    for k in range(4):
-        kl = pl.ds(128 * k, 128)
-        pltpu.make_async_copy(own_pool.at[:, kl], pooled.at[:, lanes(k, x, c)], spool.at[0, k]).wait()
+    for s, (src_v, src_c) in enumerate(((views, crops), (cot_views, cot_crops))):
         for dr in (1, 2, 3):
-            rr = (r + dr) % 4
-            sent(own_pool.at[:, kl], spool.at[dr, k])
-            got(pooled.at[:, lanes(k, rr // 2, rr % 2)], rpool.at[rr, k])
-    spread_sent(views, crops, 0)
-    spread_sent(cot_views, cot_crops, 1)
+            for k in range(4):
+                sent(src_v.at[:, :, kl(k)], sx.at[s, 0, dr, k])
+                sent(src_c.at[:, :, kl(k)], sx.at[s, 1, dr, k])
     for n in range(7):
         sent(pg.at[i], spg.at[n])
     for n in range(10):
         sent(pgs.at[r], spp.at[n])
-    for n in range(7):
-        sent(ws_own, sw.at[1, n])
-        sent(we_own, sw.at[2, n])
+    line_sent(1, parts_ws)
+    line_sent(2, whole_we)
     for kind in range(2):
         n = pl.ds(0, KINDS[kind][1])
         for op in range(3):
-            sent(csend.at[op, kind, :, n], scs.at[op, kind])
+            for xx in range(2):
+                sent(csend.at[op, kind, xx, n], scs.at[op, kind, xx])
             sent(xsend.at[op, kind, n], sxs.at[op, kind])
             for m in range(3):
                 sent(act1.at[r, kind_rows(kind)], sag.at[op, kind, m])
     for q, (ys, zs, fin) in enumerate(((ysend_e, zsend_e, fin_e), (ysend_s, zsend_s, fin_s))):
-        sent(ys, sgy.at[q])
-        for dz in (1, 2, 3):
-            sent(zs.at[z], sgz.at[q, dz])
+        for k in range(4):
+            sent(ys.at[k], sgy.at[q, k])
+        for n in range(3):
+            sent(zs.at[z], sgz.at[q, n])
         for n in range(3):
             sent(fin.at[r], sfin.at[q, n])
 
     @pl.when(y != c)
     def _():
-        sent(ysend_r, sgy.at[2])
+        for k in range(4):
+            sent(ysend_r.at[k], sgy.at[2, k])
 
     @pl.when(y == c)
     def _():
-        for n in range(7):
-            sent(wr_own, sw.at[0, n])
-        for dz in (1, 2, 3):
-            sent(zsend_r.at[z], sgz.at[2, dz])
+        line_sent(0, whole_wr)
+        for n in range(3):
+            sent(zsend_r.at[z], sgz.at[2, n])
         for n in range(3):
             sent(fin_r.at[x], sfin.at[2, n])
 
 
-def fused(views, crops, w_reduce, w_spatial, w_expand, cot_views, cot_crops, params):
-    hbm, vmem = pl.BlockSpec(memory_space=pl.ANY), pl.BlockSpec(memory_space=pltpu.VMEM)
+def store_kernel(
+    out_v, out_c, pool, grad_v, grad_c, fin_e, fin_s, fin_r, sums,
+    out_views, out_crops, pooled, grad_views, grad_crops, grad_reduce, grad_spatial, grad_expand,
+    gain_a, shift_a, gain_b, shift_b, gain_c, shift_c,
+    oc, pl_, gc, gr, gs, ge, sem,
+):
+    i = lax.axis_index("dp")
+    z, y = i // 2, i % 2
+    copies = []
+
+    def store(src, dst):
+        one = pltpu.make_async_copy(src, dst, sem.at[len(copies)])
+        one.start()
+        copies.append(one)
+
+    store(out_v, out_views)
+    store(grad_v, grad_views)
+    for s in range(4):
+        for t in range(9):
+            gs[t, :, 128 * s : 128 * s + 128] = fin_s[s, :, 128 * t : 128 * t + 128].astype(F32)
+    store(gs, grad_spatial)
+    for s in range(4):
+        for k in range(4):
+            lo = 512 * k + 256 * (s % 2) + 128 * (s // 2)
+            ge[:, lo : lo + 128] = fin_e[s, :, 128 * k : 128 * k + 128].astype(F32)
+    store(ge, grad_expand)
+    gr[...] = fin_r[...].astype(F32).reshape(256, 512)
+    store(gr, grad_reduce)
+    oc[...] = out_c[...].reshape(16, 4, 2048)
+    store(oc, out_crops)
+    gc[...] = grad_c[...].reshape(16, 4, 2048)
+    store(gc, grad_crops)
+    pl_[...] = pool[0:24, :].astype(F32).reshape(6, 4, 2048)
+    store(pl_, pooled)
+    for n, out in enumerate((gain_a, shift_a, gain_b, shift_b)):
+        row = sums[i // 2, n : n + 1, :]
+        out[...] = jnp.where(i % 2 == 0, row[:, :64], row[:, 64:]).reshape(64)
+    for n, out in enumerate((gain_c, shift_c)):
+        out[...] = jnp.concatenate([sums[2 * m + y, pl.ds(4 + 4 * n + z, 1), :] for m in range(2)], axis=1).reshape(256)
+    for one in copies:
+        one.wait()
+
+
+def fused(views, crops, w_reduce, w_spatial, w_expand, cot_views, cot_crops, *params):
+    hbm, vmem = pl.BlockSpec(memory_space=pltpu.HBM), pl.BlockSpec(memory_space=pltpu.VMEM)
 
     def shape(dims, dtype):
         return jax.ShapeDtypeStruct(dims, dtype)
@@ -894,39 +1010,56 @@
     def dma(*dims):
         return pltpu.SemaphoreType.DMA(dims)
 
-    return pl.pallas_call(
+    held = pl.pallas_call(
         block_kernel,
         out_shape=[
-            shape((8, 16, 2048), BF16), shape((64, 2048), BF16), shape((24, 2048), F32),
-            shape((8, 16, 2048), BF16), shape((64, 2048), BF16),
-            shape((256, 512), F32), shape((9, 64, 512), F32), shape((64, 2048), F32), shape((4, 16, 128), F32),
+            buf((8, 16, 2048)), buf((64, 2048)), buf((32, 2048)), buf((8, 16, 2048)), buf((64, 2048)),
+            buf((4, 64, 512)), buf((4, 64, 1152)), buf((2, 128, 512)), buf((4, 16, 128), F32),
         ],
-        in_specs=[hbm] * 8,
-        out_specs=[hbm] * 5 + [vmem] * 4,
+        in_specs=[hbm] * 13,
+        out_specs=[vmem] * 9,
         scratch_shapes=[
-            buf((8, 4, 16, 512)), buf((4, 64, 512)), buf((8, 4, 16, 512)), buf((4, 64, 512)),
-            buf((4, 128, 512)), buf((9, 8, 64, 128)), buf((8, 64, 512)), buf((8, 8, 128), F32),
+            buf((8, 4, 16, 512)), buf((4, 16, 4, 512)), buf((4, 64, 512)),
+            buf((8, 4, 16, 512)), buf((4, 16, 4, 512)), buf((4, 64, 512)),
+            buf((4, 128, 512)), buf((9, 8, 64, 128)), buf((8, 64, 512)), buf((64,)), buf((64,)), buf((64,)), buf((64,)), buf((256,)), buf((256,)), buf((8, 8, 128), F32),
             buf((3, 4, N, 128), F32), buf((3, 2, 2, NV, 128)), buf((3, 2, 2, NV, 128)),
             buf((3, 2, NV, 128)), buf((3, 2, NV, 128)),
             buf((4, N, 128)), buf((4, N, 128)), buf((4, N, 128)), buf((N, 1152), F32),
             buf((N, 128), F32), buf((N, 128), F32), buf((N, 128), F32), buf((N, 128), F32),
             buf((N, 512), F32), buf((N, 512), F32), buf((N, 512)), buf((N, 1152)),
             buf((8, 4, 16, 512)), buf((4, 64, 512)), buf((8, 4, 16, 512)), buf((4, 64, 512)),
-            buf((16, 8, 512), F32), buf((24, 512), F32),
+            buf((16, 8, 512), F32), buf((32, 512), F32), buf((32, 512)),
             buf((4, 2, 64, 512), F32), buf((4, 2, 64, 1152), F32), buf((4, 128, 512), F32),
             buf((4, 64, 512)), buf((4, 64, 512)), buf((4, 64, 512)), buf((4, 64, 512)),
             buf((4, 64, 1152)), buf((4, 64, 1152)), buf((4, 64, 1152)), buf((4, 64, 1152)),
             buf((4, 128, 512)), buf((4, 128, 512)), buf((4, 128, 512)), buf((4, 128, 512)),
-            buf((4, 64, 512)), buf((4, 64, 1152)), buf((2, 128, 512)),
-            buf((8, 16, 128), F32), buf((4, 16, 128), F32),
-            dma(24), dma(2, 2, 4, 4), dma(2, 2, 4), dma(3, 7), dma(3, 8), dma(7), dma(8),
-            dma(3, 2), dma(3, 2), dma(3, 2), dma(3, 2), dma(3, 2, 3), dma(3, 2, 4),
-            dma(2, 2, 4, 4), dma(2, 2, 4, 4), dma(3), dma(3), dma(3, 4), dma(3, 4), dma(3, 3), dma(3, 4),
+            buf((64, 512)), buf((64, 1152)), buf((128, 512)), buf((64, 512), F32), buf((64, 1152), F32), buf((128, 512), F32),
+            buf((8, 16, 128), F32),
+            dma(32), dma(2, 2, 4, 4), dma(2, 2, 4), dma(3, 3, 8), dma(3, 3, 2, 4), dma(7), dma(8),
+            dma(3, 2, 2), dma(3, 2, 2), dma(3, 2), dma(3, 2), dma(3, 2, 3), dma(3, 2, 4),
+            dma(2, 2, 4, 4), dma(2, 2, 4, 4), dma(3, 4), dma(3, 4), dma(3, 4), dma(3, 5), dma(3, 3), dma(3, 4),
             dma(10), dma(2, 8), dma(4, 4), dma(4, 4),
         ],
-        compiler_params=pltpu.CompilerParams(collective_id=0, has_side_effects=True, vmem_limit_bytes=56 << 20),
+        compiler_params=pltpu.CompilerParams(collective_id=0, has_side_effects=True, vmem_limit_bytes=58 << 20),
         cost_estimate=pl.CostEstimate(flops=5_200_000_000, bytes_accessed=8_000_000, transcendentals=2_000_000),
-    )(views, crops, w_reduce, w_spatial, w_expand, cot_views, cot_crops, params)
+    )(views, crops, w_reduce, w_spatial, w_expand, cot_views, cot_crops, *params)
+    held = [pltpu.with_memory_space_constraint(one, pltpu.VMEM) for one in held]
+    return pl.pallas_call(
+        store_kernel,
+        out_shape=[
+            shape((8, 16, 2048), BF16), shape((16, 4, 2048), BF16), shape((6, 4, 2048), F32),
+            shape((8, 16, 2048), BF16), shape((16, 4, 2048), BF16),
+            shape((256, 512), F32), shape((9, 64, 512), F32), shape((64, 2048), F32),
+            shape((64,), F32), shape((64,), F32), shape((64,), F32), shape((64,), F32), shape((256,), F32), shape((256,), F32),
+        ],
+        in_specs=[vmem] * 9,
+        out_specs=[hbm] * 8 + [vmem] * 6,
+        scratch_shapes=[
+            buf((16, 4, 2048)), buf((6, 4, 2048), F32), buf((16, 4, 2048)),
+            buf((256, 512), F32), buf((9, 64, 512), F32), buf((64, 2048), F32), dma(8),
+        ],
+        compiler_params=pltpu.CompilerParams(vmem_limit_bytes=16 << 20),
+    )(*held)
 
 
 def step(
@@ -939,35 +1072,26 @@
     )
     if (dp, rows) != (8, 4) or views.shape != (4, 2, 2, 8, 2048) or crops.shape != (4, 4, 1, 4, 2048):
         return body(*args)
-    params = jnp.concatenate(
-        [jnp.concatenate([v, v]) for v in (gain_one, shift_one, gain_two, shift_two)] + [gain_three, shift_three]
-    ).astype(F32).reshape(8, 128)
-    outs = fused(
-        views.reshape(8, 16, 2048), crops.reshape(64, 2048), w_reduce, w_spatial.reshape(9, 64, 512), w_expand,
-        cot_views.reshape(8, 16, 2048), cot_crops.reshape(64, 2048), params,
+    out_v, out_c, pooled, grad_v, grad_c, grad_r, grad_s, grad_e, ga, sa, gb, sb, gc, sc = fused(
+        views.reshape(8, 16, 2048), crops.reshape(16, 4, 2048), w_reduce, w_spatial.reshape(9, 64, 512), w_expand,
+        cot_views.reshape(8, 16, 2048), cot_crops.reshape(16, 4, 2048),
+        gain_one, shift_one, gain_two, shift_two, gain_three, shift_three,
     )
-    out_v, out_c, pooled, grad_v, grad_c, grad_r, grad_s, grad_e, grads = outs
-    i = lax.axis_index("dp")
-    small = lax.dynamic_index_in_dim(grads, i // 2, 0, keepdims=False)[:4]
-    small = lax.dynamic_slice_in_dim(small, 64 * (i % 2), 64, axis=1)
-    wide = grads.reshape(2, 2, 16, 128)[:, :, 4:12].reshape(2, 2, 2, 4, 128)
-    wide = lax.dynamic_index_in_dim(wide, i % 2, 1, keepdims=False)
-    wide = lax.dynamic_index_in_dim(wide, i // 2, 2, keepdims=False)
     return (
         out_v.reshape(views.shape),
         out_c.reshape(crops.shape),
-        jnp.transpose(pooled.reshape(6, 4, 2048), (1, 0, 2)),
+        jnp.transpose(pooled, (1, 0, 2)),
         grad_v.reshape(views.shape),
         grad_c.reshape(crops.shape),
         grad_r,
-        small[0],
-        small[1],
+        ga,
+        sa,
         grad_s.reshape(w_spatial.shape[:3] + (512,)),
-        small[2],
-        small[3],
+        gb,
+        sb,
         grad_e,
-        wide[:, 0].reshape(256),
-        wide[:, 1].reshape(256),
+        gc,
+        sc,
     )
 
 

time: 134 us -> 99.7 us (0.74)
  local copies, waits for them, and re-layouts: 21.7 us -> 0 us
  Pallas kernels: 109 us -> 98.1 us
    pallas_call x1 -> x2, Pallas kernels: 109 us -> 98.1 us  [the longest x1 95.5 us: fused(): pl.pallas_call(block_kernel, out_shape=[buf((8, 16, 2048)), buf((64, 2048...]
    reshape x5 -> x0, local copies, waits for them, and re-layouts: 7.71 us -> none  [the longest x1 1.76 us: step(): out_c.reshape(crops.shape)]
    concatenate x1 -> x0, local copies, waits for them, and re-layouts: 6.75 us -> none  [step(): jnp.concatenate([jnp.concatenate([v, v]) for v in (gain_one, shift_one, g...]
    unnamed x17 -> x0, local copies, waits for them, and re-layouts: 4.59 us -> none
    slice x3 -> x0, local copies, waits for them, and re-layouts: 2.08 us -> none  [the longest x1 0.76 us: step(): wide = grads.reshape(2, 2, 16, 128)[:, :, 4:12].reshape(2, 2, 2, 4, 128)]
where the time goes in v2:
time: 99.7 us; the launch traced here: 98.8 us
  Pallas kernels  98.1 us (98%)
    pallas_call x1, Pallas kernels, fused(): pl.pallas_call(block_kernel, out_shape=[buf((8, 16, 2048)), buf((64, 2048...  95.5 us
    pallas_call x1, Pallas kernels, fused(): pl.pallas_call(store_kernel, out_shape=[shape((8, 16, 2048), BF16), shape...  2.59 us

profile of v2, /device:TPU:0, one launch (start us, length us, event | category | flops | bytes accessed | tf_op | source)
XLA Modules:
  0.0 98.8 jit_solution(17992684766332667618)
XLA Ops:
  0.7 95.5 %shard_map.236 = (bf16[8,16,2048]{2,1,0:T(8,128)(2,1)S(1)}, bf16[64,2048]{1,0:T(8,128)(2,1)S(1)}, bf16[32,2048]{1,0:T(8,128)(2,1)S(1)}, bf16[8,16,2048]{2,1,0:T(...) custom-call(bf16[8,16,2048]{2,1,0:T(8,128)(2,1)} %bitcast.17, ...), custom_call_target="tpu_custom_call" | custom-call | flops 5200000000 | bytes 8000000 | tf_op jit(solution)/shard_map/pallas_call | solution.py:1013
  96.2 2.6 %shard_map.237 = (bf16[8,16,2048]{2,1,0:T(8,128)(2,1)}, bf16[16,4,2048]{2,1,0:T(4,128)(2,1)}, f32[6,4,2048]{2,1,0:T(4,128)}, bf16[8,16,2048]{2,1,0:T(8,128)(2,1)...) custom-call(bf16[8,16,2048]{2,1,0:T(8,128)(2,1)S(1)} %get-tuple-elem, ...), custom_call_target="tpu_custom_call" | custom-call | tf_op jit(solution)/shard_map/pallas_call | solution.py:1047

commit v3 on v2

--- a/solution.py
+++ b/solution.py
@@ -268,6 +268,7 @@
 
 
 MESH = pl.DeviceIdType.MESH
+SEMAPHORES = 159
 F32 = jnp.float32
 BF16 = jnp.bfloat16
 NV = 512
@@ -311,13 +312,13 @@
 
 def block_kernel(
     views, crops, w_reduce, w_spatial, w_expand, cot_views, cot_crops, gain_a, shift_a, gain_b, shift_b, gain_c, shift_c,
-    out_views, out_crops, pooled, grad_views, grad_crops, fin_e, fin_s, fin_r, pgs,
+    out_views, out_crops, fin_p, grad_views, grad_crops, fin_e, fin_s, fin_r, pgs,
     xv, xc4, xc, cv, cc4, cc, wr, ws, we, raw_a, raw_b, raw_c, raw_d, raw_e, raw_f, pg,
     part, csend, crecv, xsend, xrecv,
-    act1, act2, dred, conv, xhat1, slope1, xhat2, slope2, ex, dpre, dex, pat, ov, oc, gv, gc, pool, rows_pool, own_pool,
+    act1, act2, dred, conv, xhat1, slope1, xhat2, slope2, ex, dpre, dex, pat, ov, oc, gv, gc, pool, rows_pool,
     ge, gs, gr, ysend_e, yrecv_e, zsend_e, zrecv_e, ysend_s, yrecv_s, zsend_s, zrecv_s, ysend_r, yrecv_r, zsend_r, zrecv_r,
     relay_e, relay_s, relay_r, acc_e, acc_s, acc_r, pgr,
-    loc, sx, rx, sw, rw, spg, rpg, scs, rcs, sxs, rxs, sag, rag, sout, rout, sgy, rgy, sgz, rgz, sfin, rfin, spp, rpp, spool, rpool,
+    sem,
 ):
     i, r = lax.axis_index("dp"), lax.axis_index("rows")
     z, y = i // 2, i % 2
@@ -334,16 +335,25 @@
     def on_line(places):
         return (2 * (z + places * step) + y, r)
 
+    taken = [0]
+
+    def new(count=1):
+        taken[0] += count
+        return taken[0] - count
+
     def copy(src, dst, send, recv, dev):
         return pltpu.make_async_remote_copy(
-            src_ref=src, dst_ref=dst, send_sem=send, recv_sem=recv, device_id=dev, device_id_type=MESH
+            src_ref=src, dst_ref=dst, send_sem=sem.at[send], recv_sem=sem.at[recv], device_id=dev, device_id_type=MESH
         )
 
-    def got(dst, recv):
-        copy(dst, dst, recv, recv, cp).wait_recv()
-
-    def sent(src, send):
-        copy(src, src, send, send, cp).wait_send()
+    def got(ref, recv):
+        copy(ref, ref, recv, recv, cp).wait_recv()
+
+    def sent(ref, send):
+        copy(ref, ref, send, send, cp).wait_send()
+
+    def stored(ref, one):
+        pltpu.make_async_copy(ref, ref, sem.at[one]).wait()
 
     def lanes(k, xx, cc_):
         return pl.ds(pl.multiple_of(512 * k + 256 * cc_ + 128 * xx, 128), 128)
@@ -354,31 +364,28 @@
     def kind_rows(kind):
         return pl.ds(*KINDS[kind])
 
-    local = {}
-
-    def stage(name, src, dst):
-        cp_ = pltpu.make_async_copy(src, dst, loc.at[len(local)])
-        cp_.start()
-        local[name] = cp_
-
-    wr_stage = pltpu.make_async_copy(w_reduce.at[pl.ds(pl.multiple_of(128 * x, 128), 128)], wr.at[z], loc.at[31])
+    def stage(src, dst, one):
+        pltpu.make_async_copy(src, dst, sem.at[one]).start()
+
+    l_wr, l_ws, l_we, l_gain = new(), new(), new(), new(6)
+    l_x, l_cot = (new(), new()), (new(), new())
 
     @pl.when(y == c)
     def _():
-        wr_stage.start()
-
-    stage("ws", w_spatial.at[:, :, pl.ds(pl.multiple_of(128 * r, 128), 128)], ws.at[:, i])
+        stage(w_reduce.at[pl.ds(pl.multiple_of(128 * x, 128), 128)], wr.at[z], l_wr)
+
+    stage(w_spatial.at[:, :, pl.ds(pl.multiple_of(128 * r, 128), 128)], ws.at[:, i], l_ws)
     raw = (raw_a, raw_b, raw_c, raw_d, raw_e, raw_f)
     for n, vec in enumerate((gain_a, shift_a, gain_b, shift_b, gain_c, shift_c)):
-        stage(("g", n), vec, raw[n])
+        stage(vec, raw[n], l_gain + n)
     for k in range(4):
-        stage(("we", k), w_expand.at[:, lanes(k, x, c)], we.at[i, :, kl(k)])
+        stage(views.at[:, :, lanes(k, x, c)], xv.at[:, r, :, kl(k)], l_x[0])
+        stage(crops.at[:, :, lanes(k, x, c)], xc4.at[r, :, :, kl(k)], l_x[1])
     for k in range(4):
-        stage(("xv", k), views.at[:, :, lanes(k, x, c)], xv.at[:, r, :, kl(k)])
-        stage(("xc", k), crops.at[:, :, lanes(k, x, c)], xc4.at[r, :, :, kl(k)])
+        stage(w_expand.at[:, lanes(k, x, c)], we.at[i, :, kl(k)], l_we)
     for k in range(4):
-        stage(("cv", k), cot_views.at[:, :, lanes(k, x, c)], cv.at[:, r, :, kl(k)])
-        stage(("cc", k), cot_crops.at[:, :, lanes(k, x, c)], cc4.at[r, :, :, kl(k)])
+        stage(cot_views.at[:, :, lanes(k, x, c)], cv.at[:, r, :, kl(k)], l_cot[0])
+        stage(cot_crops.at[:, :, lanes(k, x, c)], cc4.at[r, :, :, kl(k)], l_cot[1])
 
     bar = pltpu.get_barrier_semaphore()
     peers = [((i + n) % 8, r) for n in range(1, 8)] + [cp, xp, xcp]
@@ -386,44 +393,48 @@
         pl.semaphore_signal(bar, inc=1, device_id=dev, device_id_type=MESH)
     pl.semaphore_wait(bar, len(peers))
 
-    def whole_wr(k):
-        return (wr.at[k],)
-
-    def parts_ws(k):
-        return tuple(ws.at[pl.ds(3 * n, 3), 2 * k + y] for n in range(3))
-
-    def parts_ws_other(k):
-        return tuple(ws.at[pl.ds(3 * n, 3), 2 * k + 1 - y] for n in range(3))
-
-    def whole_we(k):
-        return (we.at[2 * k + y],)
-
-    def whole_we_other(k):
-        return (we.at[2 * k + 1 - y],)
-
-    def line_send(a, parts):
-        for h, own in enumerate(parts(z)):
-
-            def go(n, dev, own=own, h=h):
-                copy(own, own, sw.at[a, h, n], rw.at[a, h, y, z], dev).start()
-
-            go(0, on_line(2))
-            go(1, on_line(1))
+    class Share:
+        def __init__(self, parts, others):
+            self.parts, self.others = parts, others
+            count = len(parts(0))
+            self.send = new()
+            self.along_z = [new(3) for _ in range(count)]
+            self.along_y = [new() for _ in range(count)]
+
+    share_r = Share(lambda k: (wr.at[k],), None)
+    share_s = Share(
+        lambda k: tuple(ws.at[pl.ds(3 * h, 3), 2 * k + y] for h in range(3)),
+        lambda h: ws.at[pl.ds(3 * h, 3), pl.ds(0, 4)],
+    )
+    share_e = Share(lambda k: (we.at[2 * k + y],), lambda h: we.at[pl.ds(0, 4)])
+    passed_r = new()
+
+    inner = ((z + 1) // 2) * (2 - (z + 1) // 2)
+
+    def line_send(share):
+        for h, own in enumerate(share.parts(z)):
+
+            def go(slot, dev, own=own):
+                copy(own, own, share.send, slot, dev).start()
+
+            go(share.along_z[h], on_line(2))
+            go(share.along_z[h] + 2 - inner, on_line(1))
 
             @pl.when(middle)
-            def _(go=go):
-                go(2, on_line(-1))
-
-            go(3, yp)
-
-    def line_pass(a, parts, h):
-        def take(places, n, on=False):
-            k = z + places * step
-            ref = parts(k)[h]
-            got(ref, rw.at[a, h, y, k])
+            def _(go=go, h=h):
+                go(share.along_z[h] + 1, on_line(-1))
+
+            go(share.along_y[h], yp)
+
+    def line_pass(share, h, send=None):
+        send = share.send if send is None else send
+
+        def take(places, slot, on=False):
+            ref = share.parts(z + places * step)[h]
+            got(ref, share.along_z[h] + slot)
             if on:
-                copy(ref, ref, sw.at[a, h, 7], rw.at[a, h, y, k], on_line(-1)).start()
-            copy(ref, ref, sw.at[a, h, 4 + n], rw.at[a, h, y, k], yp).start()
+                copy(ref, ref, send, share.along_z[h] + 2, on_line(-1)).start()
+            copy(ref, ref, send, share.along_y[h], yp).start()
 
         @pl.when(middle)
         def _():
@@ -437,46 +448,42 @@
             take(1, 1)
             take(3, 2)
 
-    def line_got(a, parts_other, h):
-        for k in range(4):
-            got(parts_other(k)[h], rw.at[a, h, 1 - y, k])
-
-    def line_sent(a, parts):
-        for h, own in enumerate(parts(z)):
-            for n in (0, 1, 3, 4, 5, 6):
-                sent(own, sw.at[a, h, n])
-
-            @pl.when(middle)
-            def _(own=own, h=h):
-                sent(own, sw.at[a, h, 2])
-                sent(own, sw.at[a, h, 7])
+    def line_got(share):
+        for h, slot in enumerate(share.along_y):
+            got(share.others(h), slot)
+
+    def line_sent(send, for_middle, for_end):
+        @pl.when(middle)
+        def _():
+            sent(for_middle, send)
+
+        @pl.when(jnp.logical_not(middle))
+        def _():
+            sent(for_end, send)
 
     @pl.when(y == c)
     def _():
-        wr_stage.wait()
-        line_send(0, whole_wr)
+        stored(wr.at[z], l_wr)
+        line_send(share_r)
+
+    s_sx, s_rx = ((new(), new()), (new(), new())), ((new(), new()), (new(), new()))
 
     def spread_v(src, dst, s, devs):
         for dev in devs:
-            rr = dev[1]
             for k in range(4):
-                dr = (rr + 4 - r) % 4
-                copy(src.at[:, :, lanes(k, rr // 2, rr % 2)], dst.at[:, r, :, kl(k)], sx.at[s, 0, dr, k], rx.at[s, 0, r], dev).start()
+                copy(src.at[:, :, lanes(k, dev[1] // 2, dev[1] % 2)], dst.at[:, r, :, kl(k)], s_sx[s][0], s_rx[s][0], dev).start()
 
     def spread_c(src, dst, s, devs):
         for dev in devs:
-            rr = dev[1]
             for k in range(4):
-                dr = (rr + 4 - r) % 4
-                copy(src.at[:, :, lanes(k, rr // 2, rr % 2)], dst.at[r, :, :, kl(k)], sx.at[s, 1, dr, k], rx.at[s, 1, r], dev).start()
+                copy(src.at[:, :, lanes(k, dev[1] // 2, dev[1] % 2)], dst.at[r, :, :, kl(k)], s_sx[s][1], s_rx[s][1], dev).start()
 
     spread_v(views, xv, 0, rest)
     spread_c(crops, xc4, 0, rest)
-
     spread_v(cot_views, cv, 1, rest[:1])
 
     for n in range(6):
-        local["g", n].wait()
+        stored(raw[n], l_gain + n)
     pg[i] = jnp.zeros((8, 128), F32)
     for n in range(4):
         vec = raw[n][...].reshape(1, 64).astype(F32)
@@ -484,85 +491,81 @@
     for n in range(2):
         for m in range(2):
             pg[i, 4 + 2 * n + m : 5 + 2 * n + m, :] = raw[4 + n][128 * m : 128 * m + 128].reshape(1, 128).astype(F32)
-    for n, dev in enumerate(peers[:7]):
-        copy(pg.at[i], pg.at[i], spg.at[n], rpg.at[i], dev).start()
+    s_pg, r_pg = new(), new()
+    for dev in peers[:7]:
+        copy(pg.at[i], pg.at[i], s_pg, r_pg, dev).start()
 
     @pl.when(y == c)
     def _():
-        line_pass(0, whole_wr, 0)
+        line_pass(share_r, 0, passed_r)
+
+    stored(xv.at[:, r], l_x[0])
+    got(xv.at[:, pl.ds(0, 3)], s_rx[0][0])
+    stored(ws.at[:, i], l_ws)
+    line_send(share_s)
 
     @pl.when(y != c)
     def _():
-        for k in range(4):
-            got(wr.at[k], rw.at[0, 0, 1 - y, k])
-
-    local["ws"].wait()
-    line_send(1, parts_ws)
+        got(wr, share_r.along_y[0])
+
+    s_cs, r_cs = new(3), new(12)
+    s_xs, r_xs = new(3), new(6)
+    s_ag, r_ag = new(3), new(12)
 
     def scatter_start(op, kind, sums):
         rows = kind_rows(kind)
         n = pl.ds(0, KINDS[kind][1])
         for s in range(4):
             part[op, s, rows, :] = sums[:, 128 * s : 128 * s + 128]
-        for xx in (1 - x, x):
+        for near, xx in enumerate((1 - x, x)):
             csend[op, kind, xx, n, :] = part[op, 2 * xx + 1 - c, rows, :].astype(BF16)
             own = csend.at[op, kind, xx, n]
-            copy(own, crecv.at[op, kind, xx, n], scs.at[op, kind, xx], rcs.at[op, kind, xx], cp).start()
+            copy(own, crecv.at[op, kind, xx, n], s_cs + op, r_cs + 4 * op + 2 * kind + near, cp).start()
 
     def scatter_mid(op, kind):
         rows = kind_rows(kind)
         n = pl.ds(0, KINDS[kind][1])
-        got(crecv.at[op, kind, 1 - x, n], rcs.at[op, kind, 1 - x])
+        got(crecv.at[op, kind, 1 - x, n], r_cs + 4 * op + 2 * kind)
         far = part[op, 2 * (1 - x) + c, rows, :] + crecv[op, kind, 1 - x, n, :].astype(F32)
         xsend[op, kind, n, :] = far.astype(BF16)
-        copy(xsend.at[op, kind, n], xrecv.at[op, kind, n], sxs.at[op, kind], rxs.at[op, kind], xp).start()
+        copy(xsend.at[op, kind, n], xrecv.at[op, kind, n], s_xs + op, r_xs + 2 * op + kind, xp).start()
 
     def scatter_end(op, kind):
         rows = kind_rows(kind)
         n = pl.ds(0, KINDS[kind][1])
-        got(crecv.at[op, kind, x, n], rcs.at[op, kind, x])
+        got(crecv.at[op, kind, x, n], r_cs + 4 * op + 2 * kind + 1)
         near = part[op, 2 * x + c, rows, :] + crecv[op, kind, x, n, :].astype(F32)
-        got(xrecv.at[op, kind, n], rxs.at[op, kind])
+        got(xrecv.at[op, kind, n], r_xs + 2 * op + kind)
         return near + xrecv[op, kind, n, :].astype(F32)
 
     def gather_start(op, kind, buf, value):
         rows = kind_rows(kind)
         buf[r, rows, :] = value
         own = buf.at[r, rows]
-        copy(own, own, sag.at[op, kind, 0], rag.at[op, kind, r], xp).start()
-        copy(own, own, sag.at[op, kind, 1], rag.at[op, kind, r], cp).start()
+        copy(own, own, s_ag + op, r_ag + 4 * op + 2 * kind, xp).start()
+        copy(own, own, s_ag + op, r_ag + 4 * op + 2 * kind + 1, cp).start()
 
     def gather_mid(op, kind, buf):
-        rows = kind_rows(kind)
-        far = buf.at[xp[1], rows]
-        got(far, rag.at[op, kind, xp[1]])
-        copy(far, far, sag.at[op, kind, 2], rag.at[op, kind, xp[1]], cp).start()
+        far = buf.at[xp[1], kind_rows(kind)]
+        got(far, r_ag + 4 * op + 2 * kind)
+        copy(far, far, s_ag + op, r_ag + 4 * op + 2 * kind + 1, cp).start()
 
     def gather_end(op, kind, buf):
         rows = kind_rows(kind)
-        got(buf.at[cp[1], rows], rag.at[op, kind, cp[1]])
-        got(buf.at[xcp[1], rows], rag.at[op, kind, xcp[1]])
+        got(buf.at[pl.ds(0, 2), rows], r_ag + 4 * op + 2 * kind + 1)
         return jnp.concatenate([buf[s, rows, :] for s in range(4)], axis=1)
 
     weight_r = wr[...].reshape(512, 512)
-    for k in range(4):
-        local["xv", k].wait()
-    for dev in rest:
-        got(xv.at[:, dev[1]], rx.at[0, 0, dev[1]])
     scatter_start(0, 0, dot(xv[...].reshape(NV, 512), weight_r))
-    for k in range(4):
-        local["xc", k].wait()
-    for dev in rest:
-        got(xc4.at[dev[1]], rx.at[0, 1, dev[1]])
+    stored(xc4.at[r], l_x[1])
+    got(xc4.at[pl.ds(0, 3)], s_rx[0][1])
     xc[...] = xc4[...].reshape(4, 64, 512)
     scatter_start(0, 1, dot(xc[...].reshape(NC, 512), weight_r))
     scatter_mid(0, 0)
     scatter_mid(0, 1)
     spread_c(cot_crops, cc4, 1, rest[:1])
-    line_pass(1, parts_ws, 0)
-
-    for dev in peers[:7]:
-        got(pg.at[dev[0]], rpg.at[dev[0]])
+
+    got(pg.at[pl.ds(0, 7)], r_pg)
     half = lax.broadcasted_iota(jnp.int32, (1, 128), 1) < 64
     gain1, shift1, gain2, shift2 = [
         jnp.where(half, pg[2 * r, q : q + 1, :], pg[2 * r + 1, q : q + 1, :]) for q in range(4)
@@ -579,7 +582,9 @@
         sig = sigmoid(norm)
         return rstd, xhat, sig * (1.0 + norm * (1.0 - sig)), (norm * sig).astype(BF16)
 
-    rstd1, rstd2, rstd3 = [None, None], [None, None], [None, None]
+    line_pass(share_s, 0)
+    line_pass(share_s, 1)
+    rstd1, rstd2 = [None, None], [None, None]
     for kind in range(2):
         rows = KINDS[kind][1]
         rstd1[kind], xh, sl, act = norm_act(scatter_end(0, kind), rows, gain1, shift1)
@@ -588,15 +593,13 @@
         slope1[kind_rows(kind), :] = sl
     spread_v(cot_views, cv, 1, rest[1:])
     spread_c(cot_crops, cc4, 1, rest[1:])
-    line_pass(1, parts_ws, 1)
-    line_pass(1, parts_ws, 2)
-    for k in range(4):
-        local["we", k].wait()
-    line_send(2, whole_we)
+    line_pass(share_s, 2)
+    stored(we.at[i], l_we)
+    line_send(share_e)
     for kind in range(2):
         gather_mid(0, kind, act1)
-    for h in range(3):
-        line_got(1, parts_ws_other, h)
+    line_got(share_s)
+    line_pass(share_e, 0)
 
     def weight_s():
         return jnp.concatenate([ws[t].reshape(512, 128) for t in range(9)], axis=1)
@@ -614,18 +617,15 @@
         gather_start(1, kind, act2, act)
         xhat2[kind_rows(kind), :] = xh
         slope2[kind_rows(kind), :] = sl
-    line_pass(2, whole_we, 0)
     pool[...] = jnp.zeros_like(pool)
     for kind in range(2):
         gather_mid(1, kind, act2)
-    for k in range(4):
-        local["cv", k].wait()
-        local["cc", k].wait()
-    for dev in rest:
-        got(cv.at[:, dev[1]], rx.at[1, 0, dev[1]])
-        got(cc4.at[dev[1]], rx.at[1, 1, dev[1]])
+    stored(cv.at[:, r], l_cot[0])
+    stored(cc4.at[r], l_cot[1])
+    got(cv.at[:, pl.ds(0, 3)], s_rx[1][0])
+    got(cc4.at[pl.ds(0, 3)], s_rx[1][1])
     cc[...] = cc4[...].reshape(4, 64, 512)
-    line_got(2, whole_we_other, 0)
+    line_got(share_e)
     weight_e = we[...].reshape(512, 512)
 
     sum_x3, sum_d3 = [], []
@@ -679,101 +679,113 @@
 
         lax.fori_loop(0, rows // 32, back, 0)
 
+    s_out, r_out = ((new(), new()), (new(), new())), ((new(), new()), (new(), new()))
+    l_out = ((new(), new()), (new(), new()))
+
     def hand_v(src, dst, s, devs):
         for dev in devs:
-            dr = (dev[1] + 4 - r) % 4
             for k in range(4):
-                copy(src.at[:, dev[1], :, kl(k)], dst.at[:, :, lanes(k, x, c)], sout.at[s, 0, dr, k], rout.at[s, 0, r, k], dev).start()
+                copy(src.at[:, dev[1], :, kl(k)], dst.at[:, :, lanes(k, x, c)], s_out[s][0], r_out[s][0], dev).start()
 
     def hand_c(src, dst, s, devs):
         for dev in devs:
-            dr = (dev[1] + 4 - r) % 4
             for k in range(4):
-                copy(src.at[dev[1], :, kl(k)], dst.at[:, lanes(k, x, c)], sout.at[s, 1, dr, k], rout.at[s, 1, r, k], dev).start()
-
-    def hand_own(src_v, src_c, dst_v, dst_c, s, end=False):
+                copy(src.at[dev[1], :, kl(k)], dst.at[:, lanes(k, x, c)], s_out[s][1], r_out[s][1], dev).start()
+
+    def hand_own(src_v, src_c, dst_v, dst_c, s):
         for k in range(4):
-            for m, (src, dst) in enumerate(
-                ((src_v.at[:, r, :, kl(k)], dst_v.at[:, :, lanes(k, x, c)]), (src_c.at[r, :, kl(k)], dst_c.at[:, lanes(k, x, c)]))
-            ):
-                own = pltpu.make_async_copy(src, dst, sout.at[s, m, 0, k])
-                if end:
-                    own.wait()
-                else:
-                    own.start()
+            stage(src_v.at[:, r, :, kl(k)], dst_v.at[:, :, lanes(k, x, c)], l_out[s][0])
+            stage(src_c.at[r, :, kl(k)], dst_c.at[:, lanes(k, x, c)], l_out[s][1])
 
     def handed(src_v, src_c, dst_v, dst_c, s):
-        hand_own(src_v, src_c, dst_v, dst_c, s, True)
-        for dev in rest:
-            rr = dev[1]
-            dr = (rr + 4 - r) % 4
-            for k in range(4):
-                sent(src_v.at[:, rr, :, kl(k)], sout.at[s, 0, dr, k])
-                sent(src_c.at[rr, :, kl(k)], sout.at[s, 1, dr, k])
-                got(dst_v.at[:, :, lanes(k, rr // 2, rr % 2)], rout.at[s, 0, rr, k])
-                got(dst_c.at[:, lanes(k, rr // 2, rr % 2)], rout.at[s, 1, rr, k])
+        stored(src_v.at[:, 0], l_out[s][0])
+        stored(src_c.at[0], l_out[s][1])
+        sent(src_v.at[:, pl.ds(0, 3)], s_out[s][0])
+        sent(src_c.at[pl.ds(0, 3)], s_out[s][1])
+        got(dst_v.at[:, :, pl.ds(0, 1536)], r_out[s][0])
+        got(dst_c.at[:, pl.ds(0, 1536)], r_out[s][1])
 
     far_of = jnp.where(middle, z + 2 * step, z + 3 * step)
     mid_of = jnp.where(middle, z - step, z + 2 * step)
     order = [far_of, mid_of, z + step, z]
 
-    def grad_y(full, send, recv, q, both):
-        for k in order:
-            send[k] = (full[k, 1 - y] if both else full[k]).astype(BF16)
-            copy(send.at[k], recv.at[k], sgy.at[q, k], rgy.at[q, k], yp).start()
-
-    def grad_add(full, yrecv, q, k, both):
-        got(yrecv.at[k], rgy.at[q, k])
-        return (full[k, y] if both else full[k]) + yrecv[k].astype(F32)
-
-    def grad_z(full, yrecv, send, recv, relay, q, n, both=True):
-        k = order[n]
-        if n == 0:
-
+    class Grad:
+        def __init__(self, full, ysend, yrecv, zsend, zrecv, relay, acc, both=True):
+            self.full, self.ysend, self.yrecv, self.zsend, self.zrecv = full, ysend, yrecv, zsend, zrecv
+            self.relay, self.acc, self.both = relay, acc, both
+            self.s_y, self.r_y, self.s_z, self.r_z, self.r_relay = new(), new(4), new(), new(), new()
+
+        def start(self):
+            for k in order:
+                self.ysend[k] = (self.full[k, 1 - y] if self.both else self.full[k]).astype(BF16)
+                copy(self.ysend.at[k], self.yrecv.at[k], self.s_y, self.r_y + k, yp).start()
+
+        def add(self, k):
+            got(self.yrecv.at[k], self.r_y + k)
+            return (self.full[k, y] if self.both else self.full[k]) + self.yrecv[k].astype(F32)
+
+        def send(self, k, value):
+            self.zsend[k] = value.astype(BF16)
+            copy(self.zsend.at[k], self.zrecv.at[z], self.s_z, self.r_z, (2 * k + y, r)).start()
+
+        def along(self):
             @pl.when(jnp.logical_not(middle))
             def _():
-                send[k] = grad_add(full, yrecv, q, k, both).astype(BF16)
-                copy(send.at[k], relay, sgz.at[q, 0], rgz.at[q, 4], on_line(1)).start()
-
-        else:
-            send[k] = grad_add(full, yrecv, q, k, both).astype(BF16)
-            copy(send.at[k], recv.at[z], sgz.at[q, n], rgz.at[q, z], (2 * k + y, r)).start()
-
-    def grad_relay(full, yrecv, send, recv, relay, q, both=True):
-        @pl.when(middle)
-        def _():
-            k = order[0]
-            total = grad_add(full, yrecv, q, k, both)
-            got(relay, rgz.at[q, 4])
-            send[k] = (total + relay[...].astype(F32)).astype(BF16)
-            copy(send.at[k], recv.at[z], sgz.at[q, 0], rgz.at[q, z], (2 * k + y, r)).start()
-
-    def grad_sum(full, yrecv, recv, acc, q, both=True):
-        acc[...] = grad_add(full, yrecv, q, z, both)
-        for k in (z + step, z + 2 * step):
-            got(recv.at[k], rgz.at[q, k])
-            acc[...] += recv[k].astype(F32)
-
-        @pl.when(middle)
-        def _():
-            k = z - step
-            got(recv.at[k], rgz.at[q, k])
-            acc[...] += recv[k].astype(F32)
-
-        return acc[...]
-
-    def fin_start(buf, value, q):
-        buf[r] = value.astype(BF16)
-        copy(buf.at[r], buf.at[r], sfin.at[q, 0], rfin.at[q, r], xp).start()
-        copy(buf.at[r], buf.at[r], sfin.at[q, 1], rfin.at[q, r], cp).start()
-
-    def fin_mid(buf, q):
-        got(buf.at[xp[1]], rfin.at[q, xp[1]])
-        copy(buf.at[xp[1]], buf.at[xp[1]], sfin.at[q, 2], rfin.at[q, xp[1]], cp).start()
-
-    def fin_end(buf, q):
-        got(buf.at[cp[1]], rfin.at[q, cp[1]])
-        got(buf.at[xcp[1]], rfin.at[q, xcp[1]])
+                k = order[0]
+                self.zsend[k] = self.add(k).astype(BF16)
+                copy(self.zsend.at[k], self.relay, self.s_z, self.r_relay, on_line(1)).start()
+
+            self.send(order[1], self.add(order[1]))
+            self.send(order[2], self.add(order[2]))
+
+        def hand_on(self):
+            @pl.when(middle)
+            def _():
+                total = self.add(order[0])
+                got(self.relay, self.r_relay)
+                self.send(order[0], total + self.relay[...].astype(F32))
+
+        def total(self):
+            self.acc[...] = self.add(z)
+
+            @pl.when(middle)
+            def _():
+                got(self.zrecv.at[pl.ds(0, 3)], self.r_z)
+                self.acc[...] += self.zrecv[z - step].astype(F32)
+
+            @pl.when(jnp.logical_not(middle))
+            def _():
+                got(self.zrecv.at[pl.ds(0, 2)], self.r_z)
+
+            return self.acc[...] + self.zrecv[z + step].astype(F32) + self.zrecv[z + 2 * step].astype(F32)
+
+        def sent(self):
+            sent(self.zsend.at[pl.ds(0, 3)], self.s_z)
+
+    class Slices:
+        def __init__(self, buf):
+            self.buf, self.send, self.far, self.near = buf, new(), new(), new()
+
+        def start(self, value):
+            self.buf[r] = value.astype(BF16)
+            copy(self.buf.at[r], self.buf.at[r], self.send, self.far, xp).start()
+            copy(self.buf.at[r], self.buf.at[r], self.send, self.near, cp).start()
+
+        def mid(self):
+            far = self.buf.at[xp[1]]
+            got(far, self.far)
+            copy(far, far, self.send, self.near, cp).start()
+
+        def end(self):
+            got(self.buf.at[pl.ds(0, 2)], self.near)
+            sent(self.buf.at[pl.ds(0, 3)], self.send)
+
+    grad_e = Grad(ge, ysend_e, yrecv_e, zsend_e, zrecv_e, relay_e, acc_e)
+    grad_s = [
+        Grad(*(one.at[q] for one in (gs, ysend_s, yrecv_s, zsend_s, zrecv_s, relay_s, acc_s))) for q in range(3)
+    ]
+    grad_r = Grad(gr, ysend_r, yrecv_r, zsend_r, zrecv_r, relay_r, acc_r, False)
+    slices_p, slices_e, slices_s = Slices(fin_p), Slices(fin_e), [Slices(fin_s.at[q]) for q in range(3)]
 
     expand(0)
     scatter_start(1, 0, dot(dex[kind_rows(0), :], weight_e, NT))
@@ -781,7 +793,7 @@
     scatter_mid(1, 0)
     scatter_start(1, 1, dot(dex[kind_rows(1), :], weight_e, NT))
     ge[...] = dot(jnp.concatenate([act2[s] for s in range(4)], axis=1), dex[...], TN).reshape(4, 2, 64, 512)
-    grad_y(ge, ysend_e, yrecv_e, 0, True)
+    grad_e.start()
     scatter_mid(1, 1)
     hand_v(ov, out_views, 0, rest[:1])
     hand_own(ov, oc, out_views, out_crops, 0)
@@ -810,14 +822,13 @@
         if kind == 1:
             scatter_mid(2, 0)
     scatter_mid(2, 1)
-    gs[...] = dot(jnp.concatenate([act1[s] for s in range(4)], axis=1), pat[...], TN).reshape(4, 2, 64, 1152)
-    grad_y(gs, ysend_s, yrecv_s, 1, True)
-    for n in range(4):
-        if n < 3:
-            grad_z(ge, yrecv_e, zsend_e, zrecv_e, relay_e, 0, n)
-        else:
-            grad_relay(ge, yrecv_e, zsend_e, zrecv_e, relay_e, 0)
-    hand_v(ov, out_views, 0, rest[1:2])
+    hand_c(oc, out_crops, 0, rest[:1])
+    full1 = jnp.concatenate([act1[s] for s in range(4)], axis=1)
+    for q in range(3):
+        gs[q] = dot(full1, pat[:, 384 * q : 384 * q + 384], TN).reshape(4, 2, 64, 384)
+        grad_s[q].start()
+    grad_e.along()
+    grad_e.hand_on()
 
     sum_d1, sum_x1 = [], []
     for kind in range(2):
@@ -832,9 +843,11 @@
     gx3, gd3 = sum_x3[0] + sum_x3[1], sum_d3[0] + sum_d3[1]
     rows3 = [g[:, 128 * k : 128 * k + 128] for g in (gx3, gd3) for k in range(4)]
     pgr[i] = jnp.concatenate(rows12 + rows3 + [jnp.zeros((4, 128), F32)], axis=0)
-    for n, dev in enumerate(peers[:7]):
-        copy(pgr.at[i], pgr.at[i], spp.at[n], rpp.at[0, i], dev).start()
-    hand_c(oc, out_crops, 0, rest[:2])
+    s_pp, r_pp, s_ps, r_ps = new(), new(), new(), new()
+    for dev in peers[:7]:
+        copy(pgr.at[i], pgr.at[i], s_pp, r_pp, dev).start()
+    hand_v(ov, out_views, 0, rest[1:2])
+    hand_c(oc, out_crops, 0, rest[1:2])
 
     rows_pool[...] = jnp.zeros_like(rows_pool)
     for n in range(8):
@@ -843,16 +856,12 @@
         for m in range(2):
             row = 4 * (2 + 2 * (n % 2) + m) + n // 2
             rows_pool[row : row + 1, :] = jnp.sum(pool[8 + n, 4 * m : 4 * m + 4, :], axis=0, keepdims=True) / 16.0
-    own_pool[...] = rows_pool[...].astype(BF16)
-    for k in range(4):
-        pltpu.make_async_copy(own_pool.at[:, kl(k)], pooled.at[:, lanes(k, x, c)], spool.at[0, k]).start()
-        for n, dev in enumerate(rest):
-            copy(own_pool.at[:, kl(k)], pooled.at[:, lanes(k, x, c)], spool.at[1 + n, k], rpool.at[r, k], dev).start()
-
-    grad_z(gs, yrecv_s, zsend_s, zrecv_s, relay_s, 1, 0)
-    for kind in range(2):
-        gather_mid(2, kind, dred)
-    grad_z(gs, yrecv_s, zsend_s, zrecv_s, relay_s, 1, 1)
+    slices_p.start(rows_pool[...])
+    grad_s[0].along()
+    gather_mid(2, 0, dred)
+    grad_s[1].along()
+    gather_mid(2, 1, dred)
+    grad_s[0].hand_on()
     full_d = [gather_end(2, kind, dred) for kind in range(2)]
 
     for m in range(4):
@@ -861,98 +870,93 @@
 
     @pl.when(y != c)
     def _():
-        grad_y(gr, ysend_r, yrecv_r, 2, False)
-
-    grad_z(gs, yrecv_s, zsend_s, zrecv_s, relay_s, 1, 2)
-    grad_relay(gs, yrecv_s, zsend_s, zrecv_s, relay_s, 1)
-    fin_start(fin_e, grad_sum(ge, yrecv_e, zrecv_e, acc_e, 0), 0)
+        grad_r.start()
+
     gv[...] = (dpre[kind_rows(0), :] + dot(full_d[0], weight_r, NT)).astype(BF16).reshape(8, 4, 16, 512)
     hand_v(gv, grad_views, 1, rest)
     gc[...] = (dpre[kind_rows(1), :] + dot(full_d[1], weight_r, NT)).astype(BF16).reshape(4, 64, 512)
     hand_c(gc, grad_crops, 1, rest)
     hand_own(gv, gc, grad_views, grad_crops, 1)
+    grad_s[2].along()
+    grad_s[1].hand_on()
+    slices_e.start(grad_e.total())
+    slices_p.mid()
+    grad_s[2].hand_on()
+    slices_s[0].start(grad_s[0].total())
 
     @pl.when(y == c)
     def _():
-        for n in range(3):
-            grad_z(gr, yrecv_r, zsend_r, zrecv_r, relay_r, 2, n, False)
-        grad_relay(gr, yrecv_r, zsend_r, zrecv_r, relay_r, 2, False)
-
-    fin_start(fin_s, grad_sum(gs, yrecv_s, zrecv_s, acc_s, 1), 1)
-    fin_mid(fin_e, 0)
-
-    total = pgr[i]
-    for n in range(7):
-        ii = (i + 1 + n) % 8
-        got(pgr.at[ii], rpp.at[0, ii])
-        total = total + pgr[ii]
-    pgs[r] = total
-    for n, dev in enumerate(rest):
-        copy(pgs.at[r], pgs.at[r], spp.at[7 + n], rpp.at[1, r], dev).start()
+        grad_r.along()
+
+    slices_s[1].start(grad_s[1].total())
+    slices_e.mid()
 
     @pl.when(y == c)
     def _():
-        fin_r[x] = grad_sum(gr, yrecv_r, zrecv_r, acc_r, 2, False).astype(BF16)
-        for n, dev in enumerate(rest):
-            copy(fin_r.at[x], fin_r.at[x], sfin.at[2, n], rfin.at[2, x], dev).start()
-
-    fin_mid(fin_s, 1)
-    fin_end(fin_e, 0)
-    fin_end(fin_s, 1)
+        grad_r.hand_on()
+
+    slices_s[2].start(grad_s[2].total())
+    slices_s[0].mid()
+
+    got(pgr.at[pl.ds(0, 7)], r_pp)
+    total = pgr[0]
+    for n in range(1, 8):
+        total = total + pgr[n]
+    pgs[r] = total
     for dev in rest:
-        got(pgs.at[dev[1]], rpp.at[1, dev[1]])
+        copy(pgs.at[r], pgs.at[r], s_ps, r_ps, dev).start()
+    slices_s[1].mid()
+
+    s_fr, r_fr = new(), new()
+
+    @pl.when(y == c)
+    def _():
+        fin_r[x] = grad_r.total().astype(BF16)
+        copy(fin_r.at[x], fin_r.at[x], s_fr, r_fr, xp).start()
+        copy(fin_r.at[x], fin_r.at[x], s_fr, r_fr, cp).start()
+
+    slices_s[2].mid()
+
+    @pl.when(y == c)
+    def _():
+        far = fin_r.at[1 - x]
+        got(far, r_fr)
+        copy(far, far, s_fr, r_fr, cp).start()
+
+    for one in (slices_p, slices_e, *slices_s):
+        one.end()
+    got(pgs.at[pl.ds(0, 3)], r_ps)
     handed(ov, oc, out_views, out_crops, 0)
     handed(gv, gc, grad_views, grad_crops, 1)
-    for k in range(4):
-        pltpu.make_async_copy(own_pool.at[:, kl(k)], pooled.at[:, lanes(k, x, c)], spool.at[0, k]).wait()
-        for n, dev in enumerate(rest):
-            sent(own_pool.at[:, kl(k)], spool.at[1 + n, k])
-            got(pooled.at[:, lanes(k, dev[1] // 2, dev[1] % 2)], rpool.at[dev[1], k])
-    got(fin_r.at[1 - x], rfin.at[2, 1 - x])
+    for s, (own_v, own_c) in enumerate(((xv, xc4), (cv, cc4))):
+        sent(own_v.at[:, pl.ds(0, 3)], s_sx[s][0])
+        sent(own_c.at[pl.ds(0, 3)], s_sx[s][1])
+    sent(pg.at[pl.ds(0, 7)], s_pg)
+    sent(pgr.at[pl.ds(0, 7)], s_pp)
+    sent(pgs.at[pl.ds(0, 3)], s_ps)
+    line_sent(share_s.send, ws, ws.at[:, pl.ds(0, 6)])
+    line_sent(share_e.send, we, we.at[pl.ds(0, 6)])
+    for op in range(3):
+        sent(act1.at[pl.ds(0, 2)], s_cs + op)
+        sent(act1.at[0], s_xs + op)
+        sent(act1.at[pl.ds(0, 3)], s_ag + op)
+    for one in (grad_e, *grad_s):
+        sent(one.ysend, one.s_y)
+        one.sent()
 
     @pl.when(y != c)
     def _():
-        got(fin_r.at[x], rfin.at[2, x])
-
-    for s, (src_v, src_c) in enumerate(((views, crops), (cot_views, cot_crops))):
-        for dr in (1, 2, 3):
-            for k in range(4):
-                sent(src_v.at[:, :, kl(k)], sx.at[s, 0, dr, k])
-                sent(src_c.at[:, :, kl(k)], sx.at[s, 1, dr, k])
-    for n in range(7):
-        sent(pg.at[i], spg.at[n])
-    for n in range(10):
-        sent(pgs.at[r], spp.at[n])
-    line_sent(1, parts_ws)
-    line_sent(2, whole_we)
-    for kind in range(2):
-        n = pl.ds(0, KINDS[kind][1])
-        for op in range(3):
-            for xx in range(2):
-                sent(csend.at[op, kind, xx, n], scs.at[op, kind, xx])
-            sent(xsend.at[op, kind, n], sxs.at[op, kind])
-            for m in range(3):
-                sent(act1.at[r, kind_rows(kind)], sag.at[op, kind, m])
-    for q, (ys, zs, fin) in enumerate(((ysend_e, zsend_e, fin_e), (ysend_s, zsend_s, fin_s))):
-        for k in range(4):
-            sent(ys.at[k], sgy.at[q, k])
-        for n in range(3):
-            sent(zs.at[z], sgz.at[q, n])
-        for n in range(3):
-            sent(fin.at[r], sfin.at[q, n])
-
-    @pl.when(y != c)
-    def _():
-        for k in range(4):
-            sent(ysend_r.at[k], sgy.at[2, k])
+        sent(ysend_r, grad_r.s_y)
+        got(fin_r, r_fr)
 
     @pl.when(y == c)
     def _():
-        line_sent(0, whole_wr)
-        for n in range(3):
-            sent(zsend_r.at[z], sgz.at[2, n])
-        for n in range(3):
-            sent(fin_r.at[x], sfin.at[2, n])
+        line_sent(share_r.send, wr, wr.at[pl.ds(0, 3)])
+        line_sent(passed_r, wr, wr.at[pl.ds(0, 3)])
+        grad_r.sent()
+        sent(wr.at[pl.ds(0, 3)], s_fr)
+
+    assert taken[0] == SEMAPHORES, taken
 
 
 def store_kernel(
@@ -974,7 +978,7 @@
     store(grad_v, grad_views)
     for s in range(4):
         for t in range(9):
-            gs[t, :, 128 * s : 128 * s + 128] = fin_s[s, :, 128 * t : 128 * t + 128].astype(F32)
+            gs[t, :, 128 * s : 128 * s + 128] = fin_s[t // 3, s, :, 128 * (t % 3) : 128 * (t % 3) + 128].astype(F32)
     store(gs, grad_spatial)
     for s in range(4):
         for k in range(4):
@@ -987,7 +991,10 @@
     store(oc, out_crops)
     gc[...] = grad_c[...].reshape(16, 4, 2048)
     store(gc, grad_crops)
-    pl_[...] = pool[0:24, :].astype(F32).reshape(6, 4, 2048)
+    for s in range(4):
+        for k in range(4):
+            lo = 512 * k + 256 * (s % 2) + 128 * (s // 2)
+            pl_[:, :, lo : lo + 128] = pool[s, 0:24, 128 * k : 128 * k + 128].astype(F32).reshape(6, 4, 128)
     store(pl_, pooled)
     for n, out in enumerate((gain_a, shift_a, gain_b, shift_b)):
         row = sums[i // 2, n : n + 1, :]
@@ -1013,8 +1020,8 @@
     held = pl.pallas_call(
         block_kernel,
         out_shape=[
-            buf((8, 16, 2048)), buf((64, 2048)), buf((32, 2048)), buf((8, 16, 2048)), buf((64, 2048)),
-            buf((4, 64, 512)), buf((4, 64, 1152)), buf((2, 128, 512)), buf((4, 16, 128), F32),
+            buf((8, 16, 2048)), buf((64, 2048)), buf((4, 32, 512)), buf((8, 16, 2048)), buf((64, 2048)),
+            buf((4, 64, 512)), buf((3, 4, 64, 384)), buf((2, 128, 512)), buf((4, 16, 128), F32),
         ],
         in_specs=[hbm] * 13,
         out_specs=[vmem] * 9,
@@ -1028,17 +1035,14 @@
             buf((N, 128), F32), buf((N, 128), F32), buf((N, 128), F32), buf((N, 128), F32),
             buf((N, 512), F32), buf((N, 512), F32), buf((N, 512)), buf((N, 1152)),
             buf((8, 4, 16, 512)), buf((4, 64, 512)), buf((8, 4, 16, 512)), buf((4, 64, 512)),
-            buf((16, 8, 512), F32), buf((32, 512), F32), buf((32, 512)),
-            buf((4, 2, 64, 512), F32), buf((4, 2, 64, 1152), F32), buf((4, 128, 512), F32),
+            buf((16, 8, 512), F32), buf((32, 512), F32),
+            buf((4, 2, 64, 512), F32), buf((3, 4, 2, 64, 384), F32), buf((4, 128, 512), F32),
             buf((4, 64, 512)), buf((4, 64, 512)), buf((4, 64, 512)), buf((4, 64, 512)),
-            buf((4, 64, 1152)), buf((4, 64, 1152)), buf((4, 64, 1152)), buf((4, 64, 1152)),
+            buf((3, 4, 64, 384)), buf((3, 4, 64, 384)), buf((3, 4, 64, 384)), buf((3, 4, 64, 384)),
             buf((4, 128, 512)), buf((4, 128, 512)), buf((4, 128, 512)), buf((4, 128, 512)),
-            buf((64, 512)), buf((64, 1152)), buf((128, 512)), buf((64, 512), F32), buf((64, 1152), F32), buf((128, 512), F32),
+            buf((64, 512)), buf((3, 64, 384)), buf((128, 512)), buf((64, 512), F32), buf((3, 64, 384), F32), buf((128, 512), F32),
             buf((8, 16, 128), F32),
-            dma(32), dma(2, 2, 4, 4), dma(2, 2, 4), dma(3, 3, 8), dma(3, 3, 2, 4), dma(7), dma(8),
-            dma(3, 2, 2), dma(3, 2, 2), dma(3, 2), dma(3, 2), dma(3, 2, 3), dma(3, 2, 4),
-            dma(2, 2, 4, 4), dma(2, 2, 4, 4), dma(3, 4), dma(3, 4), dma(3, 4), dma(3, 5), dma(3, 3), dma(3, 4),
-            dma(10), dma(2, 8), dma(4, 4), dma(4, 4),
+            dma(SEMAPHORES),
         ],
         compiler_params=pltpu.CompilerParams(collective_id=0, has_side_effects=True, vmem_limit_bytes=58 << 20),
         cost_estimate=pl.CostEstimate(flops=5_200_000_000, bytes_accessed=8_000_000, transcendentals=2_000_000),

time: 99.7 us -> 96.7 us (0.970)
  Pallas kernels: 98.1 us -> 95.9 us
    pallas_call x1, Pallas kernels: 95.5 us -> 93.3 us  [fused(): pl.pallas_call(block_kernel, out_shape=[buf((8, 16, 2048)), buf((64, 2048...]
where the time goes in v3:
time: 96.7 us; the launch traced here: 96.5 us
  Pallas kernels  95.9 us (99%)
    pallas_call x1, Pallas kernels, fused(): pl.pallas_call(block_kernel, out_shape=[buf((8, 16, 2048)), buf((64, 2048...  93.3 us
    pallas_call x1, Pallas kernels, fused(): pl.pallas_call(store_kernel, out_shape=[shape((8, 16, 2048), BF16), shape...  2.59 us

profile of v3, /device:TPU:0, one launch (start us, length us, event | category | flops | bytes accessed | tf_op | source)
XLA Modules:
  0.0 96.5 jit_solution(5832559432650842678)
XLA Ops:
  0.7 93.3 %shard_map.236 = (bf16[8,16,2048]{2,1,0:T(8,128)(2,1)S(1)}, bf16[64,2048]{1,0:T(8,128)(2,1)S(1)}, bf16[4,32,512]{2,1,0:T(8,128)(2,1)S(1)}, bf16[8,16,2048]{2,1,0...) custom-call(bf16[8,16,2048]{2,1,0:T(8,128)(2,1)} %bitcast.17, ...), custom_call_target="tpu_custom_call" | custom-call | flops 5200000000 | bytes 8000000 | tf_op jit(solution)/shard_map/pallas_call | solution.py:1020
  93.9 2.6 %shard_map.237 = (bf16[8,16,2048]{2,1,0:T(8,128)(2,1)}, bf16[16,4,2048]{2,1,0:T(4,128)(2,1)}, f32[6,4,2048]{2,1,0:T(4,128)}, bf16[8,16,2048]{2,1,0:T(8,128)(2,1)...) custom-call(bf16[8,16,2048]{2,1,0:T(8,128)(2,1)S(1)} %get-tuple-elem, ...), custom_call_target="tpu_custom_call" | custom-call | tf_op jit(solution)/shard_map/pallas_call | solution.py:1051

commit v4 on v3

--- a/solution.py
+++ b/solution.py
@@ -268,7 +268,7 @@
 
 
 MESH = pl.DeviceIdType.MESH
-SEMAPHORES = 159
+SEMAPHORES = 164
 F32 = jnp.float32
 BF16 = jnp.bfloat16
 NV = 512
@@ -313,9 +313,9 @@
 def block_kernel(
     views, crops, w_reduce, w_spatial, w_expand, cot_views, cot_crops, gain_a, shift_a, gain_b, shift_b, gain_c, shift_c,
     out_views, out_crops, fin_p, grad_views, grad_crops, fin_e, fin_s, fin_r, pgs,
-    xv, xc4, xc, cv, cc4, cc, wr, ws, we, raw_a, raw_b, raw_c, raw_d, raw_e, raw_f, pg,
+    xv, xc4, xc, cv, cc4, cc, xo_v, xo_c, co_v, co_c, wr, ws, we, aff, raw_a, raw_b, raw_c, raw_d, raw_e, raw_f, pg,
     part, csend, crecv, xsend, xrecv,
-    act1, act2, dred, conv, xhat1, slope1, xhat2, slope2, ex, dpre, dex, pat, ov, oc, gv, gc, pool, rows_pool,
+    act1, act2, dred, conv, xhat1, slope1, xhat2, slope2, ex, dpre, dex, pat, dpo, pool, rows_pool,
     ge, gs, gr, ysend_e, yrecv_e, zsend_e, zrecv_e, ysend_s, yrecv_s, zsend_s, zrecv_s, ysend_r, yrecv_r, zsend_r, zrecv_r,
     relay_e, relay_s, relay_r, acc_e, acc_s, acc_r, pgr,
     sem,
@@ -367,12 +367,12 @@
     def stage(src, dst, one):
         pltpu.make_async_copy(src, dst, sem.at[one]).start()
 
-    l_wr, l_ws, l_we, l_gain = new(), new(), new(), new(6)
-    l_x, l_cot = (new(), new()), (new(), new())
+    l_wr, l_ws, l_we, l_we2, l_gain = new(), new(), new(), new(), new(6)
+    l_x, l_cot, l_own = (new(), new()), (new(), new()), new(4)
 
     @pl.when(y == c)
     def _():
-        stage(w_reduce.at[pl.ds(pl.multiple_of(128 * x, 128), 128)], wr.at[z], l_wr)
+        stage(w_reduce.at[pl.ds(pl.multiple_of(128 * x, 128), 128)], wr.at[r, z], l_wr)
 
     stage(w_spatial.at[:, :, pl.ds(pl.multiple_of(128 * r, 128), 128)], ws.at[:, i], l_ws)
     raw = (raw_a, raw_b, raw_c, raw_d, raw_e, raw_f)
@@ -382,10 +382,13 @@
         stage(views.at[:, :, lanes(k, x, c)], xv.at[:, r, :, kl(k)], l_x[0])
         stage(crops.at[:, :, lanes(k, x, c)], xc4.at[r, :, :, kl(k)], l_x[1])
     for k in range(4):
-        stage(w_expand.at[:, lanes(k, x, c)], we.at[i, :, kl(k)], l_we)
+        stage(w_expand.at[:, lanes(k, x, c)], we.at[r, i, :, kl(k)], l_we)
+        stage(w_expand.at[:, lanes(k, 1 - x, c)], we.at[xp[1], i, :, kl(k)], l_we2)
     for k in range(4):
         stage(cot_views.at[:, :, lanes(k, x, c)], cv.at[:, r, :, kl(k)], l_cot[0])
         stage(cot_crops.at[:, :, lanes(k, x, c)], cc4.at[r, :, :, kl(k)], l_cot[1])
+    for n, (src, dst) in enumerate(((views, xo_v), (crops, xo_c), (cot_views, co_v), (cot_crops, co_c))):
+        stage(src, dst, l_own + n)
 
     bar = pltpu.get_barrier_semaphore()
     peers = [((i + n) % 8, r) for n in range(1, 8)] + [cp, xp, xcp]
@@ -401,12 +404,13 @@
             self.along_z = [new(3) for _ in range(count)]
             self.along_y = [new() for _ in range(count)]
 
-    share_r = Share(lambda k: (wr.at[k],), None)
+    share_r = Share(lambda k: (wr.at[r, k],), None)
     share_s = Share(
         lambda k: tuple(ws.at[pl.ds(3 * h, 3), 2 * k + y] for h in range(3)),
         lambda h: ws.at[pl.ds(3 * h, 3), pl.ds(0, 4)],
     )
-    share_e = Share(lambda k: (we.at[2 * k + y],), lambda h: we.at[pl.ds(0, 4)])
+    share_e = Share(lambda k: (we.at[r, 2 * k + y],), lambda h: we.at[0, pl.ds(0, 4)])
+    share_o = Share(lambda k: (we.at[xp[1], 2 * k + y],), lambda h: we.at[0, pl.ds(0, 4)])
     passed_r = new()
 
     inner = ((z + 1) // 2) * (2 - (z + 1) // 2)
@@ -463,7 +467,7 @@
 
     @pl.when(y == c)
     def _():
-        stored(wr.at[z], l_wr)
+        stored(wr.at[r, z], l_wr)
         line_send(share_r)
 
     s_sx, s_rx = ((new(), new()), (new(), new())), ((new(), new()), (new(), new()))
@@ -506,7 +510,7 @@
 
     @pl.when(y != c)
     def _():
-        got(wr, share_r.along_y[0])
+        got(wr.at[r], share_r.along_y[0])
 
     s_cs, r_cs = new(3), new(12)
     s_xs, r_xs = new(3), new(6)
@@ -555,7 +559,7 @@
         got(buf.at[pl.ds(0, 2), rows], r_ag + 4 * op + 2 * kind + 1)
         return jnp.concatenate([buf[s, rows, :] for s in range(4)], axis=1)
 
-    weight_r = wr[...].reshape(512, 512)
+    weight_r = wr[r].reshape(512, 512)
     scatter_start(0, 0, dot(xv[...].reshape(NV, 512), weight_r))
     stored(xc4.at[r], l_x[1])
     got(xc4.at[pl.ds(0, 3)], s_rx[0][1])
@@ -594,12 +598,21 @@
     spread_v(cot_views, cv, 1, rest[1:])
     spread_c(cot_crops, cc4, 1, rest[1:])
     line_pass(share_s, 2)
-    stored(we.at[i], l_we)
+    stored(we.at[r, i], l_we)
     line_send(share_e)
     for kind in range(2):
         gather_mid(0, kind, act1)
+
+    s_ow, s_xw, r_xw, r_ow = new(), new(), new(), new(2)
+
+    def over_x(k):
+        copy(wr.at[r, k], wr.at[r, k], s_xw, r_xw, xp).start()
+
+    def between(ref, n):
+        copy(ref, ref, s_ow, r_ow + n, cp).start()
+
+    between(wr.at[r], 0)
     line_got(share_s)
-    line_pass(share_e, 0)
 
     def weight_s():
         return jnp.concatenate([ws[t].reshape(512, 128) for t in range(9)], axis=1)
@@ -617,6 +630,12 @@
         gather_start(1, kind, act2, act)
         xhat2[kind_rows(kind), :] = xh
         slope2[kind_rows(kind), :] = sl
+        if kind == 0:
+            line_pass(share_e, 0)
+            stored(we.at[r, i], l_we2)
+            line_send(share_o)
+    over_x(0)
+    over_x(1)
     pool[...] = jnp.zeros_like(pool)
     for kind in range(2):
         gather_mid(1, kind, act2)
@@ -626,7 +645,8 @@
     got(cc4.at[pl.ds(0, 3)], s_rx[1][1])
     cc[...] = cc4[...].reshape(4, 64, 512)
     line_got(share_e)
-    weight_e = we[...].reshape(512, 512)
+    between(we.at[r], 1)
+    weight_e = we[r].reshape(512, 512)
 
     sum_x3, sum_d3 = [], []
     zero8 = jnp.zeros((8, 512), F32)
@@ -656,10 +676,8 @@
             d = cot.astype(F32) * (sig * (1.0 + pre * (1.0 - sig)))
             dpre[rs, :] = d
             if kind == 0:
-                ov[b // 4, b % 4] = activation.astype(BF16)
                 pool[b // 4] += activation[:8] + activation[8:]
             else:
-                oc[b // 4, qs, :] = activation.astype(BF16)
                 pool[8 + 2 * (b % 4)] += activation[:8]
                 pool[9 + 2 * (b % 4)] += activation[8:]
             dx = d * xhat
@@ -671,6 +689,8 @@
         sum_x3.append(sxx)
         scale = gain3 * rstd
         mean_d, mean_x = sd / rows, sxx / rows
+        aff[r, 2 * kind : 2 * kind + 1, :] = scale
+        aff[r, 2 * kind + 1 : 2 * kind + 2, :] = shift3 - scale * mean
 
         def back(b, _):
             rs = pl.ds(pl.multiple_of(start + 32 * b, 32), 32)
@@ -679,31 +699,42 @@
 
         lax.fori_loop(0, rows // 32, back, 0)
 
-    s_out, r_out = ((new(), new()), (new(), new())), ((new(), new()), (new(), new()))
-    l_out = ((new(), new()), (new(), new()))
-
-    def hand_v(src, dst, s, devs):
-        for dev in devs:
-            for k in range(4):
-                copy(src.at[:, dev[1], :, kl(k)], dst.at[:, :, lanes(k, x, c)], s_out[s][0], r_out[s][0], dev).start()
-
-    def hand_c(src, dst, s, devs):
-        for dev in devs:
-            for k in range(4):
-                copy(src.at[dev[1], :, kl(k)], dst.at[:, lanes(k, x, c)], s_out[s][1], r_out[s][1], dev).start()
-
-    def hand_own(src_v, src_c, dst_v, dst_c, s):
+    def own_rows(buf):
+        slices = []
+        for s in range(4):
+            rows = [buf[s, pl.ds(pl.multiple_of(64 * m + 16 * r, 16), 16), :] for m in range(8)]
+            rows.append(buf[s, pl.ds(pl.multiple_of(NV + 64 * r, 64), 64), :])
+            slices.append(jnp.concatenate(rows, axis=0))
+        return jnp.concatenate(slices, axis=1)
+
+    def own_blocks(values, s):
         for k in range(4):
-            stage(src_v.at[:, r, :, kl(k)], dst_v.at[:, :, lanes(k, x, c)], l_out[s][0])
-            stage(src_c.at[r, :, kl(k)], dst_c.at[:, lanes(k, x, c)], l_out[s][1])
-
-    def handed(src_v, src_c, dst_v, dst_c, s):
-        stored(src_v.at[:, 0], l_out[s][0])
-        stored(src_c.at[0], l_out[s][1])
-        sent(src_v.at[:, pl.ds(0, 3)], s_out[s][0])
-        sent(src_c.at[pl.ds(0, 3)], s_out[s][1])
-        got(dst_v.at[:, :, pl.ds(0, 1536)], r_out[s][0])
-        got(dst_c.at[:, pl.ds(0, 1536)], r_out[s][1])
+            lo = 512 * k + 256 * (s % 2) + 128 * (s // 2)
+            yield k, slice(lo, lo + 128), (values[:128, 128 * k : 128 * k + 128], values[128:, 128 * k : 128 * k + 128])
+
+    def own_output():
+        act = own_rows(act2)
+        for s in range(4):
+            for k, cols, blocks in own_blocks(dot(act, we[s].reshape(512, 512)), s):
+                for kind, block in enumerate(blocks):
+                    scale = aff[s, 2 * kind : 2 * kind + 1, 128 * k : 128 * k + 128]
+                    shift = aff[s, 2 * kind + 1 : 2 * kind + 2, 128 * k : 128 * k + 128]
+                    src = (xo_v if kind == 0 else xo_c)[:, :, cols].reshape(block.shape).astype(F32)
+                    cot = (co_v if kind == 0 else co_c)[:, :, cols].reshape(block.shape).astype(F32)
+                    pre = src + (scale * block + shift)
+                    sig = sigmoid(pre)
+                    if kind == 0:
+                        out_views[:, :, cols] = (pre * sig).astype(BF16).reshape(8, 16, 128)
+                    else:
+                        out_crops[:, cols] = (pre * sig).astype(BF16)
+                    dpo[128 * kind : 128 * kind + block.shape[0], cols] = cot * (sig * (1.0 + pre * (1.0 - sig)))
+
+    def own_gradient():
+        back = own_rows(dred)
+        for s in range(4):
+            for _, cols, blocks in own_blocks(dot(back, wr[s].reshape(512, 512), NT), s):
+                grad_views[:, :, cols] = (dpo[:128, cols] + blocks[0]).astype(BF16).reshape(8, 16, 128)
+                grad_crops[:, cols] = (dpo[128:, cols] + blocks[1]).astype(BF16)
 
     far_of = jnp.where(middle, z + 2 * step, z + 3 * step)
     mid_of = jnp.where(middle, z - step, z + 2 * step)
@@ -789,16 +820,17 @@
 
     expand(0)
     scatter_start(1, 0, dot(dex[kind_rows(0), :], weight_e, NT))
+    line_pass(share_o, 0)
     expand(1)
     scatter_mid(1, 0)
     scatter_start(1, 1, dot(dex[kind_rows(1), :], weight_e, NT))
     ge[...] = dot(jnp.concatenate([act2[s] for s in range(4)], axis=1), dex[...], TN).reshape(4, 2, 64, 512)
     grad_e.start()
     scatter_mid(1, 1)
-    hand_v(ov, out_views, 0, rest[:1])
-    hand_own(ov, oc, out_views, out_crops, 0)
-    hand_v(ov, out_views, 0, rest[2:])
-    hand_c(oc, out_crops, 0, rest[2:])
+    s_af, r_af = new(), new()
+    for dev in rest:
+        copy(aff.at[r], aff.at[r], s_af, r_af, dev).start()
+    over_x(2)
 
     def norm_back(d, xhat, rstd, gain, rows):
         sd = jnp.sum(d, axis=0, keepdims=True)
@@ -822,13 +854,13 @@
         if kind == 1:
             scatter_mid(2, 0)
     scatter_mid(2, 1)
-    hand_c(oc, out_crops, 0, rest[:1])
     full1 = jnp.concatenate([act1[s] for s in range(4)], axis=1)
     for q in range(3):
         gs[q] = dot(full1, pat[:, 384 * q : 384 * q + 384], TN).reshape(4, 2, 64, 384)
         grad_s[q].start()
     grad_e.along()
-    grad_e.hand_on()
+    line_got(share_o)
+    between(we.at[xp[1]], 1)
 
     sum_d1, sum_x1 = [], []
     for kind in range(2):
@@ -846,8 +878,8 @@
     s_pp, r_pp, s_ps, r_ps = new(), new(), new(), new()
     for dev in peers[:7]:
         copy(pgr.at[i], pgr.at[i], s_pp, r_pp, dev).start()
-    hand_v(ov, out_views, 0, rest[1:2])
-    hand_c(oc, out_crops, 0, rest[1:2])
+    over_x(3)
+    grad_e.hand_on()
 
     rows_pool[...] = jnp.zeros_like(rows_pool)
     for n in range(8):
@@ -872,31 +904,35 @@
     def _():
         grad_r.start()
 
-    gv[...] = (dpre[kind_rows(0), :] + dot(full_d[0], weight_r, NT)).astype(BF16).reshape(8, 4, 16, 512)
-    hand_v(gv, grad_views, 1, rest)
-    gc[...] = (dpre[kind_rows(1), :] + dot(full_d[1], weight_r, NT)).astype(BF16).reshape(4, 64, 512)
-    hand_c(gc, grad_crops, 1, rest)
-    hand_own(gv, gc, grad_views, grad_crops, 1)
+    got(wr.at[0], r_xw)
+    between(wr.at[xp[1]], 0)
+    for n, ref in enumerate((xo_v, xo_c, co_v, co_c)):
+        stored(ref, l_own + n)
+    got(aff.at[pl.ds(0, 3)], r_af)
+    got(we.at[pl.ds(0, 2)], r_ow + 1)
+    own_output()
+    grad_s[1].hand_on()
     grad_s[2].along()
-    grad_s[1].hand_on()
     slices_e.start(grad_e.total())
-    slices_p.mid()
-    grad_s[2].hand_on()
     slices_s[0].start(grad_s[0].total())
+    got(wr.at[pl.ds(0, 2)], r_ow)
+    own_gradient()
 
     @pl.when(y == c)
     def _():
         grad_r.along()
 
+    grad_s[2].hand_on()
     slices_s[1].start(grad_s[1].total())
+    slices_p.mid()
     slices_e.mid()
 
     @pl.when(y == c)
     def _():
         grad_r.hand_on()
 
+    slices_s[0].mid()
     slices_s[2].start(grad_s[2].total())
-    slices_s[0].mid()
 
     got(pgr.at[pl.ds(0, 7)], r_pp)
     total = pgr[0]
@@ -926,8 +962,9 @@
     for one in (slices_p, slices_e, *slices_s):
         one.end()
     got(pgs.at[pl.ds(0, 3)], r_ps)
-    handed(ov, oc, out_views, out_crops, 0)
-    handed(gv, gc, grad_views, grad_crops, 1)
+    sent(aff.at[pl.ds(0, 3)], s_af)
+    sent(we, s_ow)
+    sent(wr.at[0], s_xw)
     for s, (own_v, own_c) in enumerate(((xv, xc4), (cv, cc4))):
         sent(own_v.at[:, pl.ds(0, 3)], s_sx[s][0])
         sent(own_c.at[pl.ds(0, 3)], s_sx[s][1])
@@ -935,7 +972,8 @@
     sent(pgr.at[pl.ds(0, 7)], s_pp)
     sent(pgs.at[pl.ds(0, 3)], s_ps)
     line_sent(share_s.send, ws, ws.at[:, pl.ds(0, 6)])
-    line_sent(share_e.send, we, we.at[pl.ds(0, 6)])
+    line_sent(share_e.send, we.at[0], we.at[0, pl.ds(0, 6)])
+    line_sent(share_o.send, we.at[0], we.at[0, pl.ds(0, 6)])
     for op in range(3):
         sent(act1.at[pl.ds(0, 2)], s_cs + op)
         sent(act1.at[0], s_xs + op)
@@ -951,10 +989,10 @@
 
     @pl.when(y == c)
     def _():
-        line_sent(share_r.send, wr, wr.at[pl.ds(0, 3)])
-        line_sent(passed_r, wr, wr.at[pl.ds(0, 3)])
+        line_sent(share_r.send, wr.at[0], wr.at[0, pl.ds(0, 3)])
+        line_sent(passed_r, wr.at[0], wr.at[0, pl.ds(0, 3)])
         grad_r.sent()
-        sent(wr.at[pl.ds(0, 3)], s_fr)
+        sent(wr.at[0, pl.ds(0, 3)], s_fr)
 
     assert taken[0] == SEMAPHORES, taken
 
@@ -1028,14 +1066,14 @@
         scratch_shapes=[
             buf((8, 4, 16, 512)), buf((4, 16, 4, 512)), buf((4, 64, 512)),
             buf((8, 4, 16, 512)), buf((4, 16, 4, 512)), buf((4, 64, 512)),
-            buf((4, 128, 512)), buf((9, 8, 64, 128)), buf((8, 64, 512)), buf((64,)), buf((64,)), buf((64,)), buf((64,)), buf((256,)), buf((256,)), buf((8, 8, 128), F32),
+            buf((8, 16, 2048)), buf((16, 4, 2048)), buf((8, 16, 2048)), buf((16, 4, 2048)),
+            buf((4, 4, 128, 512)), buf((9, 8, 64, 128)), buf((4, 8, 64, 512)), buf((4, 8, 512), F32), buf((64,)), buf((64,)), buf((64,)), buf((64,)), buf((256,)), buf((256,)), buf((8, 8, 128), F32),
             buf((3, 4, N, 128), F32), buf((3, 2, 2, NV, 128)), buf((3, 2, 2, NV, 128)),
             buf((3, 2, NV, 128)), buf((3, 2, NV, 128)),
             buf((4, N, 128)), buf((4, N, 128)), buf((4, N, 128)), buf((N, 1152), F32),
             buf((N, 128), F32), buf((N, 128), F32), buf((N, 128), F32), buf((N, 128), F32),
             buf((N, 512), F32), buf((N, 512), F32), buf((N, 512)), buf((N, 1152)),
-            buf((8, 4, 16, 512)), buf((4, 64, 512)), buf((8, 4, 16, 512)), buf((4, 64, 512)),
-            buf((16, 8, 512), F32), buf((32, 512), F32),
+            buf((192, 2048), F32), buf((16, 8, 512), F32), buf((32, 512), F32),
             buf((4, 2, 64, 512), F32), buf((3, 4, 2, 64, 384), F32), buf((4, 128, 512), F32),
             buf((4, 64, 512)), buf((4, 64, 512)), buf((4, 64, 512)), buf((4, 64, 512)),
             buf((3, 4, 64, 384)), buf((3, 4, 64, 384)), buf((3, 4, 64, 384)), buf((3, 4, 64, 384)),

time: 96.7 us -> 92.9 us (0.961)
  Pallas kernels: 95.9 us -> 92.1 us
    pallas_call x1, Pallas kernels: 93.3 us -> 89.5 us  [fused(): pl.pallas_call(block_kernel, out_shape=[buf((8, 16, 2048)), buf((64, 2048...]
where the time goes in v4:
time: 92.9 us; the launch traced here: 92.8 us
  Pallas kernels  92.1 us (99%)
    pallas_call x1, Pallas kernels, fused(): pl.pallas_call(block_kernel, out_shape=[buf((8, 16, 2048)), buf((64, 2048...  89.5 us
    pallas_call x1, Pallas kernels, fused(): pl.pallas_call(store_kernel, out_shape=[shape((8, 16, 2048), BF16), shape...  2.59 us

profile of v4, /device:TPU:0, one launch (start us, length us, event | category | flops | bytes accessed | tf_op | source)
XLA Modules:
  0.0 92.8 jit_solution(10126448280006988732)
XLA Ops:
  0.7 89.5 %shard_map.236 = (bf16[8,16,2048]{2,1,0:T(8,128)(2,1)S(1)}, bf16[64,2048]{1,0:T(8,128)(2,1)S(1)}, bf16[4,32,512]{2,1,0:T(8,128)(2,1)S(1)}, bf16[8,16,2048]{2,1,0...) custom-call(bf16[8,16,2048]{2,1,0:T(8,128)(2,1)} %bitcast.17, ...), custom_call_target="tpu_custom_call" | custom-call | flops 5200000000 | bytes 8000000 | tf_op jit(solution)/shard_map/pallas_call | solution.py:1058
  90.2 2.6 %shard_map.237 = (bf16[8,16,2048]{2,1,0:T(8,128)(2,1)}, bf16[16,4,2048]{2,1,0:T(4,128)(2,1)}, f32[6,4,2048]{2,1,0:T(4,128)}, bf16[8,16,2048]{2,1,0:T(8,128)(2,1)...) custom-call(bf16[8,16,2048]{2,1,0:T(8,128)(2,1)S(1)} %get-tuple-elem, ...), custom_call_target="tpu_custom_call" | custom-call | tf_op jit(solution)/shard_map/pallas_call | solution.py:1089

commit v5 on v4

--- a/solution.py
+++ b/solution.py
@@ -268,7 +268,7 @@
 
 
 MESH = pl.DeviceIdType.MESH
-SEMAPHORES = 164
+SEMAPHORES = 167
 F32 = jnp.float32
 BF16 = jnp.bfloat16
 NV = 512
@@ -317,7 +317,7 @@
     part, csend, crecv, xsend, xrecv,
     act1, act2, dred, conv, xhat1, slope1, xhat2, slope2, ex, dpre, dex, pat, dpo, pool, rows_pool,
     ge, gs, gr, ysend_e, yrecv_e, zsend_e, zrecv_e, ysend_s, yrecv_s, zsend_s, zrecv_s, ysend_r, yrecv_r, zsend_r, zrecv_r,
-    relay_e, relay_s, relay_r, acc_e, acc_s, acc_r, pgr,
+    acc_e, acc_s, acc_r, pgr,
     sem,
 ):
     i, r = lax.axis_index("dp"), lax.axis_index("rows")
@@ -400,7 +400,7 @@
         def __init__(self, parts, others):
             self.parts, self.others = parts, others
             count = len(parts(0))
-            self.send = new()
+            self.send, self.passed = new(), new()
             self.along_z = [new(3) for _ in range(count)]
             self.along_y = [new() for _ in range(count)]
 
@@ -411,11 +411,10 @@
     )
     share_e = Share(lambda k: (we.at[r, 2 * k + y],), lambda h: we.at[0, pl.ds(0, 4)])
     share_o = Share(lambda k: (we.at[xp[1], 2 * k + y],), lambda h: we.at[0, pl.ds(0, 4)])
-    passed_r = new()
 
     inner = ((z + 1) // 2) * (2 - (z + 1) // 2)
 
-    def line_send(share):
+    def line_send(share, direct=False):
         for h, own in enumerate(share.parts(z)):
 
             def go(slot, dev, own=own):
@@ -428,12 +427,23 @@
             def _(go=go, h=h):
                 go(share.along_z[h] + 1, on_line(-1))
 
-            go(share.along_y[h], yp)
-
-    def line_pass(share, h, send=None):
-        send = share.send if send is None else send
+            if direct:
+
+                @pl.when(jnp.logical_not(middle))
+                def _(go=go, h=h):
+                    go(share.along_z[h] + 2, on_line(3))
+
+    def line_over(share):
+        for h, own in enumerate(share.parts(z)):
+            copy(own, own, share.send, share.along_y[h], yp).start()
+
+    def line_pass(share, h, send=None, which=(0, 1, 2)):
+        relayed = send is None
+        send = share.send if relayed else send
 
         def take(places, slot, on=False):
+            if slot not in which:
+                return
             ref = share.parts(z + places * step)[h]
             got(ref, share.along_z[h] + slot)
             if on:
@@ -442,7 +452,7 @@
 
         @pl.when(middle)
         def _():
-            take(2, 0, True)
+            take(2, 0, relayed)
             take(1, 1)
             take(-1, 2)
 
@@ -468,7 +478,8 @@
     @pl.when(y == c)
     def _():
         stored(wr.at[r, z], l_wr)
-        line_send(share_r)
+        line_send(share_r, True)
+        line_over(share_r)
 
     s_sx, s_rx = ((new(), new()), (new(), new())), ((new(), new()), (new(), new()))
 
@@ -485,6 +496,9 @@
     spread_v(views, xv, 0, rest)
     spread_c(crops, xc4, 0, rest)
     spread_v(cot_views, cv, 1, rest[:1])
+    spread_c(cot_crops, cc4, 1, rest[:1])
+    stored(ws.at[:, i], l_ws)
+    line_over(share_s)
 
     for n in range(6):
         stored(raw[n], l_gain + n)
@@ -501,12 +515,12 @@
 
     @pl.when(y == c)
     def _():
-        line_pass(share_r, 0, passed_r)
-
+        line_pass(share_r, 0, share_r.passed)
+
+    got(pg.at[pl.ds(0, 7)], r_pg)
+    line_send(share_s)
     stored(xv.at[:, r], l_x[0])
     got(xv.at[:, pl.ds(0, 3)], s_rx[0][0])
-    stored(ws.at[:, i], l_ws)
-    line_send(share_s)
 
     @pl.when(y != c)
     def _():
@@ -514,7 +528,7 @@
 
     s_cs, r_cs = new(3), new(12)
     s_xs, r_xs = new(3), new(6)
-    s_ag, r_ag = new(3), new(12)
+    s_ag, r_ag = new(3), new(8)
 
     def scatter_start(op, kind, sums):
         rows = kind_rows(kind)
@@ -531,33 +545,60 @@
         n = pl.ds(0, KINDS[kind][1])
         got(crecv.at[op, kind, 1 - x, n], r_cs + 4 * op + 2 * kind)
         far = part[op, 2 * (1 - x) + c, rows, :] + crecv[op, kind, 1 - x, n, :].astype(F32)
-        xsend[op, kind, n, :] = far.astype(BF16)
-        copy(xsend.at[op, kind, n], xrecv.at[op, kind, n], s_xs + op, r_xs + 2 * op + kind, xp).start()
+        xsend[op, kind, 0, n, :] = far.astype(BF16)
+        copy(xsend.at[op, kind, 0, n], xrecv.at[op, kind, 0, n], s_xs + op, r_xs + 2 * op + kind, xp).start()
 
     def scatter_end(op, kind):
         rows = kind_rows(kind)
         n = pl.ds(0, KINDS[kind][1])
         got(crecv.at[op, kind, x, n], r_cs + 4 * op + 2 * kind + 1)
         near = part[op, 2 * x + c, rows, :] + crecv[op, kind, x, n, :].astype(F32)
-        got(xrecv.at[op, kind, n], r_xs + 2 * op + kind)
-        return near + xrecv[op, kind, n, :].astype(F32)
-
-    def gather_start(op, kind, buf, value):
+        got(xrecv.at[op, kind, 0, n], r_xs + 2 * op + kind)
+        return near + xrecv[op, kind, 0, n, :].astype(F32)
+
+    def gather_start(kind, buf, value):
         rows = kind_rows(kind)
         buf[r, rows, :] = value
         own = buf.at[r, rows]
-        copy(own, own, s_ag + op, r_ag + 4 * op + 2 * kind, xp).start()
-        copy(own, own, s_ag + op, r_ag + 4 * op + 2 * kind + 1, cp).start()
-
-    def gather_mid(op, kind, buf):
+        copy(own, own, s_ag + 1, r_ag + 6 + kind, xp).start()
+        copy(own, own, s_ag + 1, r_ag + 2 + kind, cp).start()
+
+    def gather_mid(kind, buf):
         far = buf.at[xp[1], kind_rows(kind)]
-        got(far, r_ag + 4 * op + 2 * kind)
-        copy(far, far, s_ag + op, r_ag + 4 * op + 2 * kind + 1, cp).start()
+        got(far, r_ag + 6 + kind)
+        copy(far, far, s_ag + 1, r_ag + 2 + kind, cp).start()
 
     def gather_end(op, kind, buf):
         rows = kind_rows(kind)
-        got(buf.at[pl.ds(0, 2), rows], r_ag + 4 * op + 2 * kind + 1)
+        got(buf.at[pl.ds(0, 2), rows], r_ag + 2 * op + kind)
         return jnp.concatenate([buf[s, rows, :] for s in range(4)], axis=1)
+
+    def both_mid(op, kind):
+        rows = kind_rows(kind)
+        n = pl.ds(0, KINDS[kind][1])
+        for near, xx in enumerate((1 - x, x)):
+            got(crecv.at[op, kind, xx, n], r_cs + 4 * op + 2 * kind + near)
+        for xx in range(2):
+            total = part[op, 2 * xx + c, rows, :] + crecv[op, kind, xx, n, :].astype(F32)
+            part[op, 2 * xx + c, rows, :] = total
+            xsend[op, kind, xx, n, :] = total.astype(BF16)
+        both = xsend.at[op, kind, :, n]
+        copy(both, xrecv.at[op, kind, :, n], s_xs + op, r_xs + 2 * op + kind, xp).start()
+
+    def both_end(op, kind):
+        rows = kind_rows(kind)
+        n = pl.ds(0, KINDS[kind][1])
+        got(xrecv.at[op, kind, :, n], r_xs + 2 * op + kind)
+        return jnp.concatenate(
+            [part[op, 2 * xx + c, rows, :] + xrecv[op, kind, xx, n, :].astype(F32) for xx in range(2)], axis=1
+        )
+
+    def both_out(op, kind, buf, value):
+        rows = kind_rows(kind)
+        for xx in range(2):
+            buf[2 * xx + c, rows, :] = value[:, 128 * xx : 128 * xx + 128]
+            own = buf.at[2 * xx + c, rows]
+            copy(own, own, s_ag + op, r_ag + 2 * op + kind, cp).start()
 
     weight_r = wr[r].reshape(512, 512)
     scatter_start(0, 0, dot(xv[...].reshape(NV, 512), weight_r))
@@ -565,15 +606,17 @@
     got(xc4.at[pl.ds(0, 3)], s_rx[0][1])
     xc[...] = xc4[...].reshape(4, 64, 512)
     scatter_start(0, 1, dot(xc[...].reshape(NC, 512), weight_r))
-    scatter_mid(0, 0)
-    scatter_mid(0, 1)
-    spread_c(cot_crops, cc4, 1, rest[:1])
-
-    got(pg.at[pl.ds(0, 7)], r_pg)
+    line_pass(share_s, 0, None, (0, 1))
+    both_mid(0, 0)
+    both_mid(0, 1)
+
     half = lax.broadcasted_iota(jnp.int32, (1, 128), 1) < 64
-    gain1, shift1, gain2, shift2 = [
-        jnp.where(half, pg[2 * r, q : q + 1, :], pg[2 * r + 1, q : q + 1, :]) for q in range(4)
-    ]
+
+    def slice_of(s, q):
+        return jnp.where(half, pg[2 * s, q : q + 1, :], pg[2 * s + 1, q : q + 1, :])
+
+    gain1, shift1 = [jnp.concatenate([slice_of(c, q), slice_of(2 + c, q)], axis=1) for q in range(2)]
+    gain2, shift2 = slice_of(r, 2), slice_of(r, 3)
     gain3 = jnp.concatenate([pg[2 * k + c, pl.ds(4 + x, 1), :] for k in range(4)], axis=1)
     shift3 = jnp.concatenate([pg[2 * k + c, pl.ds(6 + x, 1), :] for k in range(4)], axis=1)
 
@@ -586,22 +629,22 @@
         sig = sigmoid(norm)
         return rstd, xhat, sig * (1.0 + norm * (1.0 - sig)), (norm * sig).astype(BF16)
 
-    line_pass(share_s, 0)
-    line_pass(share_s, 1)
+    for h, which in ((1, (0, 1)), (0, (2,)), (2, (0, 1)), (1, (2,)), (2, (2,))):
+        line_pass(share_s, h, None, which)
+    stored(we.at[r, i], l_we)
+    stored(we.at[r, i], l_we2)
+    for share in (share_e, share_o):
+        line_send(share, True)
+        line_over(share)
     rstd1, rstd2 = [None, None], [None, None]
     for kind in range(2):
         rows = KINDS[kind][1]
-        rstd1[kind], xh, sl, act = norm_act(scatter_end(0, kind), rows, gain1, shift1)
-        gather_start(0, kind, act1, act)
+        rstd1[kind], xh, sl, act = norm_act(both_end(0, kind), rows, gain1, shift1)
+        both_out(0, kind, act1, act)
         xhat1[kind_rows(kind), :] = xh
         slope1[kind_rows(kind), :] = sl
-    spread_v(cot_views, cv, 1, rest[1:])
-    spread_c(cot_crops, cc4, 1, rest[1:])
-    line_pass(share_s, 2)
-    stored(we.at[r, i], l_we)
-    line_send(share_e)
-    for kind in range(2):
-        gather_mid(0, kind, act1)
+        if kind == 0:
+            spread_v(cot_views, cv, 1, rest[1:])
 
     s_ow, s_xw, r_xw, r_ow = new(), new(), new(), new(2)
 
@@ -612,7 +655,9 @@
         copy(ref, ref, s_ow, r_ow + n, cp).start()
 
     between(wr.at[r], 0)
+    line_pass(share_e, 0, share_e.passed, (0,))
     line_got(share_s)
+    line_pass(share_e, 0, share_e.passed, (1,))
 
     def weight_s():
         return jnp.concatenate([ws[t].reshape(512, 128) for t in range(9)], axis=1)
@@ -627,24 +672,20 @@
             col = turned(col, kind, 1 - j)
             spatial = col if spatial is None else spatial + col
         rstd2[kind], xh, sl, act = norm_act(spatial, rows, gain2, shift2)
-        gather_start(1, kind, act2, act)
+        gather_start(kind, act2, act)
         xhat2[kind_rows(kind), :] = xh
         slope2[kind_rows(kind), :] = sl
         if kind == 0:
-            line_pass(share_e, 0)
-            stored(we.at[r, i], l_we2)
-            line_send(share_o)
+            line_pass(share_e, 0, share_e.passed, (2,))
+    spread_c(cot_crops, cc4, 1, rest[1:])
     over_x(0)
     over_x(1)
     pool[...] = jnp.zeros_like(pool)
-    for kind in range(2):
-        gather_mid(1, kind, act2)
+    gather_mid(0, act2)
     stored(cv.at[:, r], l_cot[0])
-    stored(cc4.at[r], l_cot[1])
     got(cv.at[:, pl.ds(0, 3)], s_rx[1][0])
-    got(cc4.at[pl.ds(0, 3)], s_rx[1][1])
-    cc[...] = cc4[...].reshape(4, 64, 512)
     line_got(share_e)
+    line_pass(share_o, 0, share_o.passed)
     between(we.at[r], 1)
     weight_e = we[r].reshape(512, 512)
 
@@ -660,6 +701,8 @@
             return acc[0] + jnp.sum(e, axis=0), acc[1] + jnp.sum(e * e, axis=0)
 
         tot, sq = lax.fori_loop(0, rows // 32, moments, (zero8, zero8))
+        if kind == 0:
+            gather_mid(1, act2)
         mean = jnp.sum(tot, axis=0, keepdims=True) / rows
         rstd = lax.rsqrt(jnp.sum(sq, axis=0, keepdims=True) / rows - mean * mean + EPSILON)
 
@@ -741,10 +784,10 @@
     order = [far_of, mid_of, z + step, z]
 
     class Grad:
-        def __init__(self, full, ysend, yrecv, zsend, zrecv, relay, acc, both=True):
+        def __init__(self, full, ysend, yrecv, zsend, zrecv, acc, both=True):
             self.full, self.ysend, self.yrecv, self.zsend, self.zrecv = full, ysend, yrecv, zsend, zrecv
-            self.relay, self.acc, self.both = relay, acc, both
-            self.s_y, self.r_y, self.s_z, self.r_z, self.r_relay = new(), new(4), new(), new(), new()
+            self.acc, self.both = acc, both
+            self.s_y, self.r_y, self.s_z, self.r_z = new(), new(4), new(), new()
 
         def start(self):
             for k in order:
@@ -760,35 +803,14 @@
             copy(self.zsend.at[k], self.zrecv.at[z], self.s_z, self.r_z, (2 * k + y, r)).start()
 
         def along(self):
-            @pl.when(jnp.logical_not(middle))
-            def _():
-                k = order[0]
-                self.zsend[k] = self.add(k).astype(BF16)
-                copy(self.zsend.at[k], self.relay, self.s_z, self.r_relay, on_line(1)).start()
-
-            self.send(order[1], self.add(order[1]))
-            self.send(order[2], self.add(order[2]))
-
-        def hand_on(self):
-            @pl.when(middle)
-            def _():
-                total = self.add(order[0])
-                got(self.relay, self.r_relay)
-                self.send(order[0], total + self.relay[...].astype(F32))
+            for k in order[:3]:
+                self.send(k, self.add(k))
 
         def total(self):
             self.acc[...] = self.add(z)
-
-            @pl.when(middle)
-            def _():
-                got(self.zrecv.at[pl.ds(0, 3)], self.r_z)
-                self.acc[...] += self.zrecv[z - step].astype(F32)
-
-            @pl.when(jnp.logical_not(middle))
-            def _():
-                got(self.zrecv.at[pl.ds(0, 2)], self.r_z)
-
-            return self.acc[...] + self.zrecv[z + step].astype(F32) + self.zrecv[z + 2 * step].astype(F32)
+            got(self.zrecv.at[pl.ds(0, 3)], self.r_z)
+            self.acc[...] += self.zrecv[order[0]].astype(F32) + self.zrecv[order[1]].astype(F32)
+            return self.acc[...] + self.zrecv[order[2]].astype(F32)
 
         def sent(self):
             sent(self.zsend.at[pl.ds(0, 3)], self.s_z)
@@ -811,16 +833,18 @@
             got(self.buf.at[pl.ds(0, 2)], self.near)
             sent(self.buf.at[pl.ds(0, 3)], self.send)
 
-    grad_e = Grad(ge, ysend_e, yrecv_e, zsend_e, zrecv_e, relay_e, acc_e)
+    grad_e = Grad(ge, ysend_e, yrecv_e, zsend_e, zrecv_e, acc_e)
     grad_s = [
-        Grad(*(one.at[q] for one in (gs, ysend_s, yrecv_s, zsend_s, zrecv_s, relay_s, acc_s))) for q in range(3)
+        Grad(*(one.at[q] for one in (gs, ysend_s, yrecv_s, zsend_s, zrecv_s, acc_s))) for q in range(3)
     ]
-    grad_r = Grad(gr, ysend_r, yrecv_r, zsend_r, zrecv_r, relay_r, acc_r, False)
+    grad_r = [Grad(*(one.at[q] for one in (gr, ysend_r, yrecv_r, zsend_r, zrecv_r, acc_r)), both=False) for q in range(2)]
     slices_p, slices_e, slices_s = Slices(fin_p), Slices(fin_e), [Slices(fin_s.at[q]) for q in range(3)]
 
     expand(0)
     scatter_start(1, 0, dot(dex[kind_rows(0), :], weight_e, NT))
-    line_pass(share_o, 0)
+    stored(cc4.at[r], l_cot[1])
+    got(cc4.at[pl.ds(0, 3)], s_rx[1][1])
+    cc[...] = cc4[...].reshape(4, 64, 512)
     expand(1)
     scatter_mid(1, 0)
     scatter_start(1, 1, dot(dex[kind_rows(1), :], weight_e, NT))
@@ -830,7 +854,6 @@
     s_af, r_af = new(), new()
     for dev in rest:
         copy(aff.at[r], aff.at[r], s_af, r_af, dev).start()
-    over_x(2)
 
     def norm_back(d, xhat, rstd, gain, rows):
         sd = jnp.sum(d, axis=0, keepdims=True)
@@ -850,36 +873,39 @@
             for ti in range(3):
                 t = 3 * ti + tj
                 pat[kind_rows(kind), 128 * t : 128 * t + 128] = moved(col, kind, ti - 1).astype(BF16)
+        if kind == 1:
+            both_mid(2, 0)
         scatter_start(2, kind, dot(pat[kind_rows(kind), :], weight_s(), NT))
-        if kind == 1:
-            scatter_mid(2, 0)
-    scatter_mid(2, 1)
     full1 = jnp.concatenate([act1[s] for s in range(4)], axis=1)
+    grad_e.along()
     for q in range(3):
         gs[q] = dot(full1, pat[:, 384 * q : 384 * q + 384], TN).reshape(4, 2, 64, 384)
         grad_s[q].start()
-    grad_e.along()
+    both_mid(2, 1)
+    over_x(2)
+    over_x(3)
     line_got(share_o)
     between(we.at[xp[1]], 1)
+    grad_s[0].along()
 
     sum_d1, sum_x1 = [], []
     for kind in range(2):
         rows = KINDS[kind][1]
-        d = scatter_end(2, kind) * slope1[kind_rows(kind), :]
+        d = both_end(2, kind) * slope1[kind_rows(kind), :]
         dz_, sd, sxx = norm_back(d, xhat1[kind_rows(kind), :], rstd1[kind], gain1, rows)
         sum_d1.append(sd)
         sum_x1.append(sxx)
-        gather_start(2, kind, dred, dz_.astype(BF16))
-
-    rows12 = [sum_x1[0] + sum_x1[1], sum_d1[0] + sum_d1[1], sum_x2[0] + sum_x2[1], sum_d2[0] + sum_d2[1]]
+        both_out(2, kind, dred, dz_.astype(BF16))
+
+    gx1, gd1 = sum_x1[0] + sum_x1[1], sum_d1[0] + sum_d1[1]
+    rows12 = [jnp.where(x == 0, g[:, :128], g[:, 128:]) for g in (gx1, gd1)]
+    rows12 += [sum_x2[0] + sum_x2[1], sum_d2[0] + sum_d2[1]]
     gx3, gd3 = sum_x3[0] + sum_x3[1], sum_d3[0] + sum_d3[1]
     rows3 = [g[:, 128 * k : 128 * k + 128] for g in (gx3, gd3) for k in range(4)]
     pgr[i] = jnp.concatenate(rows12 + rows3 + [jnp.zeros((4, 128), F32)], axis=0)
     s_pp, r_pp, s_ps, r_ps = new(), new(), new(), new()
     for dev in peers[:7]:
         copy(pgr.at[i], pgr.at[i], s_pp, r_pp, dev).start()
-    over_x(3)
-    grad_e.hand_on()
 
     rows_pool[...] = jnp.zeros_like(rows_pool)
     for n in range(8):
@@ -889,50 +915,43 @@
             row = 4 * (2 + 2 * (n % 2) + m) + n // 2
             rows_pool[row : row + 1, :] = jnp.sum(pool[8 + n, 4 * m : 4 * m + 4, :], axis=0, keepdims=True) / 16.0
     slices_p.start(rows_pool[...])
-    grad_s[0].along()
-    gather_mid(2, 0, dred)
     grad_s[1].along()
-    gather_mid(2, 1, dred)
-    grad_s[0].hand_on()
     full_d = [gather_end(2, kind, dred) for kind in range(2)]
 
     for m in range(4):
         col = dot(xv[:, :, :, 128 * m : 128 * m + 128].reshape(NV, 128), full_d[0], TN)
-        gr[m] = col + dot(xc[:, :, 128 * m : 128 * m + 128].reshape(NC, 128), full_d[1], TN)
+        col = col + dot(xc[:, :, 128 * m : 128 * m + 128].reshape(NC, 128), full_d[1], TN)
+        for q in range(2):
+            gr[q, m] = col[:, 256 * q : 256 * q + 256]
 
     @pl.when(y != c)
     def _():
-        grad_r.start()
-
-    got(wr.at[0], r_xw)
-    between(wr.at[xp[1]], 0)
+        for one in grad_r:
+            one.start()
+
     for n, ref in enumerate((xo_v, xo_c, co_v, co_c)):
         stored(ref, l_own + n)
     got(aff.at[pl.ds(0, 3)], r_af)
     got(we.at[pl.ds(0, 2)], r_ow + 1)
     own_output()
-    grad_s[1].hand_on()
     grad_s[2].along()
+    slices_s[0].start(grad_s[0].total())
     slices_e.start(grad_e.total())
-    slices_s[0].start(grad_s[0].total())
+    got(wr.at[0], r_xw)
+    between(wr.at[xp[1]], 0)
+
+    @pl.when(y == c)
+    def _():
+        grad_r[0].along()
+        grad_r[1].along()
+
+
+    slices_s[1].start(grad_s[1].total())
     got(wr.at[pl.ds(0, 2)], r_ow)
     own_gradient()
-
-    @pl.when(y == c)
-    def _():
-        grad_r.along()
-
-    grad_s[2].hand_on()
-    slices_s[1].start(grad_s[1].total())
     slices_p.mid()
     slices_e.mid()
-
-    @pl.when(y == c)
-    def _():
-        grad_r.hand_on()
-
     slices_s[0].mid()
-    slices_s[2].start(grad_s[2].total())
 
     got(pgr.at[pl.ds(0, 7)], r_pp)
     total = pgr[0]
@@ -941,23 +960,26 @@
     pgs[r] = total
     for dev in rest:
         copy(pgs.at[r], pgs.at[r], s_ps, r_ps, dev).start()
+    slices_s[2].start(grad_s[2].total())
     slices_s[1].mid()
 
-    s_fr, r_fr = new(), new()
-
-    @pl.when(y == c)
-    def _():
-        fin_r[x] = grad_r.total().astype(BF16)
-        copy(fin_r.at[x], fin_r.at[x], s_fr, r_fr, xp).start()
-        copy(fin_r.at[x], fin_r.at[x], s_fr, r_fr, cp).start()
+    s_fr, r_fr = new(2), new(2)
+    for q in range(2):
+
+        @pl.when(y == c)
+        def _(q=q):
+            fin_r[q, x] = grad_r[q].total().astype(BF16)
+            copy(fin_r.at[q, x], fin_r.at[q, x], s_fr + q, r_fr + q, xp).start()
+            copy(fin_r.at[q, x], fin_r.at[q, x], s_fr + q, r_fr + q, cp).start()
 
     slices_s[2].mid()
-
-    @pl.when(y == c)
-    def _():
-        far = fin_r.at[1 - x]
-        got(far, r_fr)
-        copy(far, far, s_fr, r_fr, cp).start()
+    for q in range(2):
+
+        @pl.when(y == c)
+        def _(q=q):
+            far = fin_r.at[q, 1 - x]
+            got(far, r_fr + q)
+            copy(far, far, s_fr + q, r_fr + q, cp).start()
 
     for one in (slices_p, slices_e, *slices_s):
         one.end()
@@ -972,27 +994,30 @@
     sent(pgr.at[pl.ds(0, 7)], s_pp)
     sent(pgs.at[pl.ds(0, 3)], s_ps)
     line_sent(share_s.send, ws, ws.at[:, pl.ds(0, 6)])
-    line_sent(share_e.send, we.at[0], we.at[0, pl.ds(0, 6)])
-    line_sent(share_o.send, we.at[0], we.at[0, pl.ds(0, 6)])
+    for share in (share_e, share_o):
+        sent(we.at[0, pl.ds(0, 4)], share.send)
+        sent(we.at[0, pl.ds(0, 3)], share.passed)
     for op in range(3):
         sent(act1.at[pl.ds(0, 2)], s_cs + op)
-        sent(act1.at[0], s_xs + op)
-        sent(act1.at[pl.ds(0, 3)], s_ag + op)
+        sent(act1.at[pl.ds(0, 1 if op == 1 else 2)], s_xs + op)
+        sent(act1.at[pl.ds(0, 3 if op == 1 else 2)], s_ag + op)
     for one in (grad_e, *grad_s):
         sent(one.ysend, one.s_y)
         one.sent()
 
     @pl.when(y != c)
     def _():
-        sent(ysend_r, grad_r.s_y)
-        got(fin_r, r_fr)
+        for q, one in enumerate(grad_r):
+            sent(one.ysend, one.s_y)
+            got(fin_r.at[q], r_fr + q)
 
     @pl.when(y == c)
     def _():
-        line_sent(share_r.send, wr.at[0], wr.at[0, pl.ds(0, 3)])
-        line_sent(passed_r, wr.at[0], wr.at[0, pl.ds(0, 3)])
-        grad_r.sent()
-        sent(wr.at[0, pl.ds(0, 3)], s_fr)
+        sent(wr.at[0], share_r.send)
+        sent(wr.at[0, pl.ds(0, 3)], share_r.passed)
+        for q, one in enumerate(grad_r):
+            one.sent()
+            sent(one.zsend.at[pl.ds(0, 3)], s_fr + q)
 
     assert taken[0] == SEMAPHORES, taken
 
@@ -1023,7 +1048,8 @@
             lo = 512 * k + 256 * (s % 2) + 128 * (s // 2)
             ge[:, lo : lo + 128] = fin_e[s, :, 128 * k : 128 * k + 128].astype(F32)
     store(ge, grad_expand)
-    gr[...] = fin_r[...].astype(F32).reshape(256, 512)
+    for n in range(2):
+        gr[:, 256 * n : 256 * n + 256] = fin_r[n].astype(F32).reshape(256, 256)
     store(gr, grad_reduce)
     oc[...] = out_c[...].reshape(16, 4, 2048)
     store(oc, out_crops)
@@ -1059,7 +1085,7 @@
         block_kernel,
         out_shape=[
             buf((8, 16, 2048)), buf((64, 2048)), buf((4, 32, 512)), buf((8, 16, 2048)), buf((64, 2048)),
-            buf((4, 64, 512)), buf((3, 4, 64, 384)), buf((2, 128, 512)), buf((4, 16, 128), F32),
+            buf((4, 64, 512)), buf((3, 4, 64, 384)), buf((2, 2, 128, 256)), buf((4, 16, 128), F32),
         ],
         in_specs=[hbm] * 13,
         out_specs=[vmem] * 9,
@@ -1069,16 +1095,16 @@
             buf((8, 16, 2048)), buf((16, 4, 2048)), buf((8, 16, 2048)), buf((16, 4, 2048)),
             buf((4, 4, 128, 512)), buf((9, 8, 64, 128)), buf((4, 8, 64, 512)), buf((4, 8, 512), F32), buf((64,)), buf((64,)), buf((64,)), buf((64,)), buf((256,)), buf((256,)), buf((8, 8, 128), F32),
             buf((3, 4, N, 128), F32), buf((3, 2, 2, NV, 128)), buf((3, 2, 2, NV, 128)),
-            buf((3, 2, NV, 128)), buf((3, 2, NV, 128)),
+            buf((3, 2, 2, NV, 128)), buf((3, 2, 2, NV, 128)),
             buf((4, N, 128)), buf((4, N, 128)), buf((4, N, 128)), buf((N, 1152), F32),
-            buf((N, 128), F32), buf((N, 128), F32), buf((N, 128), F32), buf((N, 128), F32),
+            buf((N, 256), F32), buf((N, 256), F32), buf((N, 128), F32), buf((N, 128), F32),
             buf((N, 512), F32), buf((N, 512), F32), buf((N, 512)), buf((N, 1152)),
             buf((192, 2048), F32), buf((16, 8, 512), F32), buf((32, 512), F32),
-            buf((4, 2, 64, 512), F32), buf((3, 4, 2, 64, 384), F32), buf((4, 128, 512), F32),
+            buf((4, 2, 64, 512), F32), buf((3, 4, 2, 64, 384), F32), buf((2, 4, 128, 256), F32),
             buf((4, 64, 512)), buf((4, 64, 512)), buf((4, 64, 512)), buf((4, 64, 512)),
             buf((3, 4, 64, 384)), buf((3, 4, 64, 384)), buf((3, 4, 64, 384)), buf((3, 4, 64, 384)),
-            buf((4, 128, 512)), buf((4, 128, 512)), buf((4, 128, 512)), buf((4, 128, 512)),
-            buf((64, 512)), buf((3, 64, 384)), buf((128, 512)), buf((64, 512), F32), buf((3, 64, 384), F32), buf((128, 512), F32),
+            buf((2, 4, 128, 256)), buf((2, 4, 128, 256)), buf((2, 4, 128, 256)), buf((2, 4, 128, 256)),
+            buf((64, 512), F32), buf((3, 64, 384), F32), buf((2, 128, 256), F32),
             buf((8, 16, 128), F32),
             dma(SEMAPHORES),
         ],

time: 92.9 us -> 88.8 us (0.956)
  Pallas kernels: 92.1 us -> 88 us
    pallas_call x1, Pallas kernels: 89.5 us -> 85.4 us  [fused(): pl.pallas_call(block_kernel, out_shape=[buf((8, 16, 2048)), buf((64, 2048...]
where the time goes in v5:
time: 88.8 us; the launch traced here: 88.6 us
  Pallas kernels  88 us (99%)
    pallas_call x1, Pallas kernels, fused(): pl.pallas_call(block_kernel, out_shape=[buf((8, 16, 2048)), buf((64, 2048...  85.4 us
    pallas_call x1, Pallas kernels, fused(): pl.pallas_call(store_kernel, out_shape=[shape((8, 16, 2048), BF16), shape...  2.59 us

profile of v5, /device:TPU:0, one launch (start us, length us, event | category | flops | bytes accessed | tf_op | source)
XLA Modules:
  0.0 88.6 jit_solution(3711307914256876486)
XLA Ops:
  0.7 85.4 %shard_map.236 = (bf16[8,16,2048]{2,1,0:T(8,128)(2,1)S(1)}, bf16[64,2048]{1,0:T(8,128)(2,1)S(1)}, bf16[4,32,512]{2,1,0:T(8,128)(2,1)S(1)}, bf16[8,16,2048]{2,1,0...) custom-call(bf16[8,16,2048]{2,1,0:T(8,128)(2,1)} %bitcast.17, ...), custom_call_target="tpu_custom_call" | custom-call | flops 5200000000 | bytes 8000000 | tf_op jit(solution)/shard_map/pallas_call | solution.py:1084
  86.0 2.6 %shard_map.237 = (bf16[8,16,2048]{2,1,0:T(8,128)(2,1)}, bf16[16,4,2048]{2,1,0:T(4,128)(2,1)}, f32[6,4,2048]{2,1,0:T(4,128)}, bf16[8,16,2048]{2,1,0:T(8,128)(2,1)...) custom-call(bf16[8,16,2048]{2,1,0:T(8,128)(2,1)S(1)} %get-tuple-elem, ...), custom_call_target="tpu_custom_call" | custom-call | tf_op jit(solution)/shard_map/pallas_call | solution.py:1115

commit v6 on v5

--- a/solution.py
+++ b/solution.py
@@ -268,7 +268,7 @@
 
 
 MESH = pl.DeviceIdType.MESH
-SEMAPHORES = 167
+SEMAPHORES = 174
 F32 = jnp.float32
 BF16 = jnp.bfloat16
 NV = 512
@@ -317,7 +317,7 @@
     part, csend, crecv, xsend, xrecv,
     act1, act2, dred, conv, xhat1, slope1, xhat2, slope2, ex, dpre, dex, pat, dpo, pool, rows_pool,
     ge, gs, gr, ysend_e, yrecv_e, zsend_e, zrecv_e, ysend_s, yrecv_s, zsend_s, zrecv_s, ysend_r, yrecv_r, zsend_r, zrecv_r,
-    acc_e, acc_s, acc_r, pgr,
+    relay_e, relay_s, acc_e, acc_s, acc_r, pgr,
     sem,
 ):
     i, r = lax.axis_index("dp"), lax.axis_index("rows")
@@ -527,12 +527,14 @@
         got(wr.at[r], share_r.along_y[0])
 
     s_cs, r_cs = new(3), new(12)
-    s_xs, r_xs = new(3), new(6)
+    s_xs, r_xs = new(3), new(12)
     s_ag, r_ag = new(3), new(8)
 
     def scatter_start(op, kind, sums):
         rows = kind_rows(kind)
         n = pl.ds(0, KINDS[kind][1])
+        if op == 0:
+            sums = sums - jnp.sum(sums, axis=0, keepdims=True) / KINDS[kind][1]
         for s in range(4):
             part[op, s, rows, :] = sums[:, 128 * s : 128 * s + 128]
         for near, xx in enumerate((1 - x, x)):
@@ -546,14 +548,14 @@
         got(crecv.at[op, kind, 1 - x, n], r_cs + 4 * op + 2 * kind)
         far = part[op, 2 * (1 - x) + c, rows, :] + crecv[op, kind, 1 - x, n, :].astype(F32)
         xsend[op, kind, 0, n, :] = far.astype(BF16)
-        copy(xsend.at[op, kind, 0, n], xrecv.at[op, kind, 0, n], s_xs + op, r_xs + 2 * op + kind, xp).start()
+        copy(xsend.at[op, kind, 0, n], xrecv.at[op, kind, 0, n], s_xs + op, r_xs + 4 * op + 2 * kind, xp).start()
 
     def scatter_end(op, kind):
         rows = kind_rows(kind)
         n = pl.ds(0, KINDS[kind][1])
         got(crecv.at[op, kind, x, n], r_cs + 4 * op + 2 * kind + 1)
         near = part[op, 2 * x + c, rows, :] + crecv[op, kind, x, n, :].astype(F32)
-        got(xrecv.at[op, kind, 0, n], r_xs + 2 * op + kind)
+        got(xrecv.at[op, kind, 0, n], r_xs + 4 * op + 2 * kind)
         return near + xrecv[op, kind, 0, n, :].astype(F32)
 
     def gather_start(kind, buf, value):
@@ -582,23 +584,19 @@
             total = part[op, 2 * xx + c, rows, :] + crecv[op, kind, xx, n, :].astype(F32)
             part[op, 2 * xx + c, rows, :] = total
             xsend[op, kind, xx, n, :] = total.astype(BF16)
-        both = xsend.at[op, kind, :, n]
-        copy(both, xrecv.at[op, kind, :, n], s_xs + op, r_xs + 2 * op + kind, xp).start()
-
-    def both_end(op, kind):
+            one = xsend.at[op, kind, xx, n]
+            copy(one, xrecv.at[op, kind, xx, n], s_xs + op, r_xs + 4 * op + 2 * kind + xx, xp).start()
+
+    def both_end(op, kind, xx):
+        n = pl.ds(0, KINDS[kind][1])
+        got(xrecv.at[op, kind, xx, n], r_xs + 4 * op + 2 * kind + xx)
+        return part[op, 2 * xx + c, kind_rows(kind), :] + xrecv[op, kind, xx, n, :].astype(F32)
+
+    def both_out(op, kind, xx, buf, value):
         rows = kind_rows(kind)
-        n = pl.ds(0, KINDS[kind][1])
-        got(xrecv.at[op, kind, :, n], r_xs + 2 * op + kind)
-        return jnp.concatenate(
-            [part[op, 2 * xx + c, rows, :] + xrecv[op, kind, xx, n, :].astype(F32) for xx in range(2)], axis=1
-        )
-
-    def both_out(op, kind, buf, value):
-        rows = kind_rows(kind)
-        for xx in range(2):
-            buf[2 * xx + c, rows, :] = value[:, 128 * xx : 128 * xx + 128]
-            own = buf.at[2 * xx + c, rows]
-            copy(own, own, s_ag + op, r_ag + 2 * op + kind, cp).start()
+        buf[2 * xx + c, rows, :] = value
+        own = buf.at[2 * xx + c, rows]
+        copy(own, own, s_ag + op, r_ag + 2 * op + kind, cp).start()
 
     weight_r = wr[r].reshape(512, 512)
     scatter_start(0, 0, dot(xv[...].reshape(NV, 512), weight_r))
@@ -615,7 +613,7 @@
     def slice_of(s, q):
         return jnp.where(half, pg[2 * s, q : q + 1, :], pg[2 * s + 1, q : q + 1, :])
 
-    gain1, shift1 = [jnp.concatenate([slice_of(c, q), slice_of(2 + c, q)], axis=1) for q in range(2)]
+    gain1, shift1 = [[slice_of(2 * xx + c, q) for xx in range(2)] for q in range(2)]
     gain2, shift2 = slice_of(r, 2), slice_of(r, 3)
     gain3 = jnp.concatenate([pg[2 * k + c, pl.ds(4 + x, 1), :] for k in range(4)], axis=1)
     shift3 = jnp.concatenate([pg[2 * k + c, pl.ds(6 + x, 1), :] for k in range(4)], axis=1)
@@ -636,13 +634,14 @@
     for share in (share_e, share_o):
         line_send(share, True)
         line_over(share)
-    rstd1, rstd2 = [None, None], [None, None]
+    rstd1, rstd2 = [[None, None], [None, None]], [None, None]
     for kind in range(2):
         rows = KINDS[kind][1]
-        rstd1[kind], xh, sl, act = norm_act(both_end(0, kind), rows, gain1, shift1)
-        both_out(0, kind, act1, act)
-        xhat1[kind_rows(kind), :] = xh
-        slope1[kind_rows(kind), :] = sl
+        for xx in range(2):
+            rstd1[kind][xx], xh, sl, act = norm_act(both_end(0, kind, xx), rows, gain1[xx], shift1[xx])
+            both_out(0, kind, xx, act1, act)
+            xhat1[xx, kind_rows(kind), :] = xh
+            slope1[xx, kind_rows(kind), :] = sl
         if kind == 0:
             spread_v(cot_views, cv, 1, rest[1:])
 
@@ -726,7 +725,7 @@
             dx = d * xhat
             return acc[0] + (d[:8] + d[8:]), acc[1] + (dx[:8] + dx[8:])
 
-        sd, sxx = lax.fori_loop(0, rows // 16, finish, (zero8, zero8))
+        sd, sxx = lax.fori_loop(0, rows // 16, finish, (zero8, zero8), unroll=2)
         sd, sxx = jnp.sum(sd, axis=0, keepdims=True), jnp.sum(sxx, axis=0, keepdims=True)
         sum_d3.append(sd)
         sum_x3.append(sxx)
@@ -784,10 +783,10 @@
     order = [far_of, mid_of, z + step, z]
 
     class Grad:
-        def __init__(self, full, ysend, yrecv, zsend, zrecv, acc, both=True):
+        def __init__(self, full, ysend, yrecv, zsend, zrecv, acc, relay=None, both=True):
             self.full, self.ysend, self.yrecv, self.zsend, self.zrecv = full, ysend, yrecv, zsend, zrecv
-            self.acc, self.both = acc, both
-            self.s_y, self.r_y, self.s_z, self.r_z = new(), new(4), new(), new()
+            self.acc, self.relay, self.both = acc, relay, both
+            self.s_y, self.r_y, self.s_z, self.r_z, self.r_relay = new(), new(4), new(), new(), new()
 
         def start(self):
             for k in order:
@@ -803,39 +802,62 @@
             copy(self.zsend.at[k], self.zrecv.at[z], self.s_z, self.r_z, (2 * k + y, r)).start()
 
         def along(self):
-            for k in order[:3]:
-                self.send(k, self.add(k))
+            if self.relay is None:
+                self.send(order[0], self.add(order[0]))
+            else:
+
+                @pl.when(jnp.logical_not(middle))
+                def _():
+                    self.zsend[order[0]] = self.add(order[0]).astype(BF16)
+                    copy(self.zsend.at[order[0]], self.relay, self.s_z, self.r_relay, on_line(1)).start()
+
+            self.send(order[1], self.add(order[1]))
+            self.send(order[2], self.add(order[2]))
+
+        def hand_on(self):
+            @pl.when(middle)
+            def _():
+                total = self.add(order[0])
+                got(self.relay, self.r_relay)
+                self.send(order[0], total + self.relay[...].astype(F32))
 
         def total(self):
             self.acc[...] = self.add(z)
-            got(self.zrecv.at[pl.ds(0, 3)], self.r_z)
-            self.acc[...] += self.zrecv[order[0]].astype(F32) + self.zrecv[order[1]].astype(F32)
-            return self.acc[...] + self.zrecv[order[2]].astype(F32)
+            if self.relay is None:
+                got(self.zrecv.at[pl.ds(0, 3)], self.r_z)
+                self.acc[...] += self.zrecv[order[0]].astype(F32) + self.zrecv[order[1]].astype(F32)
+                return self.acc[...] + self.zrecv[order[2]].astype(F32)
+
+            @pl.when(middle)
+            def _():
+                got(self.zrecv.at[pl.ds(0, 3)], self.r_z)
+                self.acc[...] += self.zrecv[z - step].astype(F32)
+
+            @pl.when(jnp.logical_not(middle))
+            def _():
+                got(self.zrecv.at[pl.ds(0, 2)], self.r_z)
+
+            return self.acc[...] + self.zrecv[z + step].astype(F32) + self.zrecv[z + 2 * step].astype(F32)
 
         def sent(self):
             sent(self.zsend.at[pl.ds(0, 3)], self.s_z)
 
     class Slices:
         def __init__(self, buf):
-            self.buf, self.send, self.far, self.near = buf, new(), new(), new()
+            self.buf, self.send, self.come = buf, new(), new()
 
         def start(self, value):
             self.buf[r] = value.astype(BF16)
-            copy(self.buf.at[r], self.buf.at[r], self.send, self.far, xp).start()
-            copy(self.buf.at[r], self.buf.at[r], self.send, self.near, cp).start()
-
-        def mid(self):
-            far = self.buf.at[xp[1]]
-            got(far, self.far)
-            copy(far, far, self.send, self.near, cp).start()
+            for dev in rest:
+                copy(self.buf.at[r], self.buf.at[r], self.send, self.come, dev).start()
 
         def end(self):
-            got(self.buf.at[pl.ds(0, 2)], self.near)
+            got(self.buf.at[pl.ds(0, 3)], self.come)
             sent(self.buf.at[pl.ds(0, 3)], self.send)
 
-    grad_e = Grad(ge, ysend_e, yrecv_e, zsend_e, zrecv_e, acc_e)
+    grad_e = Grad(ge, ysend_e, yrecv_e, zsend_e, zrecv_e, acc_e, relay_e)
     grad_s = [
-        Grad(*(one.at[q] for one in (gs, ysend_s, yrecv_s, zsend_s, zrecv_s, acc_s))) for q in range(3)
+        Grad(*(one.at[q] for one in (gs, ysend_s, yrecv_s, zsend_s, zrecv_s, acc_s, relay_s))) for q in range(3)
     ]
     grad_r = [Grad(*(one.at[q] for one in (gr, ysend_r, yrecv_r, zsend_r, zrecv_r, acc_r)), both=False) for q in range(2)]
     slices_p, slices_e, slices_s = Slices(fin_p), Slices(fin_e), [Slices(fin_s.at[q]) for q in range(3)]
@@ -860,6 +882,11 @@
         sxx = jnp.sum(d * xhat, axis=0, keepdims=True)
         return (gain * rstd) * (d - sd / rows - xhat * (sxx / rows)), sd, sxx
 
+    def weight_grad(q):
+        full = jnp.concatenate([act1[s] for s in range(4)], axis=1)
+        gs[q] = dot(full, pat[:, 384 * q : 384 * q + 384], TN).reshape(4, 2, 64, 384)
+        grad_s[q].start()
+
     sum_d2, sum_x2 = [], []
     for kind in range(2):
         rows = KINDS[kind][1]
@@ -874,31 +901,34 @@
                 t = 3 * ti + tj
                 pat[kind_rows(kind), 128 * t : 128 * t + 128] = moved(col, kind, ti - 1).astype(BF16)
         if kind == 1:
+            weight_grad(0)
             both_mid(2, 0)
         scatter_start(2, kind, dot(pat[kind_rows(kind), :], weight_s(), NT))
-    full1 = jnp.concatenate([act1[s] for s in range(4)], axis=1)
     grad_e.along()
-    for q in range(3):
-        gs[q] = dot(full1, pat[:, 384 * q : 384 * q + 384], TN).reshape(4, 2, 64, 384)
-        grad_s[q].start()
+    weight_grad(1)
+    weight_grad(2)
     both_mid(2, 1)
     over_x(2)
     over_x(3)
     line_got(share_o)
     between(we.at[xp[1]], 1)
     grad_s[0].along()
-
-    sum_d1, sum_x1 = [], []
+    grad_e.hand_on()
+    grad_s[0].hand_on()
+
+    sum_1 = [[0.0, 0.0], [0.0, 0.0]]
     for kind in range(2):
         rows = KINDS[kind][1]
-        d = both_end(2, kind) * slope1[kind_rows(kind), :]
-        dz_, sd, sxx = norm_back(d, xhat1[kind_rows(kind), :], rstd1[kind], gain1, rows)
-        sum_d1.append(sd)
-        sum_x1.append(sxx)
-        both_out(2, kind, dred, dz_.astype(BF16))
-
-    gx1, gd1 = sum_x1[0] + sum_x1[1], sum_d1[0] + sum_d1[1]
-    rows12 = [jnp.where(x == 0, g[:, :128], g[:, 128:]) for g in (gx1, gd1)]
+        for xx in range(2):
+            d = both_end(2, kind, xx) * slope1[xx, kind_rows(kind), :]
+            dz_, sd, sxx = norm_back(d, xhat1[xx, kind_rows(kind), :], rstd1[kind][xx], gain1[xx], rows)
+            sum_1[xx][0] += sxx
+            sum_1[xx][1] += sd
+            both_out(2, kind, xx, dred, dz_.astype(BF16))
+        if kind == 0:
+            grad_s[1].along()
+
+    rows12 = [jnp.where(x == 0, sum_1[0][n], sum_1[1][n]) for n in range(2)]
     rows12 += [sum_x2[0] + sum_x2[1], sum_d2[0] + sum_d2[1]]
     gx3, gd3 = sum_x3[0] + sum_x3[1], sum_d3[0] + sum_d3[1]
     rows3 = [g[:, 128 * k : 128 * k + 128] for g in (gx3, gd3) for k in range(4)]
@@ -915,7 +945,7 @@
             row = 4 * (2 + 2 * (n % 2) + m) + n // 2
             rows_pool[row : row + 1, :] = jnp.sum(pool[8 + n, 4 * m : 4 * m + 4, :], axis=0, keepdims=True) / 16.0
     slices_p.start(rows_pool[...])
-    grad_s[1].along()
+    grad_s[1].hand_on()
     full_d = [gather_end(2, kind, dred) for kind in range(2)]
 
     for m in range(4):
@@ -938,6 +968,7 @@
     slices_s[0].start(grad_s[0].total())
     slices_e.start(grad_e.total())
     got(wr.at[0], r_xw)
+    grad_s[2].hand_on()
     between(wr.at[xp[1]], 0)
 
     @pl.when(y == c)
@@ -949,9 +980,6 @@
     slices_s[1].start(grad_s[1].total())
     got(wr.at[pl.ds(0, 2)], r_ow)
     own_gradient()
-    slices_p.mid()
-    slices_e.mid()
-    slices_s[0].mid()
 
     got(pgr.at[pl.ds(0, 7)], r_pp)
     total = pgr[0]
@@ -961,7 +989,6 @@
     for dev in rest:
         copy(pgs.at[r], pgs.at[r], s_ps, r_ps, dev).start()
     slices_s[2].start(grad_s[2].total())
-    slices_s[1].mid()
 
     s_fr, r_fr = new(2), new(2)
     for q in range(2):
@@ -969,17 +996,8 @@
         @pl.when(y == c)
         def _(q=q):
             fin_r[q, x] = grad_r[q].total().astype(BF16)
-            copy(fin_r.at[q, x], fin_r.at[q, x], s_fr + q, r_fr + q, xp).start()
-            copy(fin_r.at[q, x], fin_r.at[q, x], s_fr + q, r_fr + q, cp).start()
-
-    slices_s[2].mid()
-    for q in range(2):
-
-        @pl.when(y == c)
-        def _(q=q):
-            far = fin_r.at[q, 1 - x]
-            got(far, r_fr + q)
-            copy(far, far, s_fr + q, r_fr + q, cp).start()
+            for dev in rest:
+                copy(fin_r.at[q, x], fin_r.at[q, x], s_fr + q, r_fr + q, dev).start()
 
     for one in (slices_p, slices_e, *slices_s):
         one.end()
@@ -1018,6 +1036,7 @@
         for q, one in enumerate(grad_r):
             one.sent()
             sent(one.zsend.at[pl.ds(0, 3)], s_fr + q)
+            got(fin_r.at[q, 1 - x], r_fr + q)
 
     assert taken[0] == SEMAPHORES, taken
 
@@ -1097,14 +1116,14 @@
             buf((3, 4, N, 128), F32), buf((3, 2, 2, NV, 128)), buf((3, 2, 2, NV, 128)),
             buf((3, 2, 2, NV, 128)), buf((3, 2, 2, NV, 128)),
             buf((4, N, 128)), buf((4, N, 128)), buf((4, N, 128)), buf((N, 1152), F32),
-            buf((N, 256), F32), buf((N, 256), F32), buf((N, 128), F32), buf((N, 128), F32),
+            buf((2, N, 128), F32), buf((2, N, 128), F32), buf((N, 128), F32), buf((N, 128), F32),
             buf((N, 512), F32), buf((N, 512), F32), buf((N, 512)), buf((N, 1152)),
             buf((192, 2048), F32), buf((16, 8, 512), F32), buf((32, 512), F32),
             buf((4, 2, 64, 512), F32), buf((3, 4, 2, 64, 384), F32), buf((2, 4, 128, 256), F32),
             buf((4, 64, 512)), buf((4, 64, 512)), buf((4, 64, 512)), buf((4, 64, 512)),
             buf((3, 4, 64, 384)), buf((3, 4, 64, 384)), buf((3, 4, 64, 384)), buf((3, 4, 64, 384)),
             buf((2, 4, 128, 256)), buf((2, 4, 128, 256)), buf((2, 4, 128, 256)), buf((2, 4, 128, 256)),
-            buf((64, 512), F32), buf((3, 64, 384), F32), buf((2, 128, 256), F32),
+            buf((64, 512)), buf((3, 64, 384)), buf((64, 512), F32), buf((3, 64, 384), F32), buf((2, 128, 256), F32),
             buf((8, 16, 128), F32),
             dma(SEMAPHORES),
         ],

time: 88.8 us -> 85.7 us (0.965)
  Pallas kernels: 88 us -> 84.8 us
    pallas_call x1, Pallas kernels: 85.4 us -> 82.2 us  [fused(): pl.pallas_call(block_kernel, out_shape=[buf((8, 16, 2048)), buf((64, 2048...]
where the time goes in v6:
time: 85.7 us; the launch traced here: 85.5 us
  Pallas kernels  84.8 us (99%)
    pallas_call x1, Pallas kernels, fused(): pl.pallas_call(block_kernel, out_shape=[buf((8, 16, 2048)), buf((64, 2048...  82.2 us
    pallas_call x1, Pallas kernels, fused(): pl.pallas_call(store_kernel, out_shape=[shape((8, 16, 2048), BF16), shape...  2.59 us

profile of v6, /device:TPU:0, one launch (start us, length us, event | category | flops | bytes accessed | tf_op | source)
XLA Modules:
  0.0 85.5 jit_solution(15084966286139088781)
XLA Ops:
  0.7 82.2 %shard_map.236 = (bf16[8,16,2048]{2,1,0:T(8,128)(2,1)S(1)}, bf16[64,2048]{1,0:T(8,128)(2,1)S(1)}, bf16[4,32,512]{2,1,0:T(8,128)(2,1)S(1)}, bf16[8,16,2048]{2,1,0...) custom-call(bf16[8,16,2048]{2,1,0:T(8,128)(2,1)} %bitcast.17, ...), custom_call_target="tpu_custom_call" | custom-call | flops 5200000000 | bytes 8000000 | tf_op jit(solution)/shard_map/pallas_call | solution.py:1103
  82.9 2.6 %shard_map.237 = (bf16[8,16,2048]{2,1,0:T(8,128)(2,1)}, bf16[16,4,2048]{2,1,0:T(4,128)(2,1)}, f32[6,4,2048]{2,1,0:T(4,128)}, bf16[8,16,2048]{2,1,0:T(8,128)(2,1)...) custom-call(bf16[8,16,2048]{2,1,0:T(8,128)(2,1)S(1)} %get-tuple-elem, ...), custom_call_target="tpu_custom_call" | custom-call | tf_op jit(solution)/shard_map/pallas_call | solution.py:1134

commit v7 on v6

--- a/solution.py
+++ b/solution.py
@@ -268,7 +268,7 @@
 
 
 MESH = pl.DeviceIdType.MESH
-SEMAPHORES = 174
+SEMAPHORES = 179
 F32 = jnp.float32
 BF16 = jnp.bfloat16
 NV = 512
@@ -678,7 +678,6 @@
             line_pass(share_e, 0, share_e.passed, (2,))
     spread_c(cot_crops, cc4, 1, rest[1:])
     over_x(0)
-    over_x(1)
     pool[...] = jnp.zeros_like(pool)
     gather_mid(0, act2)
     stored(cv.at[:, r], l_cot[0])
@@ -843,16 +842,22 @@
             sent(self.zsend.at[pl.ds(0, 3)], self.s_z)
 
     class Slices:
-        def __init__(self, buf):
-            self.buf, self.send, self.come = buf, new(), new()
+        def __init__(self, buf, straight=False):
+            self.buf, self.straight, self.send, self.near, self.far = buf, straight, new(), new(), new()
 
         def start(self, value):
             self.buf[r] = value.astype(BF16)
-            for dev in rest:
-                copy(self.buf.at[r], self.buf.at[r], self.send, self.come, dev).start()
+            for dev, come in ((xp, self.near if self.straight else self.far), (cp, self.near), (xcp, self.near)):
+                if dev is not xcp or self.straight:
+                    copy(self.buf.at[r], self.buf.at[r], self.send, come, dev).start()
+
+        def mid(self):
+            far = self.buf.at[xp[1]]
+            got(far, self.far)
+            copy(far, far, self.send, self.near, cp).start()
 
         def end(self):
-            got(self.buf.at[pl.ds(0, 3)], self.come)
+            got(self.buf.at[pl.ds(0, 3 if self.straight else 2)], self.near)
             sent(self.buf.at[pl.ds(0, 3)], self.send)
 
     grad_e = Grad(ge, ysend_e, yrecv_e, zsend_e, zrecv_e, acc_e, relay_e)
@@ -860,7 +865,7 @@
         Grad(*(one.at[q] for one in (gs, ysend_s, yrecv_s, zsend_s, zrecv_s, acc_s, relay_s))) for q in range(3)
     ]
     grad_r = [Grad(*(one.at[q] for one in (gr, ysend_r, yrecv_r, zsend_r, zrecv_r, acc_r)), both=False) for q in range(2)]
-    slices_p, slices_e, slices_s = Slices(fin_p), Slices(fin_e), [Slices(fin_s.at[q]) for q in range(3)]
+    slices_p, slices_e, slices_s = Slices(fin_p), Slices(fin_e), [Slices(fin_s.at[q], q == 2) for q in range(3)]
 
     expand(0)
     scatter_start(1, 0, dot(dex[kind_rows(0), :], weight_e, NT))
@@ -876,6 +881,7 @@
     s_af, r_af = new(), new()
     for dev in rest:
         copy(aff.at[r], aff.at[r], s_af, r_af, dev).start()
+    over_x(1)
 
     def norm_back(d, xhat, rstd, gain, rows):
         sd = jnp.sum(d, axis=0, keepdims=True)
@@ -967,19 +973,19 @@
     grad_s[2].along()
     slices_s[0].start(grad_s[0].total())
     slices_e.start(grad_e.total())
-    got(wr.at[0], r_xw)
     grad_s[2].hand_on()
-    between(wr.at[xp[1]], 0)
 
     @pl.when(y == c)
     def _():
         grad_r[0].along()
         grad_r[1].along()
 
-
     slices_s[1].start(grad_s[1].total())
-    got(wr.at[pl.ds(0, 2)], r_ow)
-    own_gradient()
+    slices_p.mid()
+    slices_s[0].mid()
+    slices_e.mid()
+    got(wr.at[0], r_xw)
+    between(wr.at[xp[1]], 0)
 
     got(pgr.at[pl.ds(0, 7)], r_pp)
     total = pgr[0]
@@ -989,6 +995,9 @@
     for dev in rest:
         copy(pgs.at[r], pgs.at[r], s_ps, r_ps, dev).start()
     slices_s[2].start(grad_s[2].total())
+    slices_s[1].mid()
+    got(wr.at[pl.ds(0, 2)], r_ow)
+    own_gradient()
 
     s_fr, r_fr = new(2), new(2)
     for q in range(2):

time: 85.7 us -> 85.1 us (level)
  no operation moved by 1% of the time
where the time goes in v7:
time: 85.1 us; the launch traced here: 84.9 us
  Pallas kernels  84.3 us (99%)
    pallas_call x1, Pallas kernels, fused(): pl.pallas_call(block_kernel, out_shape=[buf((8, 16, 2048)), buf((64, 2048...  81.7 us
    pallas_call x1, Pallas kernels, fused(): pl.pallas_call(store_kernel, out_shape=[shape((8, 16, 2048), BF16), shape...  2.59 us

profile of v7, /device:TPU:0, one launch (start us, length us, event | category | flops | bytes accessed | tf_op | source)
XLA Modules:
  0.0 84.9 jit_solution(8984168823680855386)
XLA Ops:
  0.7 81.7 %shard_map.236 = (bf16[8,16,2048]{2,1,0:T(8,128)(2,1)S(1)}, bf16[64,2048]{1,0:T(8,128)(2,1)S(1)}, bf16[4,32,512]{2,1,0:T(8,128)(2,1)S(1)}, bf16[8,16,2048]{2,1,0...) custom-call(bf16[8,16,2048]{2,1,0:T(8,128)(2,1)} %bitcast.17, ...), custom_call_target="tpu_custom_call" | custom-call | flops 5200000000 | bytes 8000000 | tf_op jit(solution)/shard_map/pallas_call | solution.py:1112
  82.3 2.6 %shard_map.237 = (bf16[8,16,2048]{2,1,0:T(8,128)(2,1)}, bf16[16,4,2048]{2,1,0:T(4,128)(2,1)}, f32[6,4,2048]{2,1,0:T(4,128)}, bf16[8,16,2048]{2,1,0:T(8,128)(2,1)...) custom-call(bf16[8,16,2048]{2,1,0:T(8,128)(2,1)S(1)} %get-tuple-elem, ...), custom_call_target="tpu_custom_call" | custom-call | tf_op jit(solution)/shard_map/pallas_call | solution.py:1143

commit v8 on v7

--- a/solution.py
+++ b/solution.py
@@ -364,6 +364,11 @@
     def kind_rows(kind):
         return pl.ds(*KINDS[kind])
 
+    bar = pltpu.get_barrier_semaphore()
+    peers = [((i + n) % 8, r) for n in range(1, 8)] + [cp, xp, xcp]
+    for dev in peers:
+        pl.semaphore_signal(bar, inc=1, device_id=dev, device_id_type=MESH)
+
     def stage(src, dst, one):
         pltpu.make_async_copy(src, dst, sem.at[one]).start()
 
@@ -390,10 +395,6 @@
     for n, (src, dst) in enumerate(((views, xo_v), (crops, xo_c), (cot_views, co_v), (cot_crops, co_c))):
         stage(src, dst, l_own + n)
 
-    bar = pltpu.get_barrier_semaphore()
-    peers = [((i + n) % 8, r) for n in range(1, 8)] + [cp, xp, xcp]
-    for dev in peers:
-        pl.semaphore_signal(bar, inc=1, device_id=dev, device_id_type=MESH)
     pl.semaphore_wait(bar, len(peers))
 
     class Share:
@@ -631,9 +632,8 @@
         line_pass(share_s, h, None, which)
     stored(we.at[r, i], l_we)
     stored(we.at[r, i], l_we2)
-    for share in (share_e, share_o):
-        line_send(share, True)
-        line_over(share)
+    line_send(share_e, True)
+    line_over(share_e)
     rstd1, rstd2 = [[None, None], [None, None]], [None, None]
     for kind in range(2):
         rows = KINDS[kind][1]
@@ -654,6 +654,8 @@
         copy(ref, ref, s_ow, r_ow + n, cp).start()
 
     between(wr.at[r], 0)
+    line_send(share_o, True)
+    line_over(share_o)
     line_pass(share_e, 0, share_e.passed, (0,))
     line_got(share_s)
     line_pass(share_e, 0, share_e.passed, (1,))
@@ -950,7 +952,6 @@
         for m in range(2):
             row = 4 * (2 + 2 * (n % 2) + m) + n // 2
             rows_pool[row : row + 1, :] = jnp.sum(pool[8 + n, 4 * m : 4 * m + 4, :], axis=0, keepdims=True) / 16.0
-    slices_p.start(rows_pool[...])
     grad_s[1].hand_on()
     full_d = [gather_end(2, kind, dred) for kind in range(2)]
 
@@ -971,6 +972,7 @@
     got(we.at[pl.ds(0, 2)], r_ow + 1)
     own_output()
     grad_s[2].along()
+    slices_p.start(rows_pool[...])
     slices_s[0].start(grad_s[0].total())
     slices_e.start(grad_e.total())
     grad_s[2].hand_on()

time: 85.1 us -> 84.7 us (level)
  no operation moved by 1% of the time
where the time goes in v8:
time: 84.7 us; the launch traced here: 84.5 us
  Pallas kernels  83.8 us (99%)
    pallas_call x1, Pallas kernels, fused(): pl.pallas_call(block_kernel, out_shape=[buf((8, 16, 2048)), buf((64, 2048...  81.2 us
    pallas_call x1, Pallas kernels, fused(): pl.pallas_call(store_kernel, out_shape=[shape((8, 16, 2048), BF16), shape...  2.59 us

profile of v8, /device:TPU:0, one launch (start us, length us, event | category | flops | bytes accessed | tf_op | source)
XLA Modules:
  0.0 84.5 jit_solution(12786683689973498443)
XLA Ops:
  0.7 81.2 %shard_map.236 = (bf16[8,16,2048]{2,1,0:T(8,128)(2,1)S(1)}, bf16[64,2048]{1,0:T(8,128)(2,1)S(1)}, bf16[4,32,512]{2,1,0:T(8,128)(2,1)S(1)}, bf16[8,16,2048]{2,1,0...) custom-call(bf16[8,16,2048]{2,1,0:T(8,128)(2,1)} %bitcast.17, ...), custom_call_target="tpu_custom_call" | custom-call | flops 5200000000 | bytes 8000000 | tf_op jit(solution)/shard_map/pallas_call | solution.py:1114
  81.9 2.6 %shard_map.237 = (bf16[8,16,2048]{2,1,0:T(8,128)(2,1)}, bf16[16,4,2048]{2,1,0:T(4,128)(2,1)}, f32[6,4,2048]{2,1,0:T(4,128)}, bf16[8,16,2048]{2,1,0:T(8,128)(2,1)...) custom-call(bf16[8,16,2048]{2,1,0:T(8,128)(2,1)S(1)} %get-tuple-elem, ...), custom_call_target="tpu_custom_call" | custom-call | tf_op jit(solution)/shard_map/pallas_call | solution.py:1145
